TPU v7x, 256 devices: a whole 4x4x8 slice. The times are simulated.
256 devices in a mesh: grid: 32 (over y, z_hi, core), orb: 8 (over x, z_lo).
Axes of the slice: x: 4, y: 4, z: 8 (z_hi: 4, z_lo: 2; z = z_hi * 2 + z_lo), core: 2. Of those that a mesh axis runs over, the one named last changes fastest.
Arguments:
- orbitals: bfloat16 [131072, 1024], P('grid', 'orb'), may hold values from -6 to 6
- potentials: bfloat16 [131072, 4096], P(('grid', 'orb')), may hold values from -0.0029296875 to 0.0029296875
- point_index: int32 [4096], replicated, may hold values from 0 to 131071, as said below
Outputs:
- exchange_applied: bfloat16 [131072, 1024], P('grid', 'orb')
Inputs may be any that keep to these rules, and one draw needn't show every extreme that they name: `point_index`: the indices are distinct. Counting the grid points in aligned runs of 512, no run holds more than 32 interpolation points, and some run holds exactly 32.
All inputs are finite; a program needn't handle non-finite values.
Results may differ from a plain program's by a relative error of at most 0.005.
Values may be sent and summed in bfloat16 or wider, within the bound.
No kernel may reach another device: no remote copies, remote signals or barrier semaphores. Data moves between devices by JAX's collectives and lax.ppermute only.
A program may use at most 128 MiB of HBM per device.

v0:
```python
import jax
import jax.numpy as jnp
from jax import lax
from jax.sharding import PartitionSpec as P


def slot_tables(point_index, devices, rows_each, capacity):
    owners = point_index // rows_each
    order = jnp.argsort(owners, stable=True)
    sorted_owner = owners[order]
    number = point_index.shape[0]
    starts = jnp.searchsorted(sorted_owner, jnp.arange(devices, dtype=jnp.int32))
    ranks = jnp.arange(number, dtype=jnp.int32) - starts[sorted_owner]
    placed = jnp.zeros((number,), jnp.int32).at[order].set(sorted_owner * capacity + ranks)
    wanted = starts[:, None] + jnp.arange(capacity, dtype=jnp.int32)[None, :]
    clipped = jnp.minimum(wanted, number - 1)
    device_ids = jnp.arange(devices, dtype=jnp.int32)[:, None]
    filled = (wanted < number) & (sorted_owner[clipped] == device_ids)
    local_rows = jnp.where(filled, point_index[order][clipped] - device_ids * rows_each, 0)
    return (placed, local_rows, filled)


def shards(orbitals, potentials, point_index):
    n_grid = lax.axis_size("grid")
    n_orb = lax.axis_size("orb")
    devices = n_grid * n_orb
    rows_each = potentials.shape[0]
    npoints = potentials.shape[1]
    capacity = 2 * npoints // devices
    placed, local_rows, filled = slot_tables(point_index, devices, rows_each, capacity)
    rows_here = lax.all_to_all(orbitals, "orb", split_axis=0, concat_axis=1, tiled=True)
    myself = lax.axis_index("grid") * n_orb + lax.axis_index("orb")
    my_rows = lax.dynamic_index_in_dim(local_rows, myself, 0, keepdims=False)
    my_fill = lax.dynamic_index_in_dim(filled, myself, 0, keepdims=False)
    picked = jnp.take(rows_here, my_rows, axis=0)
    slots = jnp.where(my_fill[:, None], picked, jnp.zeros_like(picked))
    gathered = lax.all_gather(slots, ("grid", "orb"), axis=0, tiled=True)
    point_values = jnp.take(gathered, placed, axis=0)
    density = lax.dot_general(
        rows_here, point_values, (((1,), (1,)), ((), ())), preferred_element_type=jnp.float32
    )
    weighted = (potentials.astype(jnp.float32) * density).astype(jnp.bfloat16)
    applied = jnp.dot(weighted, point_values, preferred_element_type=jnp.float32)
    result = (-applied).astype(jnp.bfloat16)
    return lax.all_to_all(result, "orb", split_axis=1, concat_axis=0, tiled=True)


def solution(mesh):
    return jax.shard_map(
        shards,
        mesh=mesh,
        in_specs=(P("grid", "orb"), P(("grid", "orb"), None), P()),
        out_specs=P("grid", "orb"),
        check_vma=False,
    )
```

profile of v0, /device:TPU:1, one launch (start us, length us, event | category | flops | bytes accessed | tf_op | source)
XLA Modules:
  0.0 989.7 jit_solution(17475841637240963980)
XLA Ops:
  6.5 6.2 all-to-all-start
  13.5 5.8 sort.17
  19.3 23.0 %gather_fusion.1 = s32[4096]{0:T(1024)S(1)} fusion(s32[4096]{0:T(1024)S(1)} %add_select_fusion, s32[4096]{0:T(1024)S(1)} %get-tuple-element.103), kind=kCustom, calls=%fused_computation.1 | custom fusion | bytes 49152 | tf_op jit(solution)/shard_map/gather | solution.py:10
  42.4 23.3 %while.24 = (s32[]{:T(128)}, u32[256]{0:T(256)S(1)}, u32[256]{0:T(256)S(1)}, s32[4096]{0:T(1024)S(1)}, s32[]{:T(128)}, /*index=5*/s32[]{:T(128)}, s32[]{}) while((s32[]{:T(128)}, u32[256]{0:T(256)S(1)}, u32[256]{0:T(256)S(1)}, s32[4096]{0:T(1024)S(1)}, s32[]{:T(128)}, /*index=5*/s32[]{:T(128)}, s32[]{}) %tuple.35), condition=%wide.region_2.3_spmd.clone, body=%wide.region_1.2_spmd.clone.sunk | while | flops 4356 | bytes 16484 | solution.py:12
  42.4 1.7 gather_fusion
  44.2 1.7 gather_fusion
  46.0 1.7 gather_fusion
  47.8 1.7 gather_fusion
  49.6 1.7 gather_fusion
  51.4 1.7 gather_fusion
  53.2 1.7 gather_fusion
  55.0 1.7 gather_fusion
  56.7 1.7 gather_fusion
  58.5 1.7 gather_fusion
  65.7 23.0 %gather_fusion.4 = s32[4096]{0:T(1024)S(1)} fusion(s32[4096]{0:T(1024)S(1)} %copy-done, s32[4096]{0:T(1024)S(1)} %get-tuple-element.103), kind=kCustom, calls=%fused_computation.4 | custom fusion | bytes 49152 | tf_op jit(solution)/shard_map/gather | solution.py:19
  88.9 45.5 %gather_fusion.3 = s32[8192]{0:T(1024)S(1)} fusion(s32[4096]{0:T(1024)S(1)} %get-tuple-element.155, s32[8192]{0:T(1024)S(1)} %broadcast_clamp_fusion), kind=kCustom, calls=%fused_computation.3 | custom fusion | bytes 98304 | tf_op jit(solution)/shard_map/gather | solution.py:18
  134.5 45.5 %gather_fusion.5 = s32[8192]{0:T(1024)S(1)} fusion(s32[4096]{0:T(1024)S(1)} %gather_fusion.4, s32[8192]{0:T(1024)S(1)} %broadcast_clamp_fusion), kind=kCustom, calls=%fused_computation.5 | custom fusion | bytes 98304 | tf_op jit(solution)/shard_map/gather | solution.py:19
  183.2 25.7 %gather_fusion.2 = s32[4096]{0:T(1024)S(1)} fusion(s32[256]{0:T(256)S(1)} %convert_element_type.20, s32[4096]{0:T(1024)S(1)} %broadcast_clamp_fusion.1), kind=kCustom, calls=%fused_computation.2 | custom fusion | bytes 49152 | tf_op jit(solution)/shard_map/gather | solution.py:13
  209.0 6.5 copy.8
  215.5 15.7 %scatter_custom_fusion = s32[4096]{0:T(1024)S(1)} fusion(s32[4096]{0:T(1024)S(1)} %get-tuple-element.102, s32[4096]{0:T(1024)S(1)} %subtract_add_fusion, s32[]{:T(128)} %constant.88.clone.1), kind=kCustom, calls=%fused_computation.46 | custom fusion | bytes 16388 | tf_op jit(solution)/shard_map/scatter | solution.py:14
  231.2 686.2 %all-gather.2.cloned.1.call-done = bf16[8192,1024]{1,0:T(8,128)(2,1)} async-done(((bf16[32,1024]{1,0:T(8,128)(2,1)}), bf16[8192,1024]{1,0:T(8,128)(2,1)}) %all-gather.2.cloned.1.call-update) | async-done | bytes 16777232 | tf_op jit(solution)/shard_map/all_gather | solution.py:37
  917.4 28.9 %gather_fusion.7 = bf16[4096,1024]{1,0:T(8,128)(2,1)} fusion(bf16[8192,1024]{1,0:T(8,128)(2,1)} %all-gather.2.cloned.1.call-done, s32[4096]{0:T(1024)S(1)} %fusion.10), kind=kCustom, calls=%fused_computation.7 | custom fusion | bytes 16793600 | tf_op jit(solution)/shard_map/jit(_take)/gather | solution.py:38
  946.3 16.3 %fusion.6 = bf16[64,8,8,128]{3,2,1,0:T(8,128)(2,1)S(1)} fusion(bf16[4096,1024]{1,0:T(8,128)(2,1)} %gather_fusion.7, pred[4096]{0:T(1024)(128)(4,1)S(1)} %compare_and_fusion, bf16[512,4096]{0,1:T(8,128)(2,1)} %copy.8, bf16[8,512,128]{2,1,0:T(8,128)(2,1)S(1)} %all-to-all-done), kind=kOutput, calls=%fused_computation.22 | convolution fusion | flops 8605663232 | bytes 14684160 | tf_op jit(solution)/shard_map/dot_general | solution.py:43
  962.8 19.1 %all_to_all.38 = bf16[512,8,128]{2,0,1:T(8,128)(2,1)S(1)} all-to-all(bf16[512,8,128]{2,0,1:T(8,128)(2,1)S(1)} %bitcast.45), channel_id=1, replica_groups=mesh['grid'=32,'orb'=8] {'orb'}, dimensions={1} | all-to-all | bytes 2097152 | tf_op jit(solution)/shard_map/all_to_all | solution.py:45
  (75 shorter events, 10.8 us)
Async XLA Ops:
  6.5 175.1 %all-to-all-start = ((bf16[8,512,128]{2,1,0:T(8,128)(2,1)}), bf16[8,512,128]{2,1,0:T(8,128)(2,1)S(1)}, u32[]{:S(2)}, u32[]{:S(2)}) async-start(bf16[8,512,128]{2,1,0:T(8,128)(2,1)} %bitcast.47), calls=%async_computation | async-start | bytes 2097152 | tf_op jit(solution)/shard_map/all_to_all | solution.py:31
  12.7 904.7 %all-gather.2.cloned.1.call-start = ((), (), s32[]{:S(2)}) async-start(), calls=%async_computation.2 | async-start | bytes 16842752 | tf_op jit(solution)/shard_map/all_gather | solution.py:37
  19.3 46.3 %copy-start = (s32[4096]{0:T(1024)S(1)}, s32[4096]{0:T(1024)}, u32[]{:S(2)}) copy-start(s32[4096]{0:T(1024)} %param.7) | copy-start | bytes 49156
Sparse Core Ops, SparseCore 0:
  183.3 734.0 all-gather.1
where the time goes:
time: 994 us; the launch traced here: 990 us
  waiting for transfers between devices  686 us (69%)
  local copies, waits for them, and re-layouts  239 us (24%)
  blocking collectives  19.1 us (2%)
  matrix products  16.3 us (2%)
  between operations  13.7 us (1%)
    all_gather x1, waiting for transfers between devices, shards(): gathered = lax.all_gather(slots, ('grid', 'orb'), axis=0, tiled=True)  686 us
    gather x3, local copies, waits for them, and re-layouts, slot_tables(): point_index[order][clipped] - device_ids * rows_each  68.7 us
    gather x2, local copies, waits for them, and re-layouts, slot_tables(): filled = (wanted < number) & (sorted_owner[clipped] == device_ids)  45.6 us
    gather x1, local copies, waits for them, and re-layouts, shards(): point_values = jnp.take(gathered, placed, axis=0)  28.9 us
    gather x1, local copies, waits for them, and re-layouts, slot_tables(): ranks = jnp.arange(number, dtype=jnp.int32) - starts[sorted_owner]  25.7 us
    gather x1, local copies, waits for them, and re-layouts, slot_tables(): sorted_owner = owners[order]  23 us
    gather x13, local copies, waits for them, and re-layouts, slot_tables(): jnp.searchsorted(sorted_owner, jnp.arange(devices, dtype=jnp.int32))  22.4 us
  transfers between devices with their start and end apart: 2, of which 1 were waited for; matrix products, arithmetic and copies ran while one was open for 22% of the time, Pallas kernels for 0%

commit v1 on v0

v1 whole, which is shorter than its diff:
```python
import jax
import jax.numpy as jnp
from jax import lax
from jax.experimental import pallas as pl
from jax.experimental.pallas import tpu as pltpu
from jax.sharding import PartitionSpec as P

NY, NZH, NC, NX, NZL = 4, 4, 2, 4, 2
AXES = ("grid", "orb")
BLOCK = 512


def moves(target):
    pairs = []
    for y in range(NY):
        for zh in range(NZH):
            for c in range(NC):
                for x in range(NX):
                    for zl in range(NZL):
                        ty, tzh, tc, tx, tzl = target(y, zh, c, x, zl)
                        src = ((y * NZH + zh) * NC + c) * NX * NZL + x * NZL + zl
                        dst = ((ty % NY * NZH + tzh % NZH) * NC + tc % NC) * NX * NZL + tx % NX * NZL + tzl % NZL
                        pairs.append((src, dst))
    return pairs


def send(value, target):
    return lax.ppermute(value, AXES, moves(target))


def to_core(value):
    return send(value, lambda y, zh, c, x, zl: (y, zh, 1 - c, x, zl))


def to_y(value, d):
    return send(value, lambda y, zh, c, x, zl: (y + d, zh, c, x, zl))


def to_zh(value, d):
    return send(value, lambda y, zh, c, x, zl: (y, zh + d, c, x, zl))


def to_zl(value):
    return send(value, lambda y, zh, c, x, zl: (y, zh, c, x, 1 - zl))


def first_axis(value, d):
    return send(value, lambda y, zh, c, x, zl: (y + d * c, zh, c, x + d * (1 - c), zl))


def second_axis(value, d):
    return send(value, lambda y, zh, c, x, zl: (y + d * (1 - c), zh, c, x + d * c, zl))


def pick_kernel(place, index, mine, other, *refs):
    outs, slot_ref = refs[:4], refs[4]
    slab, half, y = place[0], place[1], place[2]
    idx = index[...]
    owner = lax.shift_right_logical(idx, 12)
    in_mine = owner == slab
    in_other = owner == (slab ^ 1)
    flags = jnp.concatenate([in_mine.astype(jnp.float32), in_other.astype(jnp.float32)], axis=0)
    rows = lax.broadcasted_iota(jnp.int32, (BLOCK, BLOCK), 0)
    lanes = lax.broadcasted_iota(jnp.int32, (BLOCK, BLOCK), 1)
    upper = (rows <= lanes).astype(jnp.float32).astype(jnp.bfloat16)
    counts = jnp.dot(flags.astype(jnp.bfloat16), upper, preferred_element_type=jnp.float32)
    totals = counts[:, BLOCK - 1 : BLOCK]
    place_row = lax.broadcasted_iota(jnp.int32, (16, 1), 0)
    before = jnp.zeros((16, 1), jnp.float32)
    for i in range(16):
        last = 8 if i < 8 else 16
        later = (place_row > i) & (place_row < last)
        before = before + jnp.where(later, totals[i : i + 1, :], 0.0)
    ranks = counts + before - 1.0
    slot = jnp.where(in_mine, ranks[:8], jnp.where(in_other, ranks[8:] + 256.0, -1.0)).astype(jnp.int32)
    slot_ref[...] = slot
    local = idx & 4095
    high = lax.shift_right_logical(local, 6).astype(jnp.float32)
    low = (local & 63).astype(jnp.float32)
    where = jnp.zeros((BLOCK, 8), jnp.float32)
    pick_row = lax.broadcasted_iota(jnp.int32, (8, BLOCK), 0)
    for b in range(8):
        one_hot = (rows == slot[b : b + 1, :]).astype(jnp.float32).astype(jnp.bfloat16)
        parts = jnp.where(pick_row == 0, high[b : b + 1, :], jnp.where(pick_row == 1, low[b : b + 1, :], 0.0))
        where = where + lax.dot_general(
            one_hot, parts.astype(jnp.bfloat16), (((1,), (1,)), ((), ())), preferred_element_type=jnp.float32
        )
    line = (where[:, 0:1] * 64.0 + where[:, 1:2]).astype(jnp.int32)
    picked = []
    wide = 1024
    lane = lax.broadcasted_iota(jnp.int32, (256, wide), 1)
    for s, block in enumerate((mine, other)):
        want = line[s * 256 : (s + 1) * 256, :]
        total = jnp.zeros((256, 128), jnp.float32)
        for k in range(4096 // wide):
            one_hot = (want - k * wide == lane).astype(jnp.float32).astype(jnp.bfloat16)
            total = total + jnp.dot(one_hot, block[k * wide : (k + 1) * wide, :], preferred_element_type=jnp.float32)
        picked.append(total)
    turned = jnp.concatenate(picked, axis=0).T.astype(jnp.bfloat16)
    for d in range(4):
        b = half * 4 + lax.rem(y + d, 4)
        row = slot_ref[pl.ds(b, 1), :]
        one_hot = (rows == row).astype(jnp.float32).astype(jnp.bfloat16)
        outs[d][...] = jnp.dot(turned, one_hot, preferred_element_type=jnp.float32).astype(jnp.bfloat16)


def pick(place, index, mine, other):
    block = jax.ShapeDtypeStruct((128, BLOCK), jnp.bfloat16)
    vmem = pl.BlockSpec(memory_space=pltpu.VMEM)
    return pl.pallas_call(
        pick_kernel,
        out_shape=[block] * 4,
        in_specs=[pl.BlockSpec(memory_space=pltpu.SMEM), vmem, vmem, vmem],
        out_specs=[vmem] * 4,
        scratch_shapes=[pltpu.VMEM((8, BLOCK), jnp.int32)],
        compiler_params=pltpu.CompilerParams(vmem_limit_bytes=32 * 1024 * 1024),
        name="pick",
    )(place, index, mine, other)


def apply_kernel(place, rows_hbm, pot_hbm, *refs):
    mine, theirs = refs[0:4], refs[4:8]
    out = refs[8]
    points, rows, pots, acc, row_sem, pot_sem, point_sem = refs[9:]
    x, y, c = place[0], place[1], place[2]
    row_copies = [
        pltpu.make_async_copy(rows_hbm.at[o], rows.at[:, o * 128 : (o + 1) * 128], row_sem.at[o]) for o in range(8)
    ]
    for copy in row_copies:
        copy.start()

    def piece(arrays, k, i):
        if k < 4:
            source, block = arrays[k].at[i], lax.rem(x - i + 4, 4)
        else:
            source, block = arrays[i].at[k - 4], lax.rem(x - i + 4, 4)
        return pltpu.make_async_copy(
            source, points.at[k, pl.ds(pl.multiple_of(block * 256, 256), 256), :], point_sem.at[k, i]
        )

    def pot_copy(k):
        block = (k // 4) * 4 + lax.rem(y - k % 4 + 4, 4)
        return pltpu.make_async_copy(
            pot_hbm.at[:, pl.ds(pl.multiple_of(block * BLOCK, BLOCK), BLOCK)], pots.at[k], pot_sem.at[k]
        )

    for k in range(8):
        pot_copy(k).start()
        own = 0 if k < 4 else 1

        @pl.when(c == own)
        def _():
            for i in range(4):
                piece(mine, k, i).start()

        @pl.when(c != own)
        def _():
            for i in range(4):
                piece(theirs, k, i).start()

    for copy in row_copies:
        copy.wait()
    for k in range(8):
        pot_copy(k).wait()
        for i in range(4):
            piece(mine, k, i).wait()
        density = jnp.dot(rows[...], points[k], preferred_element_type=jnp.float32)
        weighted = (pots[k].astype(jnp.float32) * density).astype(jnp.bfloat16)
        part = lax.dot_general(
            weighted, points[k], (((1,), (1,)), ((), ())), preferred_element_type=jnp.float32
        )
        if k == 0:
            acc[...] = part
        elif k < 7:
            acc[...] += part
        else:
            total = -(acc[...] + part)
            for o in range(8):
                out[o] = total[:, o * 128 : (o + 1) * 128].astype(jnp.bfloat16)


def apply(place, rows_here, potentials, mine, theirs):
    anyspace = pl.BlockSpec(memory_space=pl.ANY)
    rows_each = potentials.shape[0]
    return pl.pallas_call(
        apply_kernel,
        out_shape=jax.ShapeDtypeStruct((8, rows_each, 128), jnp.bfloat16),
        in_specs=[pl.BlockSpec(memory_space=pltpu.SMEM)] + [anyspace] * 10,
        out_specs=pl.BlockSpec(memory_space=pltpu.VMEM),
        scratch_shapes=[
            pltpu.VMEM((8, 1024, BLOCK), jnp.bfloat16),
            pltpu.VMEM((rows_each, 1024), jnp.bfloat16),
            pltpu.VMEM((8, rows_each, BLOCK), jnp.bfloat16),
            pltpu.VMEM((rows_each, 1024), jnp.float32),
            pltpu.SemaphoreType.DMA((8,)),
            pltpu.SemaphoreType.DMA((8,)),
            pltpu.SemaphoreType.DMA((8, 4)),
        ],
        compiler_params=pltpu.CompilerParams(vmem_limit_bytes=40 * 1024 * 1024),
        cost_estimate=pl.CostEstimate(flops=4 * rows_each * 4096 * 1024, bytes_accessed=16 * 1024 * 1024, transcendentals=0),
        name="apply",
    )(place, rows_here, potentials, *mine, *theirs)


def shards(orbitals, potentials, point_index):
    grid, orb = lax.axis_index("grid"), lax.axis_index("orb")
    c = lax.rem(grid, NC)
    y = lax.div(grid, NZH * NC)
    x, zl = lax.div(orb, NZL), lax.rem(orb, NZL)
    pick_place = jnp.stack([grid, c, y]).astype(jnp.int32)
    apply_place = jnp.stack([x, y, c]).astype(jnp.int32)

    other = to_core(orbitals)
    rows_here = lax.all_to_all(orbitals.reshape(8, -1, 128), "orb", split_axis=0, concat_axis=0, tiled=True)
    blocks = pick(pick_place, point_index.reshape(8, BLOCK), orbitals, other)
    here = blocks[0] + to_y(blocks[1], 1) + to_y(blocks[3], 3) + to_y(blocks[2], 2)
    here = here + to_zh(here, 1) + to_zh(here, 3) + to_zh(here, 2)
    beside = to_zl(here)
    pair = jnp.where(zl == 0, jnp.concatenate([here, beside]), jnp.concatenate([beside, here]))
    line = jnp.stack([pair] + [first_axis(pair, d) for d in (1, 2, 3)])
    mine = [line] + [second_axis(line, d) for d in (1, 2, 3)]
    theirs = [to_core(value) for value in mine]
    result = apply(apply_place, rows_here, potentials, mine, theirs)
    return lax.all_to_all(result, "orb", split_axis=0, concat_axis=0, tiled=True).reshape(-1, 128)


def solution(mesh):
    return jax.shard_map(
        shards,
        mesh=mesh,
        in_specs=(P("grid", "orb"), P(("grid", "orb"), None), P()),
        out_specs=P("grid", "orb"),
        check_vma=False,
    )
```

time: 994 us -> 131 us (0.13)
  waiting for transfers between devices: 686 us -> 60.2 us
  local copies, waits for them, and re-layouts: 239 us -> 1.69 us
  starting transfers between devices: 6.24 us -> 29.2 us
  Pallas kernels: 0 us -> 19.4 us
  matrix products: 16.3 us -> 0 us
  between operations: 13.7 us -> 0.09 us
    all_gather x1 -> x0, waiting for transfers between devices: 686 us -> none  [shards(): gathered = lax.all_gather(slots, ('grid', 'orb'), axis=0, tiled=True)]
    gather x22 -> x0, local copies, waits for them, and re-layouts: 215 us -> none  [the longest x3 68.7 us: slot_tables(): point_index[order][clipped] - device_ids * rows_each]
    ppermute x0 -> x18, waiting for transfers between devices: none -> 57.5 us  [send(): return lax.ppermute(value, AXES, moves(target))]
    ppermute x0 -> x18, starting transfers between devices: none -> 25.6 us  [send(): return lax.ppermute(value, AXES, moves(target))]
    pallas_call x0 -> x2, Pallas kernels: none -> 19.4 us  [the longest x1 12.8 us: apply(): pl.pallas_call(apply_kernel, out_shape=jax.ShapeDtypeStruct((8, rows_each...]
    dot_general x1 -> x0, matrix products: 16.3 us -> none  [shards(): jnp.dot(weighted, point_values, preferred_element_type=jnp.float32)]
    scatter x1 -> x0, local copies, waits for them, and re-layouts: 15.7 us -> none  [slot_tables(): jnp.zeros((number,), jnp.int32).at[order]]
  transfers between devices with their start and end apart: 2 -> 19, of which waited for: 1 -> 14; matrix products, arithmetic and copies ran while one was open for 22% -> 1% of each run, Pallas kernels for 0% -> 0%
where the time goes in v1:
time: 131 us; the launch traced here: 130 us
  waiting for transfers between devices  60.2 us (46%)
  starting transfers between devices  29.2 us (22%)
  Pallas kernels  19.4 us (15%)
  blocking collectives  19.3 us (15%)
  local copies, waits for them, and re-layouts  1.69 us (1%)
    ppermute x18, waiting for transfers between devices, send(): return lax.ppermute(value, AXES, moves(target))  57.5 us
    ppermute x18, starting transfers between devices, send(): return lax.ppermute(value, AXES, moves(target))  25.6 us
    all_to_all x1, blocking collectives, shards(): lax.all_to_all(result, 'orb', split_axis=0, concat_axis=0, tiled=True)  19.3 us
    pallas_call x1, Pallas kernels, apply(): pl.pallas_call(apply_kernel, out_shape=jax.ShapeDtypeStruct((8, rows_each...  12.8 us
    pallas_call x1, Pallas kernels, pick(): pl.pallas_call(pick_kernel, out_shape=[block] * 4, in_specs=[pl.BlockSpec...  6.6 us
    all_to_all x1, starting transfers between devices, shards(): lax.all_to_all(orbitals.reshape(8, -1, 128), 'orb', split_axis=0, concat_...  3.56 us
    all_to_all x1, waiting for transfers between devices, shards(): lax.all_to_all(orbitals.reshape(8, -1, 128), 'orb', split_axis=0, concat_...  2.67 us
  transfers between devices with their start and end apart: 19, of which 14 were waited for; matrix products, arithmetic and copies ran while one was open for 1% of the time, Pallas kernels for 0%

profile of v1, /device:TPU:1, one launch (start us, length us, event | category | flops | bytes accessed | tf_op | source)
XLA Modules:
  0.0 130.3 jit_solution(16658165441270167443)
XLA Ops:
  0.0 3.2 %collective-permute-start = (bf16[4096,128]{1,0:T(8,128)(2,1)}, bf16[4096,128]{1,0:T(8,128)(2,1)S(1)}, u32[]{:S(2)}, u32[]{:S(2)}) collective-permute-start(bf16[4096,128]{1,0:T(8,128)(2,1)} %mine.1), channel_id=1, source_target_pairs={{0,8},{1,9},{2,10},{3,11},{4,12},{5,13},{6,14},{7,15},{8,0},{9,1},... | collective-permute-start | bytes 3145736 | tf_op jit(solution)/shard_map/ppermute | solution.py:28
  4.0 1.7 %collective-permute-done.other = bf16[4096,128]{1,0:T(8,128)(2,1)S(1)} collective-permute-done((bf16[4096,128]{1,0:T(8,128)(2,1)}, bf16[4096,128]{1,0:T(8,128)(2,1)S(1)}, u32[]{:S(2)}, u32[]{:S(2)}) %collective-permute-start) | collective-permute-done | bytes 1048608 | tf_op jit(solution)/shard_map/ppermute | solution.py:28
  5.7 6.6 %pick.1 = (bf16[128,512]{1,0:T(8,128)(2,1)S(1)}, bf16[128,512]{1,0:T(8,128)(2,1)S(1)}, bf16[128,512]{1,0:T(8,128)(2,1)S(1)}, bf16[128,512]{1,0:T(8,128)(2,1)S(1)}) custom-call(s32[3]{0:T(128)S(1)} %pad_add_fusion.1.place, s32[8,512]{1,0:T(8,128)S(1)} %reshape.65.index, bf16[4096,128]{1,0:T(8,128)(2,1)} %mine.1, bf16[4096,128]{1,0:T(8,128)(2,1)S(1)} %collective-permute-done.other), custom_call_target="tpu_custom_call" | custom-call | tf_op jit(solution)/shard_map/pick/pallas_call | solution.py:110
  12.4 2.7 %collective-permute-start.2 = (bf16[128,512]{1,0:T(8,128)(2,1)S(1)}, bf16[128,512]{1,0:T(8,128)(2,1)S(1)}, u32[]{:S(2)}, u32[]{:S(2)}) collective-permute-start(bf16[128,512]{1,0:T(8,128)(2,1)S(1)} %get-tuple-element.11), channel_id=1, source_target_pairs={{0,192},{1,193},{2,194},{3,195},{4,196},{5,197},{6,198},{7,199},{8... | collective-permute-start | bytes 393224 | tf_op jit(solution)/shard_map/ppermute | solution.py:28
  15.1 3.2 %collective-permute-done.1 = bf16[128,512]{1,0:T(8,128)(2,1)S(1)} collective-permute-done((bf16[128,512]{1,0:T(8,128)(2,1)S(1)}, bf16[128,512]{1,0:T(8,128)(2,1)S(1)}, u32[]{:S(2)}, u32[]{:S(2)}) %collective-permute-start.1) | collective-permute-done | bytes 131104 | tf_op jit(solution)/shard_map/ppermute | solution.py:28
  18.3 1.9 %collective-permute-done.2 = bf16[128,512]{1,0:T(8,128)(2,1)S(1)} collective-permute-done((bf16[128,512]{1,0:T(8,128)(2,1)S(1)}, bf16[128,512]{1,0:T(8,128)(2,1)S(1)}, u32[]{:S(2)}, u32[]{:S(2)}) %collective-permute-start.2) | collective-permute-done | bytes 131104 | tf_op jit(solution)/shard_map/ppermute | solution.py:28
  20.5 7.2 %collective-permute-start.6 = (bf16[128,512]{1,0:T(8,128)(2,1)S(1)}, bf16[128,512]{1,0:T(8,128)(2,1)S(1)}, u32[]{:S(2)}, u32[]{:S(2)}) collective-permute-start(bf16[128,512]{1,0:T(8,128)(2,1)S(1)} %add_add_fusion.1), channel_id=1, source_target_pairs={{0,32},{1,33},{2,34},{3,35},{4,36},{5,37},{6,38},{7,39},{8,40},{9,... | collective-permute-start | bytes 393224 | tf_op jit(solution)/shard_map/ppermute | solution.py:28
  27.7 2.4 %collective-permute-start.4 = (bf16[128,512]{1,0:T(8,128)(2,1)S(1)}, bf16[128,512]{1,0:T(8,128)(2,1)S(1)}, u32[]{:S(2)}, u32[]{:S(2)}) collective-permute-start(bf16[128,512]{1,0:T(8,128)(2,1)S(1)} %add_add_fusion.1), channel_id=1, source_target_pairs={{0,16},{1,17},{2,18},{3,19},{4,20},{5,21},{6,22},{7,23},{8,24},{9,... | collective-permute-start | bytes 393224 | tf_op jit(solution)/shard_map/ppermute | solution.py:28
  30.1 10.4 %collective-permute-done.5 = bf16[128,512]{1,0:T(8,128)(2,1)S(1)} collective-permute-done((bf16[128,512]{1,0:T(8,128)(2,1)S(1)}, bf16[128,512]{1,0:T(8,128)(2,1)S(1)}, u32[]{:S(2)}, u32[]{:S(2)}) %collective-permute-start.5) | collective-permute-done | bytes 131104 | tf_op jit(solution)/shard_map/ppermute | solution.py:28
  40.7 4.5 %collective-permute-done.7 = bf16[128,512]{1,0:T(8,128)(2,1)S(1)} collective-permute-done((bf16[128,512]{1,0:T(8,128)(2,1)S(1)}, bf16[128,512]{1,0:T(8,128)(2,1)S(1)}, u32[]{:S(2)}, u32[]{:S(2)}) %collective-permute-start.7) | collective-permute-done | bytes 131104 | tf_op jit(solution)/shard_map/ppermute | solution.py:28
  45.3 1.3 %collective-permute-start.10 = (bf16[256,512]{1,0:T(8,128)(2,1)S(1)}, bf16[256,512]{1,0:T(8,128)(2,1)S(1)}, u32[]{:S(2)}, u32[]{:S(2)}) collective-permute-start(bf16[256,512]{1,0:T(8,128)(2,1)S(1)} %maximum_select_fusion.1), channel_id=1, source_target_pairs={{0,6},{1,7},{2,0},{3,1},{4,2},{5,3},{6,4},{7,5},{8,200},{9,201},{1... | collective-permute-start | bytes 786440 | tf_op jit(solution)/shard_map/ppermute | solution.py:28
  46.6 1.1 collective-permute-start.9
  47.7 3.1 %collective-permute-done.10 = bf16[256,512]{1,0:T(8,128)(2,1)S(1)} collective-permute-done((bf16[256,512]{1,0:T(8,128)(2,1)S(1)}, bf16[256,512]{1,0:T(8,128)(2,1)S(1)}, u32[]{:S(2)}, u32[]{:S(2)}) %collective-permute-start.10) | collective-permute-done | bytes 262176 | tf_op jit(solution)/shard_map/ppermute | solution.py:28
  50.9 2.5 %collective-permute-done.9 = bf16[256,512]{1,0:T(8,128)(2,1)S(1)} collective-permute-done((bf16[256,512]{1,0:T(8,128)(2,1)S(1)}, bf16[256,512]{1,0:T(8,128)(2,1)S(1)}, u32[]{:S(2)}, u32[]{:S(2)}) %collective-permute-start.9) | collective-permute-done | bytes 262176 | tf_op jit(solution)/shard_map/ppermute | solution.py:28
  53.4 3.0 %collective-permute-done.8 = bf16[256,512]{1,0:T(8,128)(2,1)S(1)} collective-permute-done((bf16[256,512]{1,0:T(8,128)(2,1)S(1)}, bf16[256,512]{1,0:T(8,128)(2,1)S(1)}, u32[]{:S(2)}, u32[]{:S(2)}) %collective-permute-start.8) | collective-permute-done | bytes 262176 | tf_op jit(solution)/shard_map/ppermute | solution.py:28
  56.5 2.7 %collective-permute-start.13 = (bf16[4,256,512]{2,1,0:T(8,128)(2,1)S(1)}, bf16[4,256,512]{2,1,0:T(8,128)(2,1)S(1)}, u32[]{:S(2)}, u32[]{:S(2)}) collective-permute-start(bf16[4,256,512]{2,1,0:T(8,128)(2,1)S(1)} %pad_maximum_fusion.refs_0_), channel_id=1, source_target_pairs={{0,192},{1,193},{2,194},{3,195},{4,196},{5,197},{6,198},{7,199},{8... | collective-permute-start | bytes 3145736 | tf_op jit(solution)/shard_map/ppermute | solution.py:28
  60.1 3.6 %all-to-all-start = ((bf16[8,512,128]{2,1,0:T(8,128)(2,1)}), bf16[8,512,128]{2,1,0:T(8,128)(2,1)S(1)}, u32[]{:S(2)}, u32[]{:S(2)}) async-start(bf16[8,512,128]{2,1,0:T(8,128)(2,1)} %bitcast.3), calls=%async_computation | async-start | bytes 2097152 | tf_op jit(solution)/shard_map/all_to_all | solution.py:214
  63.7 3.5 %collective-permute-start.14 = (bf16[4,256,512]{2,1,0:T(8,128)(2,1)S(1)}, bf16[4,256,512]{2,1,0:T(8,128)(2,1)}, u32[]{:S(2)}, u32[]{:S(2)}) collective-permute-start(bf16[4,256,512]{2,1,0:T(8,128)(2,1)S(1)} %pad_maximum_fusion.refs_0_), channel_id=1, source_target_pairs={{0,8},{1,9},{2,10},{3,11},{4,12},{5,13},{6,14},{7,15},{8,0},{9,1},... | collective-permute-start | bytes 3145736 | tf_op jit(solution)/shard_map/ppermute | solution.py:28
  67.2 23.5 %collective-permute-done.13.refs_3_ = bf16[4,256,512]{2,1,0:T(8,128)(2,1)S(1)} collective-permute-done((bf16[4,256,512]{2,1,0:T(8,128)(2,1)S(1)}, bf16[4,256,512]{2,1,0:T(8,128)(2,1)S(1)}, u32[]{:S(2)}, u32[]{:S(2)}) %collective-permute-start.13) | collective-permute-done | bytes 1048608 | tf_op jit(solution)/shard_map/ppermute | solution.py:28
  91.2 3.0 %collective-permute-done.11.refs_1_ = bf16[4,256,512]{2,1,0:T(8,128)(2,1)} collective-permute-done((bf16[4,256,512]{2,1,0:T(8,128)(2,1)S(1)}, bf16[4,256,512]{2,1,0:T(8,128)(2,1)}, u32[]{:S(2)}, u32[]{:S(2)}) %collective-permute-start.11) | collective-permute-done | bytes 1048608 | tf_op jit(solution)/shard_map/ppermute | solution.py:28
  94.3 2.7 %all-to-all-done.rows_hbm = bf16[8,512,128]{2,1,0:T(8,128)(2,1)S(1)} async-done(((bf16[8,512,128]{2,1,0:T(8,128)(2,1)}), bf16[8,512,128]{2,1,0:T(8,128)(2,1)S(1)}, u32[]{:S(2)}, u32[]{:S(2)}) %all-to-all-start) | async-done | bytes 1048608 | tf_op jit(solution)/shard_map/all_to_all | solution.py:214
  97.2 12.8 %apply.1 = bf16[8,512,128]{2,1,0:T(8,128)(2,1)S(1)} custom-call(s32[3]{0:T(128)S(1)} %pad_add_fusion.place, bf16[8,512,128]{2,1,0:T(8,128)(2,1)S(1)} %all-to-all-done.rows_hbm, bf16[512,4096]{1,0:T(8,128)(2,1)} %pot_hbm.1, bf16[4,256,512]{2,1,0:T(8,128)(2,1)S(1)} %pad_maximum_fusion.refs_0_, bf16[4,256,512]{2,1,0:T(8,128)(2,1)} %collective-permute-done.11.refs_1_, ...), custom_call_target="tpu_custom_call" | custom-call | flops 8589934592 | bytes 16777216 | tf_op jit(solution)/shard_map/apply/pallas_call | solution.py:185
  110.0 19.3 %all_to_all.10 = bf16[8,512,128]{2,1,0:T(8,128)(2,1)S(1)} all-to-all(bf16[8,512,128]{2,1,0:T(8,128)(2,1)S(1)} %apply.1), channel_id=1, replica_groups=mesh['grid'=32,'orb'=8] {'orb'}, dimensions={0} | all-to-all | bytes 2097152 | tf_op jit(solution)/shard_map/all_to_all | solution.py:224
  129.4 1.0 copy.5
  (26 shorter events, 3.2 us)
Async XLA Ops:
  0.0 5.7 %collective-permute-start = (bf16[4096,128]{1,0:T(8,128)(2,1)}, bf16[4096,128]{1,0:T(8,128)(2,1)S(1)}, u32[]{:S(2)}, u32[]{:S(2)}) collective-permute-start(bf16[4096,128]{1,0:T(8,128)(2,1)} %mine.1), channel_id=1, source_target_pairs={{0,8},{1,9},{2,10},{3,11},{4,12},{5,13},{6,14},{7,15},{8,0},{9,1},... | collective-permute-start | bytes 3145736 | tf_op jit(solution)/shard_map/ppermute | solution.py:28
  12.3 6.0 %collective-permute-start.1 = (bf16[128,512]{1,0:T(8,128)(2,1)S(1)}, bf16[128,512]{1,0:T(8,128)(2,1)S(1)}, u32[]{:S(2)}, u32[]{:S(2)}) collective-permute-start(bf16[128,512]{1,0:T(8,128)(2,1)S(1)} %get-tuple-element.10), channel_id=1, source_target_pairs={{0,64},{1,65},{2,66},{3,67},{4,68},{5,69},{6,70},{7,71},{8,72},{9,... | collective-permute-start | bytes 393224 | tf_op jit(solution)/shard_map/ppermute | solution.py:28
  12.4 7.8 %collective-permute-start.2 = (bf16[128,512]{1,0:T(8,128)(2,1)S(1)}, bf16[128,512]{1,0:T(8,128)(2,1)S(1)}, u32[]{:S(2)}, u32[]{:S(2)}) collective-permute-start(bf16[128,512]{1,0:T(8,128)(2,1)S(1)} %get-tuple-element.11), channel_id=1, source_target_pairs={{0,192},{1,193},{2,194},{3,195},{4,196},{5,197},{6,198},{7,199},{8... | collective-permute-start | bytes 393224 | tf_op jit(solution)/shard_map/ppermute | solution.py:28
  15.1 5.3 %collective-permute-start.3 = (bf16[128,512]{1,0:T(8,128)(2,1)S(1)}, bf16[128,512]{1,0:T(8,128)(2,1)S(1)}, u32[]{:S(2)}, u32[]{:S(2)}) collective-permute-start(bf16[128,512]{1,0:T(8,128)(2,1)S(1)} %get-tuple-element.12), channel_id=1, source_target_pairs={{0,128},{1,129},{2,130},{3,131},{4,132},{5,133},{6,134},{7,135},{8... | collective-permute-start | bytes 393224 | tf_op jit(solution)/shard_map/ppermute | solution.py:28
  20.5 9.7 %collective-permute-start.6 = (bf16[128,512]{1,0:T(8,128)(2,1)S(1)}, bf16[128,512]{1,0:T(8,128)(2,1)S(1)}, u32[]{:S(2)}, u32[]{:S(2)}) collective-permute-start(bf16[128,512]{1,0:T(8,128)(2,1)S(1)} %add_add_fusion.1), channel_id=1, source_target_pairs={{0,32},{1,33},{2,34},{3,35},{4,36},{5,37},{6,38},{7,39},{8,40},{9,... | collective-permute-start | bytes 393224 | tf_op jit(solution)/shard_map/ppermute | solution.py:28
  27.7 12.9 %collective-permute-start.5 = (bf16[128,512]{1,0:T(8,128)(2,1)S(1)}, bf16[128,512]{1,0:T(8,128)(2,1)S(1)}, u32[]{:S(2)}, u32[]{:S(2)}) collective-permute-start(bf16[128,512]{1,0:T(8,128)(2,1)S(1)} %add_add_fusion.1), channel_id=1, source_target_pairs={{0,48},{1,49},{2,50},{3,51},{4,52},{5,53},{6,54},{7,55},{8,56},{9,... | collective-permute-start | bytes 393224 | tf_op jit(solution)/shard_map/ppermute | solution.py:28
  27.7 12.9 %collective-permute-start.4 = (bf16[128,512]{1,0:T(8,128)(2,1)S(1)}, bf16[128,512]{1,0:T(8,128)(2,1)S(1)}, u32[]{:S(2)}, u32[]{:S(2)}) collective-permute-start(bf16[128,512]{1,0:T(8,128)(2,1)S(1)} %add_add_fusion.1), channel_id=1, source_target_pairs={{0,16},{1,17},{2,18},{3,19},{4,20},{5,21},{6,22},{7,23},{8,24},{9,... | collective-permute-start | bytes 393224 | tf_op jit(solution)/shard_map/ppermute | solution.py:28
  40.6 4.6 %collective-permute-start.7 = (bf16[128,512]{1,0:T(8,128)(2,1)S(1)}, bf16[128,512]{1,0:T(8,128)(2,1)S(1)}, u32[]{:S(2)}, u32[]{:S(2)}) collective-permute-start(bf16[128,512]{1,0:T(8,128)(2,1)S(1)} %add_add_fusion), channel_id=1, source_target_pairs={{0,1},{1,0},{2,3},{3,2},{4,5},{5,4},{6,7},{7,6},{8,9},{9,8},{10,11... | collective-permute-start | bytes 393224 | tf_op jit(solution)/shard_map/ppermute | solution.py:28
  45.3 5.6 %collective-permute-start.10 = (bf16[256,512]{1,0:T(8,128)(2,1)S(1)}, bf16[256,512]{1,0:T(8,128)(2,1)S(1)}, u32[]{:S(2)}, u32[]{:S(2)}) collective-permute-start(bf16[256,512]{1,0:T(8,128)(2,1)S(1)} %maximum_select_fusion.1), channel_id=1, source_target_pairs={{0,6},{1,7},{2,0},{3,1},{4,2},{5,3},{6,4},{7,5},{8,200},{9,201},{1... | collective-permute-start | bytes 786440 | tf_op jit(solution)/shard_map/ppermute | solution.py:28
  46.6 6.8 %collective-permute-start.9 = (bf16[256,512]{1,0:T(8,128)(2,1)S(1)}, bf16[256,512]{1,0:T(8,128)(2,1)S(1)}, u32[]{:S(2)}, u32[]{:S(2)}) collective-permute-start(bf16[256,512]{1,0:T(8,128)(2,1)S(1)} %maximum_select_fusion.1), channel_id=1, source_target_pairs={{0,4},{1,5},{2,6},{3,7},{4,0},{5,1},{6,2},{7,3},{8,136},{9,137},{1... | collective-permute-start | bytes 786440 | tf_op jit(solution)/shard_map/ppermute | solution.py:28
  47.7 8.7 %collective-permute-start.8 = (bf16[256,512]{1,0:T(8,128)(2,1)S(1)}, bf16[256,512]{1,0:T(8,128)(2,1)S(1)}, u32[]{:S(2)}, u32[]{:S(2)}) collective-permute-start(bf16[256,512]{1,0:T(8,128)(2,1)S(1)} %maximum_select_fusion.1), channel_id=1, source_target_pairs={{0,2},{1,3},{2,4},{3,5},{4,6},{5,7},{6,0},{7,1},{8,72},{9,73},{10,... | collective-permute-start | bytes 786440 | tf_op jit(solution)/shard_map/ppermute | solution.py:28
  56.5 34.2 %collective-permute-start.13 = (bf16[4,256,512]{2,1,0:T(8,128)(2,1)S(1)}, bf16[4,256,512]{2,1,0:T(8,128)(2,1)S(1)}, u32[]{:S(2)}, u32[]{:S(2)}) collective-permute-start(bf16[4,256,512]{2,1,0:T(8,128)(2,1)S(1)} %pad_maximum_fusion.refs_0_), channel_id=1, source_target_pairs={{0,192},{1,193},{2,194},{3,195},{4,196},{5,197},{6,198},{7,199},{8... | collective-permute-start | bytes 3145736 | tf_op jit(solution)/shard_map/ppermute | solution.py:28
  59.3 31.4 %collective-permute-start.12 = (bf16[4,256,512]{2,1,0:T(8,128)(2,1)S(1)}, bf16[4,256,512]{2,1,0:T(8,128)(2,1)}, u32[]{:S(2)}, u32[]{:S(2)}) collective-permute-start(bf16[4,256,512]{2,1,0:T(8,128)(2,1)S(1)} %pad_maximum_fusion.refs_0_), channel_id=1, source_target_pairs={{0,128},{1,129},{2,130},{3,131},{4,132},{5,133},{6,134},{7,135},{8... | collective-permute-start | bytes 3145736 | tf_op jit(solution)/shard_map/ppermute | solution.py:28
  59.6 34.6 %collective-permute-start.11 = (bf16[4,256,512]{2,1,0:T(8,128)(2,1)S(1)}, bf16[4,256,512]{2,1,0:T(8,128)(2,1)}, u32[]{:S(2)}, u32[]{:S(2)}) collective-permute-start(bf16[4,256,512]{2,1,0:T(8,128)(2,1)S(1)} %pad_maximum_fusion.refs_0_), channel_id=1, source_target_pairs={{0,64},{1,65},{2,66},{3,67},{4,68},{5,69},{6,70},{7,71},{8,10},{9,... | collective-permute-start | bytes 3145736 | tf_op jit(solution)/shard_map/ppermute | solution.py:28
  60.1 36.9 %all-to-all-start = ((bf16[8,512,128]{2,1,0:T(8,128)(2,1)}), bf16[8,512,128]{2,1,0:T(8,128)(2,1)S(1)}, u32[]{:S(2)}, u32[]{:S(2)}) async-start(bf16[8,512,128]{2,1,0:T(8,128)(2,1)} %bitcast.3), calls=%async_computation | async-start | bytes 2097152 | tf_op jit(solution)/shard_map/all_to_all | solution.py:214
  63.7 33.3 %collective-permute-start.14 = (bf16[4,256,512]{2,1,0:T(8,128)(2,1)S(1)}, bf16[4,256,512]{2,1,0:T(8,128)(2,1)}, u32[]{:S(2)}, u32[]{:S(2)}) collective-permute-start(bf16[4,256,512]{2,1,0:T(8,128)(2,1)S(1)} %pad_maximum_fusion.refs_0_), channel_id=1, source_target_pairs={{0,8},{1,9},{2,10},{3,11},{4,12},{5,13},{6,14},{7,15},{8,0},{9,1},... | collective-permute-start | bytes 3145736 | tf_op jit(solution)/shard_map/ppermute | solution.py:28
  90.7 6.3 %collective-permute-start.17 = (bf16[4,256,512]{2,1,0:T(8,128)(2,1)S(1)}, bf16[4,256,512]{2,1,0:T(8,128)(2,1)}, u32[]{:S(2)}, u32[]{:S(2)}) collective-permute-start(bf16[4,256,512]{2,1,0:T(8,128)(2,1)S(1)} %collective-permute-done.13.refs_3_), channel_id=1, source_target_pairs={{0,8},{1,9},{2,10},{3,11},{4,12},{5,13},{6,14},{7,15},{8,0},{9,1},... | collective-permute-start | bytes 3145736 | tf_op jit(solution)/shard_map/ppermute | solution.py:28
  90.7 6.3 %collective-permute-start.16 = (bf16[4,256,512]{2,1,0:T(8,128)(2,1)}, bf16[4,256,512]{2,1,0:T(8,128)(2,1)}, u32[]{:S(2)}, u32[]{:S(2)}) collective-permute-start(bf16[4,256,512]{2,1,0:T(8,128)(2,1)} %collective-permute-done.12.refs_2_), channel_id=1, source_target_pairs={{0,8},{1,9},{2,10},{3,11},{4,12},{5,13},{6,14},{7,15},{8,0},{9,1},... | collective-permute-start | bytes 3145736 | tf_op jit(solution)/shard_map/ppermute | solution.py:28
  94.2 3.0 %collective-permute-start.15 = (bf16[4,256,512]{2,1,0:T(8,128)(2,1)}, bf16[4,256,512]{2,1,0:T(8,128)(2,1)}, u32[]{:S(2)}, u32[]{:S(2)}) collective-permute-start(bf16[4,256,512]{2,1,0:T(8,128)(2,1)} %collective-permute-done.11.refs_1_), channel_id=1, source_target_pairs={{0,8},{1,9},{2,10},{3,11},{4,12},{5,13},{6,14},{7,15},{8,0},{9,1},... | collective-permute-start | bytes 3145736 | tf_op jit(solution)/shard_map/ppermute | solution.py:28

commit v2 on v1

v2 whole, which is shorter than its diff:
```python
import functools

import jax
import jax.numpy as jnp
from jax import lax
from jax.experimental import pallas as pl
from jax.experimental.pallas import tpu as pltpu
from jax.sharding import PartitionSpec as P

NY, NZH, NC, NX, NZL = 4, 4, 2, 4, 2
AXES = ("grid", "orb")
BLOCK = 512
HALF = 256


def moves(target):
    pairs = []
    for y in range(NY):
        for zh in range(NZH):
            for c in range(NC):
                for x in range(NX):
                    for zl in range(NZL):
                        ty, tzh, tc, tx, tzl = target(y, zh, c, x, zl)
                        src = ((y * NZH + zh) * NC + c) * NX * NZL + x * NZL + zl
                        dst = ((ty % NY * NZH + tzh % NZH) * NC + tc % NC) * NX * NZL + tx % NX * NZL + tzl % NZL
                        pairs.append((src, dst))
    return pairs


def send(value, target):
    return lax.ppermute(value, AXES, moves(target))


def to_core(value):
    return send(value, lambda y, zh, c, x, zl: (y, zh, 1 - c, x, zl))


def to_y(value, d):
    return send(value, lambda y, zh, c, x, zl: (y + d, zh, c, x, zl))


def to_zh(value, d):
    return send(value, lambda y, zh, c, x, zl: (y, zh + d, c, x, zl))


def to_zl(value):
    return send(value, lambda y, zh, c, x, zl: (y, zh, c, x, 1 - zl))


def first_axis(value, d):
    return send(value, lambda y, zh, c, x, zl: (y + d * c, zh, c, x + d * (1 - c), zl))


def second_axis(value, d):
    return send(value, lambda y, zh, c, x, zl: (y + d * (1 - c), zh, c, x + d * c, zl))


def table_kernel(place, index, slot_ref, where_ref):
    slab = place[0]
    idx = index[...]
    lines = idx.shape[0]
    owner = lax.shift_right_logical(idx, 12)
    in_mine = owner == slab
    in_other = owner == (slab ^ 1)
    flags = jnp.concatenate([in_mine.astype(jnp.float32), in_other.astype(jnp.float32)], axis=0)
    upper = (
        (lax.broadcasted_iota(jnp.int32, (128, 128), 0) <= lax.broadcasted_iota(jnp.int32, (128, 128), 1))
        .astype(jnp.float32)
        .astype(jnp.bfloat16)
    )
    counts = jnp.dot(flags.astype(jnp.bfloat16), upper, preferred_element_type=jnp.float32)
    totals = jnp.broadcast_to(counts[:, 127:128], (2 * lines, 128)).astype(jnp.bfloat16)
    to = lax.broadcasted_iota(jnp.int32, (2 * lines, 2 * lines), 0)
    of = lax.broadcasted_iota(jnp.int32, (2 * lines, 2 * lines), 1)
    earlier = ((of < to) & ((of < lines) == (to < lines))).astype(jnp.float32).astype(jnp.bfloat16)
    ranks = counts + jnp.dot(earlier, totals, preferred_element_type=jnp.float32) - 1.0
    slot = jnp.where(in_mine, ranks[:lines], jnp.where(in_other, ranks[lines:] + 256.0, -1.0)).astype(jnp.int32)
    slot_ref[...] = slot
    local = idx & 4095
    high = lax.shift_right_logical(local, 6).astype(jnp.float32)
    low = (local & 63).astype(jnp.float32)
    where = jnp.zeros((BLOCK, 8), jnp.float32)
    rows = lax.broadcasted_iota(jnp.int32, (BLOCK, BLOCK), 0)
    pick_row = lax.broadcasted_iota(jnp.int32, (8, BLOCK), 0)

    def line(value, b):
        return jnp.concatenate([value[i : i + 1, :] for i in range(4 * b, 4 * b + 4)], axis=1)

    for b in range(8):
        one_hot = (rows == line(slot, b)).astype(jnp.float32).astype(jnp.bfloat16)
        parts = jnp.where(pick_row == 0, line(high, b), jnp.where(pick_row == 1, line(low, b), 0.0))
        where = where + lax.dot_general(
            one_hot, parts.astype(jnp.bfloat16), (((1,), (1,)), ((), ())), preferred_element_type=jnp.float32
        )
    where_ref[...] = where


def tables(place, index):
    vmem = pl.BlockSpec(memory_space=pltpu.VMEM)
    return pl.pallas_call(
        table_kernel,
        out_shape=[jax.ShapeDtypeStruct(index.shape, jnp.int32), jax.ShapeDtypeStruct((BLOCK, 8), jnp.float32)],
        in_specs=[pl.BlockSpec(memory_space=pltpu.SMEM), vmem],
        out_specs=[vmem] * 2,
        compiler_params=pltpu.CompilerParams(vmem_limit_bytes=16 * 1024 * 1024),
        name="tables",
    )(place, index)


def pick_kernel(place, slot_ref, where_ref, mine, other_hbm, *refs):
    outs, other, other_sem = refs[:4], refs[4], refs[5]
    other_copy = pltpu.make_async_copy(other_hbm, other, other_sem)
    other_copy.start()
    half, y = place[1], place[2]
    where = where_ref[...]
    line = (where[:, 0:1] * 64.0 + where[:, 1:2]).astype(jnp.int32)
    picked = []
    wide = 1024
    lane = lax.broadcasted_iota(jnp.int32, (256, wide), 1)
    for s, block in enumerate((mine, other)):
        if s == 1:
            other_copy.wait()
        want = line[s * 256 : (s + 1) * 256, :]
        total = jnp.zeros((256, 128), jnp.float32)
        for k in range(4096 // wide):
            one_hot = (want - k * wide == lane).astype(jnp.float32).astype(jnp.bfloat16)
            total = total + jnp.dot(one_hot, block[k * wide : (k + 1) * wide, :], preferred_element_type=jnp.float32)
        picked.append(total)
    turned = jnp.concatenate(picked, axis=0).T.astype(jnp.bfloat16)
    rows = lax.broadcasted_iota(jnp.int32, (BLOCK, BLOCK), 0)
    for d in range(4):
        b = half * 4 + lax.rem(y + d, 4)
        four = slot_ref[pl.ds(b * 4, 4), :]
        row = jnp.concatenate([four[i : i + 1, :] for i in range(4)], axis=1)
        one_hot = (rows == row).astype(jnp.float32).astype(jnp.bfloat16)
        values = jnp.dot(turned, one_hot, preferred_element_type=jnp.float32).astype(jnp.bfloat16)
        outs[d][0] = values[:, :HALF]
        outs[d][1] = values[:, HALF:]


def pick(place, slot, where, mine, other):
    block = jax.ShapeDtypeStruct((2, 128, HALF), jnp.bfloat16)
    vmem = pl.BlockSpec(memory_space=pltpu.VMEM)
    return pl.pallas_call(
        pick_kernel,
        out_shape=[block] * 4,
        in_specs=[pl.BlockSpec(memory_space=pltpu.SMEM), vmem, vmem, vmem, pl.BlockSpec(memory_space=pl.ANY)],
        out_specs=[vmem] * 4,
        scratch_shapes=[pltpu.VMEM(other.shape, other.dtype), pltpu.SemaphoreType.DMA],
        compiler_params=pltpu.CompilerParams(vmem_limit_bytes=16 * 1024 * 1024),
        name="pick",
    )(place, slot, where, mine, other)


def join_kernel(place, *refs):
    pieces, messages = refs[:4], refs[4:6]
    core = place[2]
    for c in range(2):

        @pl.when(core == c)
        def _():
            for d in range(4):
                for dz in range(2):
                    for half in range(2):
                        value = pieces[d][dz, half]
                        if c == 0:
                            messages[half][d, dz] = value
                        else:
                            messages[d // 2][d % 2 * 2 + half, dz] = value


def join(place, pieces):
    vmem = pl.BlockSpec(memory_space=pltpu.VMEM)
    message = jax.ShapeDtypeStruct((4, 2, 128, HALF), jnp.bfloat16)
    return pl.pallas_call(
        join_kernel,
        out_shape=[message] * 2,
        in_specs=[pl.BlockSpec(memory_space=pltpu.SMEM)] + [vmem] * 4,
        out_specs=[vmem] * 2,
        compiler_params=pltpu.CompilerParams(vmem_limit_bytes=16 * 1024 * 1024),
        name="join",
    )(place, *pieces)


def pack_kernel(place, *refs):
    core = place[2]
    sources, outs, sem = refs[:2], refs[2:4], refs[4]
    copies = []
    for s in range(2):
        for b in range(8):
            lanes = pl.ds(pl.multiple_of((core * 8 + b) * HALF, HALF), HALF)
            copies.append(pltpu.make_async_copy(sources[s].at[:, lanes], outs[s].at[b], sem.at[s, b]))
    for copy in copies:
        copy.start()
    for copy in copies:
        copy.wait()


def pack(place, mine, theirs):
    anyspace = pl.BlockSpec(memory_space=pl.ANY)
    return pl.pallas_call(
        pack_kernel,
        out_shape=[jax.ShapeDtypeStruct((8, mine.shape[0], HALF), jnp.bfloat16)] * 2,
        in_specs=[pl.BlockSpec(memory_space=pltpu.SMEM), anyspace, anyspace],
        out_specs=[pl.BlockSpec(memory_space=pltpu.VMEM)] * 2,
        scratch_shapes=[pltpu.SemaphoreType.DMA((2, 8))],
        compiler_params=pltpu.CompilerParams(vmem_limit_bytes=16 * 1024 * 1024),
        name="pack",
    )(place, mine, theirs)


def apply_kernel(half, sides, place, *refs):
    number = len(sides)
    row_refs, refs = refs[:number], refs[number:]
    pot_refs, refs = refs[:number], refs[number:]
    messages, refs = refs[:4], refs[4:]
    if half == 1:
        before, refs = refs[0], refs[1:]
    outs, (rows, weighted) = refs[:number], refs[number:]
    each = row_refs[0].shape[1]
    x, y, core, zl = place[0], place[1], place[2], place[3]

    def pot_block(k):
        first = lax.rem(y - k + 4, 4) * 2 + half
        second = lax.rem(y - (half * 2 + k // 2) + 4, 4) * 2 + k % 2
        return jnp.where(core == 0, first, second)

    for k in range(8):
        block = lax.rem(x - k // 2 + 4, 4) * 2 + (zl ^ (k % 2))
        for s in range(number):
            rows[s * each : (s + 1) * each, k * 128 : (k + 1) * 128] = row_refs[s][block]

    def work(c):
        for k in range(4):
            if c == 0:
                value = messages[k][...].reshape(1024, HALF)
            else:
                value = jnp.concatenate([messages[e][k].reshape(HALF, HALF) for e in range(4)], axis=0)
            density = jnp.dot(rows[...], value, preferred_element_type=jnp.float32)
            for s in range(number):
                part = slice(s * each, (s + 1) * each)
                pot = pot_refs[s][pot_block(k)].astype(jnp.float32)
                weighted[part, k * HALF : (k + 1) * HALF] = (pot * density[part]).astype(jnp.bfloat16)
        for n in range(4):
            lanes = slice(n * HALF, (n + 1) * HALF)
            if c == 0:
                parts = [messages[e][n].reshape(HALF, HALF) for e in range(4)]
            else:
                parts = [messages[n][k].reshape(HALF, HALF) for k in range(4)]
            total = lax.dot_general(
                weighted[...],
                jnp.concatenate(parts, axis=1),
                (((1,), (1,)), ((), ())),
                preferred_element_type=jnp.float32,
            )
            if half == 0:
                for s in range(number):
                    outs[s][:, lanes] = total[s * each : (s + 1) * each]
            else:
                outs[0][:, lanes] = (before[:, lanes] + total).astype(outs[0].dtype)

    for c in range(2):

        @pl.when(core == c)
        def _():
            work(c)


def apply(half, place, rows, pots, messages, before=None, dtype=jnp.float32):
    vmem = pl.BlockSpec(memory_space=pltpu.VMEM)
    number, each = len(rows), pots[0].shape[1]
    extra = [before] if half == 1 else []
    out = jax.ShapeDtypeStruct((each, 1024), dtype)
    return pl.pallas_call(
        functools.partial(apply_kernel, half, tuple(range(number))),
        out_shape=[out] * number,
        in_specs=[pl.BlockSpec(memory_space=pltpu.SMEM)]
        + [vmem] * (2 * number + 4 + len(extra)),
        out_specs=[vmem] * number,
        scratch_shapes=[
            pltpu.VMEM((number * each, 1024), jnp.bfloat16),
            pltpu.VMEM((number * each, 1024), jnp.bfloat16),
        ],
        compiler_params=pltpu.CompilerParams(vmem_limit_bytes=16 * 1024 * 1024),
        cost_estimate=pl.CostEstimate(
            flops=number * each * 4 * 1024 * 1024, bytes_accessed=number * 4 * 1024 * 1024, transcendentals=0
        ),
        name="apply_high" if half else "apply_low",
    )(place, *rows, *pots, *messages, *extra)


def total_kernel(place, mine, theirs, out):
    x, zl = place[0], place[3]
    for k in range(8):
        block = lax.rem(x - k // 2 + 4, 4) * 2 + (zl ^ (k % 2))
        lanes = slice(k * 128, (k + 1) * 128)
        out[block] = (-(mine[:, lanes] + theirs[:, lanes].astype(jnp.float32))).astype(jnp.bfloat16)


def total(place, mine, theirs):
    vmem = pl.BlockSpec(memory_space=pltpu.VMEM)
    return pl.pallas_call(
        total_kernel,
        out_shape=jax.ShapeDtypeStruct((8, mine.shape[0], 128), jnp.bfloat16),
        in_specs=[pl.BlockSpec(memory_space=pltpu.SMEM), vmem, vmem],
        out_specs=vmem,
        compiler_params=pltpu.CompilerParams(vmem_limit_bytes=16 * 1024 * 1024),
        name="total",
    )(place, mine, theirs)


def shards(orbitals, potentials, point_index):
    grid, orb = lax.axis_index("grid"), lax.axis_index("orb")
    c = lax.rem(grid, NC)
    y = lax.div(grid, NZH * NC)
    x, zl = lax.div(orb, NZL), lax.rem(orb, NZL)
    pick_place = jnp.stack([grid, c, y]).astype(jnp.int32)
    place = jnp.stack([x, y, c, zl]).astype(jnp.int32)

    other = to_core(orbitals)
    other_pot = to_core(potentials)
    rows_here = lax.all_to_all(orbitals.reshape(8, -1, 128), "orb", split_axis=0, concat_axis=0, tiled=True)
    slot, where = tables(pick_place, point_index.reshape(-1, 128))
    blocks = pick(pick_place, slot, where, orbitals, other)
    here = blocks[0] + to_y(blocks[1], 1) + to_y(blocks[3], 3) + to_y(blocks[2], 2)
    here, rows_here = lax.optimization_barrier((here, rows_here))
    around = [to_zh(here, 1), to_zh(here, 3), to_zh(here, 2)]
    pots = pack(place, potentials, other_pot)
    around, pots = lax.optimization_barrier((around, pots))
    here = here + around[0] + around[1] + around[2]
    beside = to_zl(here)
    pair = jnp.stack([here, beside])
    pieces = [pair] + [first_axis(pair, d) for d in (1, 2, 3)]
    rows = [rows_here, to_core(rows_here)]
    low, high = join(place, pieces)
    low_up, low_down = second_axis(low, 1), second_axis(low, 3)
    high_up, high_down = second_axis(high, 1), second_axis(high, 3)
    lows = [low, low_up, second_axis(low_up, 1), low_down]
    highs = [high, high_up, second_axis(high_down, 3), high_down]
    parts = apply(0, place, rows, pots, lows)
    (sent,) = apply(1, place, rows[1:], pots[1:], highs, parts[1], jnp.bfloat16)
    theirs = to_core(sent)
    (kept,) = apply(1, place, rows[:1], pots[:1], highs, parts[0])
    result = total(place, kept, theirs)
    return lax.all_to_all(result, "orb", split_axis=0, concat_axis=0, tiled=True).reshape(-1, 128)


def solution(mesh):
    return jax.shard_map(
        shards,
        mesh=mesh,
        in_specs=(P("grid", "orb"), P(("grid", "orb"), None), P()),
        out_specs=P("grid", "orb"),
        check_vma=False,
    )
```

time: 131 us -> 118 us (0.901)
  waiting for transfers between devices: 60.2 us -> 27.8 us
  starting transfers between devices: 29.2 us -> 44.8 us
  Pallas kernels: 19.4 us -> 21.5 us
  local copies, waits for them, and re-layouts: 1.69 us -> 3.17 us
    ppermute x18 -> x20, waiting for transfers between devices: 57.5 us -> 27.8 us  [send(): return lax.ppermute(value, AXES, moves(target))]
    ppermute x18 -> x20, starting transfers between devices: 25.6 us -> 41.2 us  [send(): return lax.ppermute(value, AXES, moves(target))]
    pallas_call x1 -> x7, Pallas kernels: 12.8 us -> 18.4 us  [the longest x3 12.3 us: apply(): pl.pallas_call(functools.partial(apply_kernel, half, tuple(range(number))...]
    pallas_call x1, Pallas kernels: 6.6 us -> 3.02 us  [pick(): pl.pallas_call(pick_kernel, out_shape=[block] * 4, in_specs=[pl.BlockSpec...]
    all_to_all x1, waiting for transfers between devices: 2.67 us -> 0.01 us  [shards(): lax.all_to_all(orbitals.reshape(8, -1, 128), 'orb', split_axis=0, concat_...]
    unnamed x1 -> x7, local copies, waits for them, and re-layouts: 0.97 us -> 3.17 us
  transfers between devices with their start and end apart: 19 -> 21, of which waited for: 14 -> 13; matrix products, arithmetic and copies ran while one was open for 1% -> 0% of each run, Pallas kernels for 0% -> 15%
where the time goes in v2:
time: 118 us; the launch traced here: 117 us
  starting transfers between devices  44.8 us (38%)
  waiting for transfers between devices  27.8 us (24%)
  Pallas kernels  21.5 us (18%)
  blocking collectives  19.8 us (17%)
  local copies, waits for them, and re-layouts  3.17 us (3%)
    ppermute x20, starting transfers between devices, send(): return lax.ppermute(value, AXES, moves(target))  41.2 us
    ppermute x20, waiting for transfers between devices, send(): return lax.ppermute(value, AXES, moves(target))  27.8 us
    all_to_all x1, blocking collectives, shards(): lax.all_to_all(result, 'orb', split_axis=0, concat_axis=0, tiled=True)  19.8 us
    pallas_call x3, Pallas kernels, apply(): pl.pallas_call(functools.partial(apply_kernel, half, tuple(range(number))...  12.3 us
    all_to_all x1, starting transfers between devices, shards(): lax.all_to_all(orbitals.reshape(8, -1, 128), 'orb', split_axis=0, concat_...  3.64 us
    unnamed x7, local copies, waits for them, and re-layouts  3.17 us
    pallas_call x1, Pallas kernels, pick(): pl.pallas_call(pick_kernel, out_shape=[block] * 4, in_specs=[pl.BlockSpec...  3.02 us
    pallas_call x1, Pallas kernels, pack(): pl.pallas_call(pack_kernel, out_shape=[jax.ShapeDtypeStruct((8, mine.shap...  2.51 us
  transfers between devices with their start and end apart: 21, of which 13 were waited for; matrix products, arithmetic and copies ran while one was open for 0% of the time, Pallas kernels for 15%

profile of v2, /device:TPU:1, one launch (start us, length us, event | category | flops | bytes accessed | tf_op | source)
XLA Modules:
  0.0 117.4 jit_solution(17764741672677213984)
XLA Ops:
  0.0 3.2 %collective-permute-start.7 = (bf16[512,4096]{1,0:T(8,128)(2,1)}, bf16[512,4096]{1,0:T(8,128)(2,1)}, u32[]{:S(2)}, u32[]{:S(2)}) collective-permute-start(bf16[512,4096]{1,0:T(8,128)(2,1)} %refs_0_.1), channel_id=1, source_target_pairs={{0,8},{1,9},{2,10},{3,11},{4,12},{5,13},{6,14},{7,15},{8,0},{9,1},... | collective-permute-start | bytes 12582920 | tf_op jit(solution)/shard_map/ppermute | solution.py:31
  3.2 3.6 %all-to-all-start = ((bf16[8,512,128]{2,1,0:T(8,128)(2,1)}), bf16[8,512,128]{2,1,0:T(8,128)(2,1)S(1)}, u32[]{:S(2)}, u32[]{:S(2)}) async-start(bf16[8,512,128]{2,1,0:T(8,128)(2,1)} %bitcast.10), calls=%async_computation | async-start | bytes 2097152 | tf_op jit(solution)/shard_map/all_to_all | solution.py:322
  7.5 2.1 %tables.1 = (s32[32,128]{1,0:T(8,128)S(1)}, f32[512,8]{1,0:T(8,128)S(1)}) custom-call(s32[3]{0:T(128)S(1)} %pad_add_fusion.1.place, s32[32,128]{1,0:T(8,128)S(1)} %bitcast.11), custom_call_target="tpu_custom_call" | custom-call | tf_op jit(solution)/shard_map/tables/pallas_call | solution.py:100
  11.5 3.0 %pick.1 = (bf16[2,128,256]{2,1,0:T(8,128)(2,1)S(1)}, bf16[2,128,256]{2,1,0:T(8,128)(2,1)S(1)}, bf16[2,128,256]{2,1,0:T(8,128)(2,1)S(1)}, bf16[2,128,256]{2,1,0:T(8,128)(2,1)S(1)}) custom-call(s32[3]{0:T(128)S(1)} %pad_add_fusion.1.place, s32[32,128]{1,0:T(8,128)S(1)} %get-tuple-element.24.slot_ref, f32[512,8]{1,0:T(8,128)S(1)} %get-tuple-element.25.where_ref, ...), custom_call_target="tpu_custom_call" | custom-call | tf_op jit(solution)/shard_map/pick/pallas_call | solution.py:144
  14.7 2.7 %collective-permute-start.2 = (bf16[2,128,256]{2,1,0:T(8,128)(2,1)S(1)}, bf16[2,128,256]{2,1,0:T(8,128)(2,1)S(1)}, u32[]{:S(2)}, u32[]{:S(2)}) collective-permute-start(bf16[2,128,256]{2,1,0:T(8,128)(2,1)S(1)} %get-tuple-element.28), channel_id=1, source_target_pairs={{0,192},{1,193},{2,194},{3,195},{4,196},{5,197},{6,198},{7,199},{8... | collective-permute-start | bytes 393224 | tf_op jit(solution)/shard_map/ppermute | solution.py:31
  17.3 3.2 %collective-permute-done.1 = bf16[2,128,256]{2,1,0:T(8,128)(2,1)S(1)} collective-permute-done((bf16[2,128,256]{2,1,0:T(8,128)(2,1)S(1)}, bf16[2,128,256]{2,1,0:T(8,128)(2,1)S(1)}, u32[]{:S(2)}, u32[]{:S(2)}) %collective-permute-start.1) | collective-permute-done | bytes 131104 | tf_op jit(solution)/shard_map/ppermute | solution.py:31
  23.0 3.0 %collective-permute-start.4 = (bf16[2,128,256]{2,1,0:T(8,128)(2,1)S(1)}, bf16[2,128,256]{2,1,0:T(8,128)(2,1)S(1)}, u32[]{:S(2)}, u32[]{:S(2)}) collective-permute-start(bf16[2,128,256]{2,1,0:T(8,128)(2,1)S(1)} %add_add_fusion.1), channel_id=1, source_target_pairs={{0,16},{1,17},{2,18},{3,19},{4,20},{5,21},{6,22},{7,23},{8,24},{9,... | collective-permute-start | bytes 393224 | tf_op jit(solution)/shard_map/ppermute | solution.py:31
  26.0 3.1 %collective-permute-start.5 = (bf16[2,128,256]{2,1,0:T(8,128)(2,1)S(1)}, bf16[2,128,256]{2,1,0:T(8,128)(2,1)S(1)}, u32[]{:S(2)}, u32[]{:S(2)}) collective-permute-start(bf16[2,128,256]{2,1,0:T(8,128)(2,1)S(1)} %add_add_fusion.1), channel_id=1, source_target_pairs={{0,48},{1,49},{2,50},{3,51},{4,52},{5,53},{6,54},{7,55},{8,56},{9,... | collective-permute-start | bytes 393224 | tf_op jit(solution)/shard_map/ppermute | solution.py:31
  29.1 4.4 %collective-permute-start.6 = (bf16[2,128,256]{2,1,0:T(8,128)(2,1)S(1)}, bf16[2,128,256]{2,1,0:T(8,128)(2,1)S(1)}, u32[]{:S(2)}, u32[]{:S(2)}) collective-permute-start(bf16[2,128,256]{2,1,0:T(8,128)(2,1)S(1)} %add_add_fusion.1), channel_id=1, source_target_pairs={{0,32},{1,33},{2,34},{3,35},{4,36},{5,37},{6,38},{7,39},{8,40},{9,... | collective-permute-start | bytes 393224 | tf_op jit(solution)/shard_map/ppermute | solution.py:31
  33.6 2.2 %copy-done = bf16[512,4096]{1,0:T(8,128)(2,1)S(1)} copy-done((bf16[512,4096]{1,0:T(8,128)(2,1)S(1)}, bf16[512,4096]{1,0:T(8,128)(2,1)}, u32[]{:S(2)}) %copy-start) | copy-done | bytes 4194328
  35.8 2.5 %pack.1 = (bf16[8,512,256]{2,1,0:T(8,128)(2,1)S(1)}, bf16[8,512,256]{2,1,0:T(8,128)(2,1)S(1)}) custom-call(s32[4]{0:T(128)S(1)} %pad_add_fusion.place, bf16[512,4096]{1,0:T(8,128)(2,1)S(1)} %copy-done, bf16[512,4096]{1,0:T(8,128)(2,1)} %collective-permute-done.7.refs_1_), custom_call_target="tpu_custom_call" | custom-call | tf_op jit(solution)/shard_map/pack/pallas_call | solution.py:201
  38.5 3.1 %collective-permute-done.6 = bf16[2,128,256]{2,1,0:T(8,128)(2,1)S(1)} collective-permute-done((bf16[2,128,256]{2,1,0:T(8,128)(2,1)S(1)}, bf16[2,128,256]{2,1,0:T(8,128)(2,1)S(1)}, u32[]{:S(2)}, u32[]{:S(2)}) %collective-permute-start.6) | collective-permute-done | bytes 131104 | tf_op jit(solution)/shard_map/ppermute | solution.py:31
  41.6 3.6 %collective-permute-start.8 = (bf16[2,128,256]{2,1,0:T(8,128)(2,1)S(1)}, bf16[2,128,256]{2,1,0:T(8,128)(2,1)S(1)}, u32[]{:S(2)}, u32[]{:S(2)}) collective-permute-start(bf16[2,128,256]{2,1,0:T(8,128)(2,1)S(1)} %add_add_fusion), channel_id=1, source_target_pairs={{0,1},{1,0},{2,3},{3,2},{4,5},{5,4},{6,7},{7,6},{8,9},{9,8},{10,11... | collective-permute-start | bytes 393224 | tf_op jit(solution)/shard_map/ppermute | solution.py:31
  45.2 2.4 %collective-permute-done.8 = bf16[2,128,256]{2,1,0:T(8,128)(2,1)S(1)} collective-permute-done((bf16[2,128,256]{2,1,0:T(8,128)(2,1)S(1)}, bf16[2,128,256]{2,1,0:T(8,128)(2,1)S(1)}, u32[]{:S(2)}, u32[]{:S(2)}) %collective-permute-start.8) | collective-permute-done | bytes 131104 | tf_op jit(solution)/shard_map/ppermute | solution.py:31
  48.3 2.0 %collective-permute-start.11 = (bf16[2,2,128,256]{3,2,1,0:T(8,128)(2,1)S(1)}, bf16[2,2,128,256]{3,2,1,0:T(8,128)(2,1)S(1)}, u32[]{:S(2)}, u32[]{:S(2)}) collective-permute-start(bf16[2,2,128,256]{3,2,1,0:T(8,128)(2,1)S(1)} %pad_maximum_fusion.refs_0_), channel_id=1, source_target_pairs={{0,6},{1,7},{2,0},{3,1},{4,2},{5,3},{6,4},{7,5},{8,200},{9,201},{1... | collective-permute-start | bytes 786440 | tf_op jit(solution)/shard_map/ppermute | solution.py:31
  50.3 4.8 %collective-permute-start.15 = (bf16[8,512,128]{2,1,0:T(8,128)(2,1)S(1)}, bf16[8,512,128]{2,1,0:T(8,128)(2,1)S(1)}, u32[]{:S(2)}, u32[]{:S(2)}) collective-permute-start(bf16[8,512,128]{2,1,0:T(8,128)(2,1)S(1)} %all-to-all-done.refs_0_), channel_id=1, source_target_pairs={{0,8},{1,9},{2,10},{3,11},{4,12},{5,13},{6,14},{7,15},{8,0},{9,1},... | collective-permute-start | bytes 3145736 | tf_op jit(solution)/shard_map/ppermute | solution.py:31
  62.2 5.5 %collective-permute-done.16.refs_5_ = bf16[4,2,128,256]{3,2,1,0:T(8,128)(2,1)S(1)} collective-permute-done((bf16[4,2,128,256]{3,2,1,0:T(8,128)(2,1)S(1)}, bf16[4,2,128,256]{3,2,1,0:T(8,128)(2,1)S(1)}, u32[]{:S(2)}, u32[]{:S(2)}) %collective-permute-start.16) | collective-permute-done | bytes 524320 | tf_op jit(solution)/shard_map/ppermute | solution.py:31
  70.4 2.7 %collective-permute-done.18.refs_7_ = bf16[4,2,128,256]{3,2,1,0:T(8,128)(2,1)S(1)} collective-permute-done((bf16[4,2,128,256]{3,2,1,0:T(8,128)(2,1)S(1)}, bf16[4,2,128,256]{3,2,1,0:T(8,128)(2,1)S(1)}, u32[]{:S(2)}, u32[]{:S(2)}) %collective-permute-start.18) | collective-permute-done | bytes 524320 | tf_op jit(solution)/shard_map/ppermute | solution.py:31
  73.2 3.8 %collective-permute-done.17.refs_6_ = bf16[4,2,128,256]{3,2,1,0:T(8,128)(2,1)S(1)} collective-permute-done((bf16[4,2,128,256]{3,2,1,0:T(8,128)(2,1)S(1)}, bf16[4,2,128,256]{3,2,1,0:T(8,128)(2,1)S(1)}, u32[]{:S(2)}, u32[]{:S(2)}) %collective-permute-start.17) | collective-permute-done | bytes 524320 | tf_op jit(solution)/shard_map/ppermute | solution.py:31
  77.0 5.7 %apply_low.1 = (f32[512,1024]{1,0:T(8,128)S(1)}, f32[512,1024]{1,0:T(8,128)S(1)}) custom-call(s32[4]{0:T(128)S(1)} %pad_add_fusion.place, bf16[8,512,128]{2,1,0:T(8,128)(2,1)S(1)} %all-to-all-done.refs_0_, bf16[8,512,128]{2,1,0:T(8,128)(2,1)S(1)} %collective-permute-done.15.refs_1_.refs_0_, bf16[8,512,256]{2,1,0:T(8,128)(2,1)S(1)} %get-tuple-element.34.refs_2_.refs_1_, ...), custom_call_target="tpu_custom_call" | custom-call | flops 4294967296 | bytes 8388608 | tf_op jit(solution)/shard_map/apply_low/pallas_call | solution.py:274
  82.9 3.4 %apply_high.3 = bf16[512,1024]{1,0:T(8,128)(2,1)S(1)} custom-call(s32[4]{0:T(128)S(1)} %pad_add_fusion.place, bf16[8,512,128]{2,1,0:T(8,128)(2,1)S(1)} %collective-permute-done.15.refs_1_.refs_0_, bf16[8,512,256]{2,1,0:T(8,128)(2,1)S(1)} %get-tuple-element.39.refs_3_.refs_1_, bf16[4,2,128,256]{3,2,1,0:T(8,128)(2,1)S(1)} %get-tuple-element.38.refs_2_, ...), custom_call_target="tpu_custom_call" | custom-call | flops 2147483648 | bytes 4194304 | tf_op jit(solution)/shard_map/apply_high/pallas_call | solution.py:274
  86.3 6.2 %collective-permute-start.19 = (bf16[512,1024]{1,0:T(8,128)(2,1)S(1)}, bf16[512,1024]{1,0:T(8,128)(2,1)S(1)}, u32[]{:S(2)}, u32[]{:S(2)}) collective-permute-start(bf16[512,1024]{1,0:T(8,128)(2,1)S(1)} %apply_high.3), channel_id=1, source_target_pairs={{0,8},{1,9},{2,10},{3,11},{4,12},{5,13},{6,14},{7,15},{8,0},{9,1},... | collective-permute-start | bytes 3145736 | tf_op jit(solution)/shard_map/ppermute | solution.py:31
  92.5 3.2 %apply_high.2.mine = f32[512,1024]{1,0:T(8,128)S(1)} custom-call(s32[4]{0:T(128)S(1)} %pad_add_fusion.place, bf16[8,512,128]{2,1,0:T(8,128)(2,1)S(1)} %all-to-all-done.refs_0_, bf16[8,512,256]{2,1,0:T(8,128)(2,1)S(1)} %get-tuple-element.34.refs_2_.refs_1_, bf16[4,2,128,256]{3,2,1,0:T(8,128)(2,1)S(1)} %get-tuple-element.38.refs_2_, ...), custom_call_target="tpu_custom_call" | custom-call | flops 2147483648 | bytes 4194304 | tf_op jit(solution)/shard_map/apply_high/pallas_call | solution.py:274
  96.7 19.8 %all_to_all.10 = bf16[8,512,128]{2,1,0:T(8,128)(2,1)S(1)} all-to-all(bf16[8,512,128]{2,1,0:T(8,128)(2,1)S(1)} %total.1), channel_id=1, replica_groups=mesh['grid'=32,'orb'=8] {'orb'}, dimensions={0} | all-to-all | bytes 2097152 | tf_op jit(solution)/shard_map/all_to_all | solution.py:345
  (39 shorter events, 18.0 us)
Async XLA Ops:
  0.0 6.9 %copy-start.1 = (bf16[4096,128]{1,0:T(8,128)(2,1)S(1)}, bf16[4096,128]{1,0:T(8,128)(2,1)}, u32[]{:S(2)}) copy-start(bf16[4096,128]{1,0:T(8,128)(2,1)} %mine.1) | copy-start | bytes 3145732
  0.0 7.5 %copy-start.2 = (s32[4096]{0:T(1024)S(1)}, s32[4096]{0:T(1024)}, u32[]{:S(2)}) copy-start(s32[4096]{0:T(1024)} %param.5) | copy-start | bytes 49156
  0.0 33.6 %collective-permute-start.7 = (bf16[512,4096]{1,0:T(8,128)(2,1)}, bf16[512,4096]{1,0:T(8,128)(2,1)}, u32[]{:S(2)}, u32[]{:S(2)}) collective-permute-start(bf16[512,4096]{1,0:T(8,128)(2,1)} %refs_0_.1), channel_id=1, source_target_pairs={{0,8},{1,9},{2,10},{3,11},{4,12},{5,13},{6,14},{7,15},{8,0},{9,1},... | collective-permute-start | bytes 12582920 | tf_op jit(solution)/shard_map/ppermute | solution.py:31
  3.2 19.7 %all-to-all-start = ((bf16[8,512,128]{2,1,0:T(8,128)(2,1)}), bf16[8,512,128]{2,1,0:T(8,128)(2,1)S(1)}, u32[]{:S(2)}, u32[]{:S(2)}) async-start(bf16[8,512,128]{2,1,0:T(8,128)(2,1)} %bitcast.10), calls=%async_computation | async-start | bytes 2097152 | tf_op jit(solution)/shard_map/all_to_all | solution.py:322
  6.9 4.6 %collective-permute-start = (bf16[4096,128]{1,0:T(8,128)(2,1)S(1)}, bf16[4096,128]{1,0:T(8,128)(2,1)S(1)}, u32[]{:S(2)}, u32[]{:S(2)}) collective-permute-start(bf16[4096,128]{1,0:T(8,128)(2,1)S(1)} %copy-done.1), channel_id=1, source_target_pairs={{0,8},{1,9},{2,10},{3,11},{4,12},{5,13},{6,14},{7,15},{8,0},{9,1},... | collective-permute-start | bytes 3145736 | tf_op jit(solution)/shard_map/ppermute | solution.py:31
  14.6 6.0 %collective-permute-start.1 = (bf16[2,128,256]{2,1,0:T(8,128)(2,1)S(1)}, bf16[2,128,256]{2,1,0:T(8,128)(2,1)S(1)}, u32[]{:S(2)}, u32[]{:S(2)}) collective-permute-start(bf16[2,128,256]{2,1,0:T(8,128)(2,1)S(1)} %get-tuple-element.27), channel_id=1, source_target_pairs={{0,64},{1,65},{2,66},{3,67},{4,68},{5,69},{6,70},{7,71},{8,72},{9,... | collective-permute-start | bytes 393224 | tf_op jit(solution)/shard_map/ppermute | solution.py:31
  14.7 7.8 %collective-permute-start.2 = (bf16[2,128,256]{2,1,0:T(8,128)(2,1)S(1)}, bf16[2,128,256]{2,1,0:T(8,128)(2,1)S(1)}, u32[]{:S(2)}, u32[]{:S(2)}) collective-permute-start(bf16[2,128,256]{2,1,0:T(8,128)(2,1)S(1)} %get-tuple-element.28), channel_id=1, source_target_pairs={{0,192},{1,193},{2,194},{3,195},{4,196},{5,197},{6,198},{7,199},{8... | collective-permute-start | bytes 393224 | tf_op jit(solution)/shard_map/ppermute | solution.py:31
  17.3 5.6 %collective-permute-start.3 = (bf16[2,128,256]{2,1,0:T(8,128)(2,1)S(1)}, bf16[2,128,256]{2,1,0:T(8,128)(2,1)S(1)}, u32[]{:S(2)}, u32[]{:S(2)}) collective-permute-start(bf16[2,128,256]{2,1,0:T(8,128)(2,1)S(1)} %get-tuple-element.29), channel_id=1, source_target_pairs={{0,128},{1,129},{2,130},{3,131},{4,132},{5,133},{6,134},{7,135},{8... | collective-permute-start | bytes 393224 | tf_op jit(solution)/shard_map/ppermute | solution.py:31
  23.0 15.3 %collective-permute-start.4 = (bf16[2,128,256]{2,1,0:T(8,128)(2,1)S(1)}, bf16[2,128,256]{2,1,0:T(8,128)(2,1)S(1)}, u32[]{:S(2)}, u32[]{:S(2)}) collective-permute-start(bf16[2,128,256]{2,1,0:T(8,128)(2,1)S(1)} %add_add_fusion.1), channel_id=1, source_target_pairs={{0,16},{1,17},{2,18},{3,19},{4,20},{5,21},{6,22},{7,23},{8,24},{9,... | collective-permute-start | bytes 393224 | tf_op jit(solution)/shard_map/ppermute | solution.py:31
  26.0 12.5 %collective-permute-start.5 = (bf16[2,128,256]{2,1,0:T(8,128)(2,1)S(1)}, bf16[2,128,256]{2,1,0:T(8,128)(2,1)S(1)}, u32[]{:S(2)}, u32[]{:S(2)}) collective-permute-start(bf16[2,128,256]{2,1,0:T(8,128)(2,1)S(1)} %add_add_fusion.1), channel_id=1, source_target_pairs={{0,48},{1,49},{2,50},{3,51},{4,52},{5,53},{6,54},{7,55},{8,56},{9,... | collective-permute-start | bytes 393224 | tf_op jit(solution)/shard_map/ppermute | solution.py:31
  29.1 12.5 %collective-permute-start.6 = (bf16[2,128,256]{2,1,0:T(8,128)(2,1)S(1)}, bf16[2,128,256]{2,1,0:T(8,128)(2,1)S(1)}, u32[]{:S(2)}, u32[]{:S(2)}) collective-permute-start(bf16[2,128,256]{2,1,0:T(8,128)(2,1)S(1)} %add_add_fusion.1), channel_id=1, source_target_pairs={{0,32},{1,33},{2,34},{3,35},{4,36},{5,37},{6,38},{7,39},{8,40},{9,... | collective-permute-start | bytes 393224 | tf_op jit(solution)/shard_map/ppermute | solution.py:31
  33.6 2.2 %copy-start = (bf16[512,4096]{1,0:T(8,128)(2,1)S(1)}, bf16[512,4096]{1,0:T(8,128)(2,1)}, u32[]{:S(2)}) copy-start(bf16[512,4096]{1,0:T(8,128)(2,1)} %refs_0_.1) | copy-start | bytes 12582916
  41.6 5.9 %collective-permute-start.8 = (bf16[2,128,256]{2,1,0:T(8,128)(2,1)S(1)}, bf16[2,128,256]{2,1,0:T(8,128)(2,1)S(1)}, u32[]{:S(2)}, u32[]{:S(2)}) collective-permute-start(bf16[2,128,256]{2,1,0:T(8,128)(2,1)S(1)} %add_add_fusion), channel_id=1, source_target_pairs={{0,1},{1,0},{2,3},{3,2},{4,5},{5,4},{6,7},{7,6},{8,9},{9,8},{10,11... | collective-permute-start | bytes 393224 | tf_op jit(solution)/shard_map/ppermute | solution.py:31
  47.6 7.6 %collective-permute-start.10 = (bf16[2,2,128,256]{3,2,1,0:T(8,128)(2,1)S(1)}, bf16[2,2,128,256]{3,2,1,0:T(8,128)(2,1)S(1)}, u32[]{:S(2)}, u32[]{:S(2)}) collective-permute-start(bf16[2,2,128,256]{3,2,1,0:T(8,128)(2,1)S(1)} %pad_maximum_fusion.refs_0_), channel_id=1, source_target_pairs={{0,4},{1,5},{2,6},{3,7},{4,0},{5,1},{6,2},{7,3},{8,136},{9,137},{1... | collective-permute-start | bytes 786440 | tf_op jit(solution)/shard_map/ppermute | solution.py:31
  48.3 7.7 %collective-permute-start.11 = (bf16[2,2,128,256]{3,2,1,0:T(8,128)(2,1)S(1)}, bf16[2,2,128,256]{3,2,1,0:T(8,128)(2,1)S(1)}, u32[]{:S(2)}, u32[]{:S(2)}) collective-permute-start(bf16[2,2,128,256]{3,2,1,0:T(8,128)(2,1)S(1)} %pad_maximum_fusion.refs_0_), channel_id=1, source_target_pairs={{0,6},{1,7},{2,0},{3,1},{4,2},{5,3},{6,4},{7,5},{8,200},{9,201},{1... | collective-permute-start | bytes 786440 | tf_op jit(solution)/shard_map/ppermute | solution.py:31
  50.3 7.2 %collective-permute-start.9 = (bf16[2,2,128,256]{3,2,1,0:T(8,128)(2,1)S(1)}, bf16[2,2,128,256]{3,2,1,0:T(8,128)(2,1)S(1)}, u32[]{:S(2)}, u32[]{:S(2)}) collective-permute-start(bf16[2,2,128,256]{3,2,1,0:T(8,128)(2,1)S(1)} %pad_maximum_fusion.refs_0_), channel_id=1, source_target_pairs={{0,2},{1,3},{2,4},{3,5},{4,6},{5,7},{6,0},{7,1},{8,72},{9,73},{10,... | collective-permute-start | bytes 786440 | tf_op jit(solution)/shard_map/ppermute | solution.py:31
  50.3 20.1 %collective-permute-start.15 = (bf16[8,512,128]{2,1,0:T(8,128)(2,1)S(1)}, bf16[8,512,128]{2,1,0:T(8,128)(2,1)S(1)}, u32[]{:S(2)}, u32[]{:S(2)}) collective-permute-start(bf16[8,512,128]{2,1,0:T(8,128)(2,1)S(1)} %all-to-all-done.refs_0_), channel_id=1, source_target_pairs={{0,8},{1,9},{2,10},{3,11},{4,12},{5,13},{6,14},{7,15},{8,0},{9,1},... | collective-permute-start | bytes 3145736 | tf_op jit(solution)/shard_map/ppermute | solution.py:31
  58.1 9.6 %collective-permute-start.16 = (bf16[4,2,128,256]{3,2,1,0:T(8,128)(2,1)S(1)}, bf16[4,2,128,256]{3,2,1,0:T(8,128)(2,1)S(1)}, u32[]{:S(2)}, u32[]{:S(2)}) collective-permute-start(bf16[4,2,128,256]{3,2,1,0:T(8,128)(2,1)S(1)} %get-tuple-element.40.refs_4_), channel_id=1, source_target_pairs={{0,64},{1,65},{2,66},{3,67},{4,68},{5,69},{6,70},{7,71},{8,10},{9,... | collective-permute-start | bytes 1572872 | tf_op jit(solution)/shard_map/ppermute | solution.py:31
  59.2 9.6 %collective-permute-start.13 = (bf16[4,2,128,256]{3,2,1,0:T(8,128)(2,1)S(1)}, bf16[4,2,128,256]{3,2,1,0:T(8,128)(2,1)S(1)}, u32[]{:S(2)}, u32[]{:S(2)}) collective-permute-start(bf16[4,2,128,256]{3,2,1,0:T(8,128)(2,1)S(1)} %get-tuple-element.38.refs_2_), channel_id=1, source_target_pairs={{0,192},{1,193},{2,194},{3,195},{4,196},{5,197},{6,198},{7,199},{8... | collective-permute-start | bytes 1572872 | tf_op jit(solution)/shard_map/ppermute | solution.py:31
  60.9 12.3 %collective-permute-start.18 = (bf16[4,2,128,256]{3,2,1,0:T(8,128)(2,1)S(1)}, bf16[4,2,128,256]{3,2,1,0:T(8,128)(2,1)S(1)}, u32[]{:S(2)}, u32[]{:S(2)}) collective-permute-start(bf16[4,2,128,256]{3,2,1,0:T(8,128)(2,1)S(1)} %get-tuple-element.40.refs_4_), channel_id=1, source_target_pairs={{0,192},{1,193},{2,194},{3,195},{4,196},{5,197},{6,198},{7,199},{8... | collective-permute-start | bytes 1572872 | tf_op jit(solution)/shard_map/ppermute | solution.py:31
  67.7 9.2 %collective-permute-start.17 = (bf16[4,2,128,256]{3,2,1,0:T(8,128)(2,1)S(1)}, bf16[4,2,128,256]{3,2,1,0:T(8,128)(2,1)S(1)}, u32[]{:S(2)}, u32[]{:S(2)}) collective-permute-start(bf16[4,2,128,256]{3,2,1,0:T(8,128)(2,1)S(1)} %collective-permute-done.16.refs_5_), channel_id=1, source_target_pairs={{0,64},{1,65},{2,66},{3,67},{4,68},{5,69},{6,70},{7,71},{8,10},{9,... | collective-permute-start | bytes 1572872 | tf_op jit(solution)/shard_map/ppermute | solution.py:31
  67.7 15.2 %collective-permute-start.12 = (bf16[4,2,128,256]{3,2,1,0:T(8,128)(2,1)S(1)}, bf16[4,2,128,256]{3,2,1,0:T(8,128)(2,1)S(1)}, u32[]{:S(2)}, u32[]{:S(2)}) collective-permute-start(bf16[4,2,128,256]{3,2,1,0:T(8,128)(2,1)S(1)} %get-tuple-element.38.refs_2_), channel_id=1, source_target_pairs={{0,64},{1,65},{2,66},{3,67},{4,68},{5,69},{6,70},{7,71},{8,10},{9,... | collective-permute-start | bytes 1572872 | tf_op jit(solution)/shard_map/ppermute | solution.py:31
  68.8 14.1 %collective-permute-start.14 = (bf16[4,2,128,256]{3,2,1,0:T(8,128)(2,1)S(1)}, bf16[4,2,128,256]{3,2,1,0:T(8,128)(2,1)S(1)}, u32[]{:S(2)}, u32[]{:S(2)}) collective-permute-start(bf16[4,2,128,256]{3,2,1,0:T(8,128)(2,1)S(1)} %collective-permute-done.13.refs_5_), channel_id=1, source_target_pairs={{0,192},{1,193},{2,194},{3,195},{4,196},{5,197},{6,198},{7,199},{8... | collective-permute-start | bytes 1572872 | tf_op jit(solution)/shard_map/ppermute | solution.py:31
  86.3 9.5 %collective-permute-start.19 = (bf16[512,1024]{1,0:T(8,128)(2,1)S(1)}, bf16[512,1024]{1,0:T(8,128)(2,1)S(1)}, u32[]{:S(2)}, u32[]{:S(2)}) collective-permute-start(bf16[512,1024]{1,0:T(8,128)(2,1)S(1)} %apply_high.3), channel_id=1, source_target_pairs={{0,8},{1,9},{2,10},{3,11},{4,12},{5,13},{6,14},{7,15},{8,0},{9,1},... | collective-permute-start | bytes 3145736 | tf_op jit(solution)/shard_map/ppermute | solution.py:31

commit v3 on v2

--- a/solution.py
+++ b/solution.py
@@ -36,11 +36,11 @@
 
 
 def to_y(value, d):
-    return send(value, lambda y, zh, c, x, zl: (y + d, zh, c, x, zl))
+    return send(value, lambda y, zh, c, x, zl: (y ^ d, zh, c, x, zl))
 
 
 def to_zh(value, d):
-    return send(value, lambda y, zh, c, x, zl: (y, zh + d, c, x, zl))
+    return send(value, lambda y, zh, c, x, zl: (y, zh ^ d, c, x, zl))
 
 
 def to_zl(value):
@@ -48,7 +48,7 @@
 
 
 def first_axis(value, d):
-    return send(value, lambda y, zh, c, x, zl: (y + d * c, zh, c, x + d * (1 - c), zl))
+    return send(value, lambda y, zh, c, x, zl: (y ^ (d * c), zh, c, x ^ (d * (1 - c)), zl))
 
 
 def second_axis(value, d):
@@ -103,6 +103,7 @@
         in_specs=[pl.BlockSpec(memory_space=pltpu.SMEM), vmem],
         out_specs=[vmem] * 2,
         compiler_params=pltpu.CompilerParams(vmem_limit_bytes=16 * 1024 * 1024),
+        cost_estimate=pl.CostEstimate(flops=2_000_000_000, bytes_accessed=2_000_000, transcendentals=0),
         name="tables",
     )(place, index)
 
@@ -129,7 +130,7 @@
     turned = jnp.concatenate(picked, axis=0).T.astype(jnp.bfloat16)
     rows = lax.broadcasted_iota(jnp.int32, (BLOCK, BLOCK), 0)
     for d in range(4):
-        b = half * 4 + lax.rem(y + d, 4)
+        b = half * 4 + (y ^ d)
         four = slot_ref[pl.ds(b * 4, 4), :]
         row = jnp.concatenate([four[i : i + 1, :] for i in range(4)], axis=1)
         one_hot = (rows == row).astype(jnp.float32).astype(jnp.bfloat16)
@@ -148,12 +149,13 @@
         out_specs=[vmem] * 4,
         scratch_shapes=[pltpu.VMEM(other.shape, other.dtype), pltpu.SemaphoreType.DMA],
         compiler_params=pltpu.CompilerParams(vmem_limit_bytes=16 * 1024 * 1024),
+        cost_estimate=pl.CostEstimate(flops=2_500_000_000, bytes_accessed=4_000_000, transcendentals=0),
         name="pick",
     )(place, slot, where, mine, other)
 
 
 def join_kernel(place, *refs):
-    pieces, messages = refs[:4], refs[4:6]
+    pieces, messages = (refs[0], refs[3], refs[1], refs[2]), refs[4:6]
     core = place[2]
     for c in range(2):
 
@@ -178,6 +180,7 @@
         in_specs=[pl.BlockSpec(memory_space=pltpu.SMEM)] + [vmem] * 4,
         out_specs=[vmem] * 2,
         compiler_params=pltpu.CompilerParams(vmem_limit_bytes=16 * 1024 * 1024),
+        cost_estimate=pl.CostEstimate(flops=0, bytes_accessed=2_000_000, transcendentals=0),
         name="join",
     )(place, *pieces)
 
@@ -205,96 +208,157 @@
         out_specs=[pl.BlockSpec(memory_space=pltpu.VMEM)] * 2,
         scratch_shapes=[pltpu.SemaphoreType.DMA((2, 8))],
         compiler_params=pltpu.CompilerParams(vmem_limit_bytes=16 * 1024 * 1024),
+        cost_estimate=pl.CostEstimate(flops=0, bytes_accessed=8_000_000, transcendentals=0),
         name="pack",
     )(place, mine, theirs)
 
 
-def apply_kernel(half, sides, place, *refs):
-    number = len(sides)
-    row_refs, refs = refs[:number], refs[number:]
-    pot_refs, refs = refs[:number], refs[number:]
-    messages, refs = refs[:4], refs[4:]
-    if half == 1:
-        before, refs = refs[0], refs[1:]
-    outs, (rows, weighted) = refs[:number], refs[number:]
-    each = row_refs[0].shape[1]
+def low_block(core, y, e):
+    return jnp.where(core == 0, ((y - e) & 3) * 2, (y ^ (e // 2)) * 2 + e % 2)
+
+
+def high_block(core, y, e):
+    return jnp.where(core == 0, ((y - e) & 3) * 2 + 1, (y ^ (2 + e // 2)) * 2 + e % 2)
+
+
+def flat(message):
+    return message[...].reshape(1024, HALF)
+
+
+def square(message, k):
+    return message[k].reshape(HALF, HALF)
+
+
+def weigh(pots, block, density):
+    each = density.shape[0] // len(pots)
+    parts = [
+        pot[block].astype(jnp.float32) * density[s * each : (s + 1) * each] for s, pot in enumerate(pots)
+    ]
+    return jnp.concatenate(parts, axis=0).astype(jnp.bfloat16)
+
+
+def times(left, right):
+    return jnp.dot(left, right, preferred_element_type=jnp.float32)
+
+
+def spread(weighted, parts):
+    return lax.dot_general(
+        weighted, jnp.concatenate(parts, axis=1), (((1,), (1,)), ((), ())), preferred_element_type=jnp.float32
+    )
+
+
+def column_lanes(n):
+    return slice(n * HALF, (n + 1) * HALF)
+
+
+def whole_chunks(rows, pots, chunks, scratch):
+    for k, (message, block) in enumerate(chunks):
+        scratch[:, column_lanes(k)] = weigh(pots, block, times(rows[...], flat(message)))
+    for n in range(4):
+        yield n, spread(scratch[:, : len(chunks) * HALF], [square(message, n) for message, _ in chunks])
+
+
+def early_kernel(
+    place, mine, theirs, pot_mine, pot_theirs, low0, low1, high0, high3, rows, partial, out, scratch
+):
     x, y, core, zl = place[0], place[1], place[2], place[3]
-
-    def pot_block(k):
-        first = lax.rem(y - k + 4, 4) * 2 + half
-        second = lax.rem(y - (half * 2 + k // 2) + 4, 4) * 2 + k % 2
-        return jnp.where(core == 0, first, second)
-
+    each = mine.shape[1]
+    pots = (pot_mine, pot_theirs)
     for k in range(8):
-        block = lax.rem(x - k // 2 + 4, 4) * 2 + (zl ^ (k % 2))
-        for s in range(number):
-            rows[s * each : (s + 1) * each, k * 128 : (k + 1) * 128] = row_refs[s][block]
-
-    def work(c):
+        block = jnp.where(core == 0, x ^ (k // 2), (x - k // 2) & 3) * 2 + (zl ^ (k % 2))
+        lanes = slice(k * 128, (k + 1) * 128)
+        rows[:each, lanes] = mine[block]
+        rows[each:, lanes] = theirs[block]
+
+    @pl.when(core == 0)
+    def _():
+        chunks = [(low0, low_block(core, y, 0)), (low1, low_block(core, y, 1))]
+        chunks += [(high0, high_block(core, y, 0)), (high3, high_block(core, y, 3))]
+        for n, total in whole_chunks(rows, pots, chunks, scratch):
+            out[:, column_lanes(n)] = total
+
+    @pl.when(core == 1)
+    def _():
         for k in range(4):
-            if c == 0:
-                value = messages[k][...].reshape(1024, HALF)
-            else:
-                value = jnp.concatenate([messages[e][k].reshape(HALF, HALF) for e in range(4)], axis=0)
-            density = jnp.dot(rows[...], value, preferred_element_type=jnp.float32)
-            for s in range(number):
-                part = slice(s * each, (s + 1) * each)
-                pot = pot_refs[s][pot_block(k)].astype(jnp.float32)
-                weighted[part, k * HALF : (k + 1) * HALF] = (pot * density[part]).astype(jnp.bfloat16)
+            first = jnp.concatenate([square(low0, k), square(low1, k)], axis=0)
+            out[:, column_lanes(k)] = times(rows[:, : 2 * HALF], first)
+        for k in range(4):
+            partial[:, column_lanes(k)] = times(rows[:, column_lanes(0)], square(high0, k)) + times(
+                rows[:, column_lanes(3)], square(high3, k)
+            )
+
+
+def middle_kernel(place, rows, pot_mine, pot_theirs, before, low0, low1, low2, low3, out, scratch):
+    y, core = place[1], place[2]
+    pots = (pot_mine, pot_theirs)
+    lows = (low0, low1, low2, low3)
+
+    @pl.when(core == 0)
+    def _():
+        chunks = [(low2, low_block(core, y, 2)), (low3, low_block(core, y, 3))]
+        for n, total in whole_chunks(rows, pots, chunks, scratch):
+            out[:, column_lanes(n)] = before[:, column_lanes(n)] + total
+
+    @pl.when(core == 1)
+    def _():
+        for k in range(4):
+            rest = jnp.concatenate([square(low2, k), square(low3, k)], axis=0)
+            density = before[:, column_lanes(k)] + times(rows[:, 2 * HALF :], rest)
+            scratch[:, column_lanes(k)] = weigh(pots, low_block(core, y, k), density)
         for n in range(4):
-            lanes = slice(n * HALF, (n + 1) * HALF)
-            if c == 0:
-                parts = [messages[e][n].reshape(HALF, HALF) for e in range(4)]
-            else:
-                parts = [messages[n][k].reshape(HALF, HALF) for k in range(4)]
-            total = lax.dot_general(
-                weighted[...],
-                jnp.concatenate(parts, axis=1),
-                (((1,), (1,)), ((), ())),
-                preferred_element_type=jnp.float32,
-            )
-            if half == 0:
-                for s in range(number):
-                    outs[s][:, lanes] = total[s * each : (s + 1) * each]
-            else:
-                outs[0][:, lanes] = (before[:, lanes] + total).astype(outs[0].dtype)
-
-    for c in range(2):
-
-        @pl.when(core == c)
-        def _():
-            work(c)
-
-
-def apply(half, place, rows, pots, messages, before=None, dtype=jnp.float32):
+            out[:, column_lanes(n)] = spread(scratch[...], [square(lows[n], k) for k in range(4)])
+
+
+def late_kernel(side, place, rows, pot, before, partial, high0, high1, high2, high3, out, scratch):
+    y, core = place[1], place[2]
+    each = out.shape[0]
+    part = slice(side * each, (side + 1) * each)
+    highs = (high0, high1, high2, high3)
+
+    @pl.when(core == 0)
+    def _():
+        chunks = [(high1, high_block(core, y, 1)), (high2, high_block(core, y, 2))]
+        for n, total in whole_chunks(rows.at[part], (pot,), chunks, scratch):
+            out[:, column_lanes(n)] = (before[part, column_lanes(n)] + total).astype(out.dtype)
+
+    @pl.when(core == 1)
+    def _():
+        for k in range(4):
+            rest = jnp.concatenate([square(high1, k), square(high2, k)], axis=0)
+            density = partial[part, column_lanes(k)] + times(rows[part, HALF : 3 * HALF], rest)
+            scratch[:, column_lanes(k)] = weigh((pot,), high_block(core, y, k), density)
+        for n in range(4):
+            total = spread(scratch[...], [square(highs[n], k) for k in range(4)])
+            out[:, column_lanes(n)] = (before[part, column_lanes(n)] + total).astype(out.dtype)
+
+
+def call(kernel, name, outs, work, *operands, aliases=None):
     vmem = pl.BlockSpec(memory_space=pltpu.VMEM)
-    number, each = len(rows), pots[0].shape[1]
-    extra = [before] if half == 1 else []
-    out = jax.ShapeDtypeStruct((each, 1024), dtype)
-    return pl.pallas_call(
-        functools.partial(apply_kernel, half, tuple(range(number))),
-        out_shape=[out] * number,
-        in_specs=[pl.BlockSpec(memory_space=pltpu.SMEM)]
-        + [vmem] * (2 * number + 4 + len(extra)),
-        out_specs=[vmem] * number,
-        scratch_shapes=[
-            pltpu.VMEM((number * each, 1024), jnp.bfloat16),
-            pltpu.VMEM((number * each, 1024), jnp.bfloat16),
-        ],
+    lines = outs[-1].shape[0]
+    return pl.pallas_call(
+        kernel,
+        out_shape=outs,
+        in_specs=[pl.BlockSpec(memory_space=pltpu.SMEM)] + [vmem] * (len(operands) - 1),
+        out_specs=[vmem] * len(outs),
+        scratch_shapes=[pltpu.VMEM((lines, 1024), jnp.bfloat16)],
+        input_output_aliases=aliases or {},
         compiler_params=pltpu.CompilerParams(vmem_limit_bytes=16 * 1024 * 1024),
         cost_estimate=pl.CostEstimate(
-            flops=number * each * 4 * 1024 * 1024, bytes_accessed=number * 4 * 1024 * 1024, transcendentals=0
+            flops=work * lines * 1024 * 1024, bytes_accessed=4 * 1024 * 1024, transcendentals=0
         ),
-        name="apply_high" if half else "apply_low",
-    )(place, *rows, *pots, *messages, *extra)
+        name=name,
+    )(*operands)
 
 
 def total_kernel(place, mine, theirs, out):
-    x, zl = place[0], place[3]
+    x, core, zl = place[0], place[2], place[3]
     for k in range(8):
-        block = lax.rem(x - k // 2 + 4, 4) * 2 + (zl ^ (k % 2))
-        lanes = slice(k * 128, (k + 1) * 128)
-        out[block] = (-(mine[:, lanes] + theirs[:, lanes].astype(jnp.float32))).astype(jnp.bfloat16)
+        first, second = x ^ (k // 2), (x - k // 2) & 3
+        here = jnp.where(core == 0, first, second) * 256 + (zl ^ (k % 2)) * 128
+        there = jnp.where(core == 0, second, first) * 256 + (zl ^ (k % 2)) * 128
+        value = mine[:, pl.ds(pl.multiple_of(here, 128), 128)]
+        value = value + theirs[:, pl.ds(pl.multiple_of(there, 128), 128)].astype(jnp.float32)
+        out[k] = (-value).astype(jnp.bfloat16)
 
 
 def total(place, mine, theirs):
@@ -322,25 +386,40 @@
     rows_here = lax.all_to_all(orbitals.reshape(8, -1, 128), "orb", split_axis=0, concat_axis=0, tiled=True)
     slot, where = tables(pick_place, point_index.reshape(-1, 128))
     blocks = pick(pick_place, slot, where, orbitals, other)
-    here = blocks[0] + to_y(blocks[1], 1) + to_y(blocks[3], 3) + to_y(blocks[2], 2)
+    here = to_y(blocks[2], 2) + to_y(blocks[1], 1) + to_y(blocks[3], 3) + blocks[0]
     here, rows_here = lax.optimization_barrier((here, rows_here))
-    around = [to_zh(here, 1), to_zh(here, 3), to_zh(here, 2)]
+    around = [to_zh(here, 2), to_zh(here, 1), to_zh(here, 3)]
     pots = pack(place, potentials, other_pot)
     around, pots = lax.optimization_barrier((around, pots))
     here = here + around[0] + around[1] + around[2]
     beside = to_zl(here)
     pair = jnp.stack([here, beside])
-    pieces = [pair] + [first_axis(pair, d) for d in (1, 2, 3)]
+    pair, rows_here = lax.optimization_barrier((pair, rows_here))
     rows = [rows_here, to_core(rows_here)]
+    pieces = [pair] + [first_axis(pair, d) for d in (2, 3, 1)]
     low, high = join(place, pieces)
     low_up, low_down = second_axis(low, 1), second_axis(low, 3)
     high_up, high_down = second_axis(high, 1), second_axis(high, 3)
     lows = [low, low_up, second_axis(low_up, 1), low_down]
     highs = [high, high_up, second_axis(high_down, 3), high_down]
-    parts = apply(0, place, rows, pots, lows)
-    (sent,) = apply(1, place, rows[1:], pots[1:], highs, parts[1], jnp.bfloat16)
+    each = potentials.shape[0]
+    sums = jax.ShapeDtypeStruct((2 * each, 1024), jnp.float32)
+    lines = jax.ShapeDtypeStruct((2 * each, 1024), jnp.bfloat16)
+    low0, low1, low2, low3 = lows
+    high0, high1, high2, high3 = highs
+    lined, partial, early = call(
+        early_kernel, "early", [lines, sums, sums], 3, place, *rows, *pots, low0, low1, high0, high3
+    )
+    (acc,) = call(
+        middle_kernel, "middle", [sums], 3, place, lined, *pots, early, low0, low1, low2, low3, aliases={4: 0}
+    )
+    halves = []
+    for side, dtype in ((1, jnp.bfloat16), (0, jnp.float32)):
+        out = jax.ShapeDtypeStruct((each, 1024), dtype)
+        kernel = functools.partial(late_kernel, side)
+        halves += call(kernel, "late", [out], 3, place, lined, pots[side], acc, partial, *highs)
+    sent, kept = halves
     theirs = to_core(sent)
-    (kept,) = apply(1, place, rows[:1], pots[:1], highs, parts[0])
     result = total(place, kept, theirs)
     return lax.all_to_all(result, "orb", split_axis=0, concat_axis=0, tiled=True).reshape(-1, 128)
 

time: 118 us -> 112 us (0.949)
  starting transfers between devices: 44.8 us -> 30.4 us
  waiting for transfers between devices: 27.8 us -> 36.8 us
  blocking collectives: 19.8 us -> 18.6 us
    ppermute x20, starting transfers between devices: 41.2 us -> 26.8 us  [send(): return lax.ppermute(value, AXES, moves(target))]
    ppermute x20, waiting for transfers between devices: 27.8 us -> 36.8 us  [send(): return lax.ppermute(value, AXES, moves(target))]
    pallas_call x3 -> x4, Pallas kernels: 12.3 us -> 12.4 us  [call(): pl.pallas_call(kernel, out_shape=outs, in_specs=[pl.BlockSpec(memory_spac...]
  transfers between devices with their start and end apart: 21 -> 21, of which waited for: 13 -> 12; matrix products, arithmetic and copies ran while one was open for 0% -> 0% of each run, Pallas kernels for 15% -> 16%
where the time goes in v3:
time: 112 us
  waiting for transfers between devices  36.8 us (33%)
  starting transfers between devices  30.4 us (27%)
  Pallas kernels  21.7 us (19%)
  blocking collectives  18.6 us (17%)
  local copies, waits for them, and re-layouts  3.88 us (3%)
    ppermute x20, waiting for transfers between devices, send(): return lax.ppermute(value, AXES, moves(target))  36.8 us
    ppermute x20, starting transfers between devices, send(): return lax.ppermute(value, AXES, moves(target))  26.8 us
    all_to_all x1, blocking collectives, shards(): lax.all_to_all(result, 'orb', split_axis=0, concat_axis=0, tiled=True)  18.6 us
    pallas_call x4, Pallas kernels, call(): pl.pallas_call(kernel, out_shape=outs, in_specs=[pl.BlockSpec(memory_spac...  12.4 us
    unnamed x7, local copies, waits for them, and re-layouts  3.88 us
    all_to_all x1, starting transfers between devices, shards(): lax.all_to_all(orbitals.reshape(8, -1, 128), 'orb', split_axis=0, concat_...  3.64 us
    pallas_call x1, Pallas kernels, pick(): pl.pallas_call(pick_kernel, out_shape=[block] * 4, in_specs=[pl.BlockSpec...  3.01 us
    pallas_call x1, Pallas kernels, pack(): pl.pallas_call(pack_kernel, out_shape=[jax.ShapeDtypeStruct((8, mine.shap...  2.51 us
  transfers between devices with their start and end apart: 21, of which 12 were waited for; matrix products, arithmetic and copies ran while one was open for 0% of the time, Pallas kernels for 16%

profile of v3, /device:TPU:1, one launch (start us, length us, event | category | flops | bytes accessed | tf_op | source)
XLA Modules:
  0.0 111.9 jit_solution(12284790882920041531)
XLA Ops:
  0.0 3.2 %collective-permute-start.7 = (bf16[512,4096]{1,0:T(8,128)(2,1)}, bf16[512,4096]{1,0:T(8,128)(2,1)}, u32[]{:S(2)}, u32[]{:S(2)}) collective-permute-start(bf16[512,4096]{1,0:T(8,128)(2,1)} %refs_0_.1), channel_id=1, source_target_pairs={{0,8},{1,9},{2,10},{3,11},{4,12},{5,13},{6,14},{7,15},{8,0},{9,1},... | collective-permute-start | bytes 12582920 | tf_op jit(solution)/shard_map/ppermute | solution.py:31
  3.2 3.6 %all-to-all-start = ((bf16[8,512,128]{2,1,0:T(8,128)(2,1)}), bf16[8,512,128]{2,1,0:T(8,128)(2,1)S(1)}, u32[]{:S(2)}, u32[]{:S(2)}) async-start(bf16[8,512,128]{2,1,0:T(8,128)(2,1)} %bitcast.10), calls=%async_computation | async-start | bytes 2097152 | tf_op jit(solution)/shard_map/all_to_all | solution.py:386
  8.1 2.1 %tables.1 = (s32[32,128]{1,0:T(8,128)S(1)}, f32[512,8]{1,0:T(8,128)S(1)}) custom-call(s32[3]{0:T(128)S(1)} %pad_add_fusion.1.place, s32[32,128]{1,0:T(8,128)S(1)} %bitcast.11), custom_call_target="tpu_custom_call" | custom-call | flops 2000000000 | bytes 2000000 | tf_op jit(solution)/shard_map/tables/pallas_call | solution.py:100
  10.1 1.6 %collective-permute-done.other_hbm = bf16[4096,128]{1,0:T(8,128)(2,1)S(1)} collective-permute-done((bf16[4096,128]{1,0:T(8,128)(2,1)}, bf16[4096,128]{1,0:T(8,128)(2,1)S(1)}, u32[]{:S(2)}, u32[]{:S(2)}) %collective-permute-start) | collective-permute-done | bytes 1048608 | tf_op jit(solution)/shard_map/ppermute | solution.py:31
  11.7 3.0 %pick.1 = (bf16[2,128,256]{2,1,0:T(8,128)(2,1)S(1)}, bf16[2,128,256]{2,1,0:T(8,128)(2,1)S(1)}, bf16[2,128,256]{2,1,0:T(8,128)(2,1)S(1)}, bf16[2,128,256]{2,1,0:T(8,128)(2,1)S(1)}) custom-call(s32[3]{0:T(128)S(1)} %pad_add_fusion.1.place, s32[32,128]{1,0:T(8,128)S(1)} %get-tuple-element.27.slot_ref, f32[512,8]{1,0:T(8,128)S(1)} %get-tuple-element.28.where_ref, ...), custom_call_target="tpu_custom_call" | custom-call | flops 2500000000 | bytes 4000000 | tf_op jit(solution)/shard_map/pick/pallas_call | solution.py:145
  18.1 3.0 %collective-permute-done.1 = bf16[2,128,256]{2,1,0:T(8,128)(2,1)S(1)} collective-permute-done((bf16[2,128,256]{2,1,0:T(8,128)(2,1)S(1)}, bf16[2,128,256]{2,1,0:T(8,128)(2,1)S(1)}, u32[]{:S(2)}, u32[]{:S(2)}) %collective-permute-start.1) | collective-permute-done | bytes 131104 | tf_op jit(solution)/shard_map/ppermute | solution.py:31
  21.1 1.7 %collective-permute-done.2 = bf16[2,128,256]{2,1,0:T(8,128)(2,1)S(1)} collective-permute-done((bf16[2,128,256]{2,1,0:T(8,128)(2,1)S(1)}, bf16[2,128,256]{2,1,0:T(8,128)(2,1)S(1)}, u32[]{:S(2)}, u32[]{:S(2)}) %collective-permute-start.2) | collective-permute-done | bytes 131104 | tf_op jit(solution)/shard_map/ppermute | solution.py:31
  24.4 5.1 %collective-permute-start.4 = (bf16[2,128,256]{2,1,0:T(8,128)(2,1)S(1)}, bf16[2,128,256]{2,1,0:T(8,128)(2,1)S(1)}, u32[]{:S(2)}, u32[]{:S(2)}) collective-permute-start(bf16[2,128,256]{2,1,0:T(8,128)(2,1)S(1)} %add_add_fusion.1), channel_id=1, source_target_pairs={{0,32},{1,33},{2,34},{3,35},{4,36},{5,37},{6,38},{7,39},{8,40},{9,... | collective-permute-start | bytes 393224 | tf_op jit(solution)/shard_map/ppermute | solution.py:31
  30.8 2.2 %copy-done = bf16[512,4096]{1,0:T(8,128)(2,1)S(1)} copy-done((bf16[512,4096]{1,0:T(8,128)(2,1)S(1)}, bf16[512,4096]{1,0:T(8,128)(2,1)}, u32[]{:S(2)}) %copy-start) | copy-done | bytes 4194328
  33.0 2.5 %pack.1 = (bf16[8,512,256]{2,1,0:T(8,128)(2,1)S(1)}, bf16[8,512,256]{2,1,0:T(8,128)(2,1)S(1)}) custom-call(s32[4]{0:T(128)S(1)} %pad_add_fusion.place, bf16[512,4096]{1,0:T(8,128)(2,1)S(1)} %copy-done, bf16[512,4096]{1,0:T(8,128)(2,1)} %collective-permute-done.7.refs_1_), custom_call_target="tpu_custom_call" | custom-call | bytes 8000000 | tf_op jit(solution)/shard_map/pack/pallas_call | solution.py:204
  35.5 7.3 %collective-permute-done.5 = bf16[2,128,256]{2,1,0:T(8,128)(2,1)S(1)} collective-permute-done((bf16[2,128,256]{2,1,0:T(8,128)(2,1)S(1)}, bf16[2,128,256]{2,1,0:T(8,128)(2,1)S(1)}, u32[]{:S(2)}, u32[]{:S(2)}) %collective-permute-start.5) | collective-permute-done | bytes 131104 | tf_op jit(solution)/shard_map/ppermute | solution.py:31
  43.0 4.5 %collective-permute-done.8 = bf16[2,128,256]{2,1,0:T(8,128)(2,1)S(1)} collective-permute-done((bf16[2,128,256]{2,1,0:T(8,128)(2,1)S(1)}, bf16[2,128,256]{2,1,0:T(8,128)(2,1)S(1)}, u32[]{:S(2)}, u32[]{:S(2)}) %collective-permute-start.8) | collective-permute-done | bytes 131104 | tf_op jit(solution)/shard_map/ppermute | solution.py:31
  49.0 3.1 %collective-permute-start.10 = (bf16[2,2,128,256]{3,2,1,0:T(8,128)(2,1)S(1)}, bf16[2,2,128,256]{3,2,1,0:T(8,128)(2,1)S(1)}, u32[]{:S(2)}, u32[]{:S(2)}) collective-permute-start(bf16[2,2,128,256]{3,2,1,0:T(8,128)(2,1)S(1)} %pad_maximum_fusion.refs_0_), channel_id=1, source_target_pairs={{0,4},{1,5},{2,6},{3,7},{4,0},{5,1},{6,2},{7,3},{8,136},{9,137},{1... | collective-permute-start | bytes 786440 | tf_op jit(solution)/shard_map/ppermute | solution.py:31
  52.7 3.5 %collective-permute-done.10.refs_1_ = bf16[2,2,128,256]{3,2,1,0:T(8,128)(2,1)S(1)} collective-permute-done((bf16[2,2,128,256]{3,2,1,0:T(8,128)(2,1)S(1)}, bf16[2,2,128,256]{3,2,1,0:T(8,128)(2,1)S(1)}, u32[]{:S(2)}, u32[]{:S(2)}) %collective-permute-start.10) | collective-permute-done | bytes 262176 | tf_op jit(solution)/shard_map/ppermute | solution.py:31
  56.1 2.8 %collective-permute-done.11.refs_2_ = bf16[2,2,128,256]{3,2,1,0:T(8,128)(2,1)S(1)} collective-permute-done((bf16[2,2,128,256]{3,2,1,0:T(8,128)(2,1)S(1)}, bf16[2,2,128,256]{3,2,1,0:T(8,128)(2,1)S(1)}, u32[]{:S(2)}, u32[]{:S(2)}) %collective-permute-start.11) | collective-permute-done | bytes 262176 | tf_op jit(solution)/shard_map/ppermute | solution.py:31
  63.9 5.8 %collective-permute-done.13.low1 = bf16[4,2,128,256]{3,2,1,0:T(8,128)(2,1)S(1)} collective-permute-done((bf16[4,2,128,256]{3,2,1,0:T(8,128)(2,1)S(1)}, bf16[4,2,128,256]{3,2,1,0:T(8,128)(2,1)S(1)}, u32[]{:S(2)}, u32[]{:S(2)}) %collective-permute-start.13) | collective-permute-done | bytes 524320 | tf_op jit(solution)/shard_map/ppermute | solution.py:31
  70.5 1.8 %collective-permute-start.18 = (bf16[4,2,128,256]{3,2,1,0:T(8,128)(2,1)S(1)}, bf16[4,2,128,256]{3,2,1,0:T(8,128)(2,1)S(1)}, u32[]{:S(2)}, u32[]{:S(2)}) collective-permute-start(bf16[4,2,128,256]{3,2,1,0:T(8,128)(2,1)S(1)} %collective-permute-done.14.high3), channel_id=1, source_target_pairs={{0,192},{1,193},{2,194},{3,195},{4,196},{5,197},{6,198},{7,199},{8... | collective-permute-start | bytes 1572872 | tf_op jit(solution)/shard_map/ppermute | solution.py:31
  72.3 3.5 %early.1 = (bf16[1024,1024]{1,0:T(8,128)(2,1)S(1)}, f32[1024,1024]{1,0:T(8,128)S(1)}, f32[1024,1024]{1,0:T(8,128)S(1)}) custom-call(s32[4]{0:T(128)S(1)} %pad_add_fusion.place, bf16[8,512,128]{2,1,0:T(8,128)(2,1)S(1)} %all-to-all-done.mine, bf16[8,512,128]{2,1,0:T(8,128)(2,1)S(1)} %collective-permute-done.9.theirs, ...), custom_call_target="tpu_custom_call" | custom-call | flops 3221225472 | bytes 4194304 | tf_op jit(solution)/shard_map/early/pallas_call | solution.py:338
  75.8 3.3 %collective-permute-done.15.low2 = bf16[4,2,128,256]{3,2,1,0:T(8,128)(2,1)S(1)} collective-permute-done((bf16[4,2,128,256]{3,2,1,0:T(8,128)(2,1)S(1)}, bf16[4,2,128,256]{3,2,1,0:T(8,128)(2,1)S(1)}, u32[]{:S(2)}, u32[]{:S(2)}) %collective-permute-start.15) | collective-permute-done | bytes 524320 | tf_op jit(solution)/shard_map/ppermute | solution.py:31
  79.1 4.2 %middle.1.before = f32[1024,1024]{1,0:T(8,128)S(1)} custom-call(s32[4]{0:T(128)S(1)} %pad_add_fusion.place, bf16[1024,1024]{1,0:T(8,128)(2,1)S(1)} %get-tuple-element.46.rows, bf16[8,512,256]{2,1,0:T(8,128)(2,1)S(1)} %get-tuple-element.41.pot_mine.pot, bf16[8,512,256]{2,1,0:T(8,128)(2,1)S(1)} %get-tuple-element.42.pot_theirs.pot, ...), custom_call_target="tpu_custom_call", output_to_operand_aliasing={{}: (4, {})} | custom-call | flops 3221225472 | bytes 4194304 | tf_op jit(solution)/shard_map/middle/pallas_call | solution.py:338
  84.8 2.3 %late.3 = bf16[512,1024]{1,0:T(8,128)(2,1)S(1)} custom-call(s32[4]{0:T(128)S(1)} %pad_add_fusion.place, bf16[1024,1024]{1,0:T(8,128)(2,1)S(1)} %get-tuple-element.46.rows, bf16[8,512,256]{2,1,0:T(8,128)(2,1)S(1)} %get-tuple-element.42.pot_theirs.pot, f32[1024,1024]{1,0:T(8,128)S(1)} %middle.1.before, f32[1024,1024]{1,0:T(8,128)S(1)} %get-tuple-element.48.partial, ...), custom_call_target="tpu_custom_call" | custom-call | flops 1610612736 | bytes 4194304 | tf_op jit(solution)/shard_map/late/pallas_call | solution.py:338
  87.1 1.7 %collective-permute-start.19 = (bf16[512,1024]{1,0:T(8,128)(2,1)S(1)}, bf16[512,1024]{1,0:T(8,128)(2,1)S(1)}, u32[]{:S(2)}, u32[]{:S(2)}) collective-permute-start(bf16[512,1024]{1,0:T(8,128)(2,1)S(1)} %late.3), channel_id=1, source_target_pairs={{0,8},{1,9},{2,10},{3,11},{4,12},{5,13},{6,14},{7,15},{8,0},{9,1},... | collective-permute-start | bytes 3145736 | tf_op jit(solution)/shard_map/ppermute | solution.py:31
  88.8 2.3 %late.2.mine = f32[512,1024]{1,0:T(8,128)S(1)} custom-call(s32[4]{0:T(128)S(1)} %pad_add_fusion.place, bf16[1024,1024]{1,0:T(8,128)(2,1)S(1)} %get-tuple-element.46.rows, bf16[8,512,256]{2,1,0:T(8,128)(2,1)S(1)} %get-tuple-element.41.pot_mine.pot, f32[1024,1024]{1,0:T(8,128)S(1)} %middle.1.before, f32[1024,1024]{1,0:T(8,128)S(1)} %get-tuple-element.48.partial, ...), custom_call_target="tpu_custom_call" | custom-call | flops 1610612736 | bytes 4194304 | tf_op jit(solution)/shard_map/late/pallas_call | solution.py:338
  92.3 18.6 %all_to_all.10 = bf16[8,512,128]{2,1,0:T(8,128)(2,1)S(1)} all-to-all(bf16[8,512,128]{2,1,0:T(8,128)(2,1)S(1)} %total.1), channel_id=1, replica_groups=mesh['grid'=32,'orb'=8] {'orb'}, dimensions={0} | all-to-all | bytes 2097152 | tf_op jit(solution)/shard_map/all_to_all | solution.py:424
  (40 shorter events, 18.9 us)
Async XLA Ops:
  0.0 30.8 %collective-permute-start.7 = (bf16[512,4096]{1,0:T(8,128)(2,1)}, bf16[512,4096]{1,0:T(8,128)(2,1)}, u32[]{:S(2)}, u32[]{:S(2)}) collective-permute-start(bf16[512,4096]{1,0:T(8,128)(2,1)} %refs_0_.1), channel_id=1, source_target_pairs={{0,8},{1,9},{2,10},{3,11},{4,12},{5,13},{6,14},{7,15},{8,0},{9,1},... | collective-permute-start | bytes 12582920 | tf_op jit(solution)/shard_map/ppermute | solution.py:31
  3.2 21.1 %all-to-all-start = ((bf16[8,512,128]{2,1,0:T(8,128)(2,1)}), bf16[8,512,128]{2,1,0:T(8,128)(2,1)S(1)}, u32[]{:S(2)}, u32[]{:S(2)}) async-start(bf16[8,512,128]{2,1,0:T(8,128)(2,1)} %bitcast.10), calls=%async_computation | async-start | bytes 2097152 | tf_op jit(solution)/shard_map/all_to_all | solution.py:386
  6.9 4.9 %copy-start.1 = (bf16[4096,128]{1,0:T(8,128)(2,1)S(1)}, bf16[4096,128]{1,0:T(8,128)(2,1)}, u32[]{:S(2)}) copy-start(bf16[4096,128]{1,0:T(8,128)(2,1)} %mine.1) | copy-start | bytes 3145732
  6.9 4.9 %collective-permute-start = (bf16[4096,128]{1,0:T(8,128)(2,1)}, bf16[4096,128]{1,0:T(8,128)(2,1)S(1)}, u32[]{:S(2)}, u32[]{:S(2)}) collective-permute-start(bf16[4096,128]{1,0:T(8,128)(2,1)} %mine.1), channel_id=1, source_target_pairs={{0,8},{1,9},{2,10},{3,11},{4,12},{5,13},{6,14},{7,15},{8,0},{9,1},... | collective-permute-start | bytes 3145736 | tf_op jit(solution)/shard_map/ppermute | solution.py:31
  7.3 0.7 copy-start.2
  14.8 6.3 %collective-permute-start.1 = (bf16[2,128,256]{2,1,0:T(8,128)(2,1)S(1)}, bf16[2,128,256]{2,1,0:T(8,128)(2,1)S(1)}, u32[]{:S(2)}, u32[]{:S(2)}) collective-permute-start(bf16[2,128,256]{2,1,0:T(8,128)(2,1)S(1)} %get-tuple-element.29), channel_id=1, source_target_pairs={{0,128},{1,129},{2,130},{3,131},{4,132},{5,133},{6,134},{7,135},{8... | collective-permute-start | bytes 393224 | tf_op jit(solution)/shard_map/ppermute | solution.py:31
  16.2 6.6 %collective-permute-start.2 = (bf16[2,128,256]{2,1,0:T(8,128)(2,1)S(1)}, bf16[2,128,256]{2,1,0:T(8,128)(2,1)S(1)}, u32[]{:S(2)}, u32[]{:S(2)}) collective-permute-start(bf16[2,128,256]{2,1,0:T(8,128)(2,1)S(1)} %get-tuple-element.30), channel_id=1, source_target_pairs={{0,64},{1,65},{2,66},{3,67},{4,68},{5,69},{6,70},{7,71},{8,72},{9,... | collective-permute-start | bytes 393224 | tf_op jit(solution)/shard_map/ppermute | solution.py:31
  16.6 7.7 %collective-permute-start.3 = (bf16[2,128,256]{2,1,0:T(8,128)(2,1)S(1)}, bf16[2,128,256]{2,1,0:T(8,128)(2,1)S(1)}, u32[]{:S(2)}, u32[]{:S(2)}) collective-permute-start(bf16[2,128,256]{2,1,0:T(8,128)(2,1)S(1)} %get-tuple-element.31), channel_id=1, source_target_pairs={{0,192},{1,193},{2,194},{3,195},{4,196},{5,197},{6,198},{7,199},{8... | collective-permute-start | bytes 393224 | tf_op jit(solution)/shard_map/ppermute | solution.py:31
  24.4 11.1 %collective-permute-start.4 = (bf16[2,128,256]{2,1,0:T(8,128)(2,1)S(1)}, bf16[2,128,256]{2,1,0:T(8,128)(2,1)S(1)}, u32[]{:S(2)}, u32[]{:S(2)}) collective-permute-start(bf16[2,128,256]{2,1,0:T(8,128)(2,1)S(1)} %add_add_fusion.1), channel_id=1, source_target_pairs={{0,32},{1,33},{2,34},{3,35},{4,36},{5,37},{6,38},{7,39},{8,40},{9,... | collective-permute-start | bytes 393224 | tf_op jit(solution)/shard_map/ppermute | solution.py:31
  29.5 13.3 %collective-permute-start.5 = (bf16[2,128,256]{2,1,0:T(8,128)(2,1)S(1)}, bf16[2,128,256]{2,1,0:T(8,128)(2,1)S(1)}, u32[]{:S(2)}, u32[]{:S(2)}) collective-permute-start(bf16[2,128,256]{2,1,0:T(8,128)(2,1)S(1)} %add_add_fusion.1), channel_id=1, source_target_pairs={{0,16},{1,17},{2,18},{3,19},{4,20},{5,21},{6,22},{7,23},{8,24},{9,... | collective-permute-start | bytes 393224 | tf_op jit(solution)/shard_map/ppermute | solution.py:31
  30.7 12.1 %collective-permute-start.6 = (bf16[2,128,256]{2,1,0:T(8,128)(2,1)S(1)}, bf16[2,128,256]{2,1,0:T(8,128)(2,1)S(1)}, u32[]{:S(2)}, u32[]{:S(2)}) collective-permute-start(bf16[2,128,256]{2,1,0:T(8,128)(2,1)S(1)} %add_add_fusion.1), channel_id=1, source_target_pairs={{0,48},{1,49},{2,50},{3,51},{4,52},{5,53},{6,54},{7,55},{8,56},{9,... | collective-permute-start | bytes 393224 | tf_op jit(solution)/shard_map/ppermute | solution.py:31
  30.8 2.2 %copy-start = (bf16[512,4096]{1,0:T(8,128)(2,1)S(1)}, bf16[512,4096]{1,0:T(8,128)(2,1)}, u32[]{:S(2)}) copy-start(bf16[512,4096]{1,0:T(8,128)(2,1)} %refs_0_.1) | copy-start | bytes 12582916
  42.9 4.6 %collective-permute-start.8 = (bf16[2,128,256]{2,1,0:T(8,128)(2,1)S(1)}, bf16[2,128,256]{2,1,0:T(8,128)(2,1)S(1)}, u32[]{:S(2)}, u32[]{:S(2)}) collective-permute-start(bf16[2,128,256]{2,1,0:T(8,128)(2,1)S(1)} %add_add_fusion), channel_id=1, source_target_pairs={{0,1},{1,0},{2,3},{3,2},{4,5},{5,4},{6,7},{7,6},{8,9},{9,8},{10,11... | collective-permute-start | bytes 393224 | tf_op jit(solution)/shard_map/ppermute | solution.py:31
  47.5 24.8 %collective-permute-start.9 = (bf16[8,512,128]{2,1,0:T(8,128)(2,1)S(1)}, bf16[8,512,128]{2,1,0:T(8,128)(2,1)S(1)}, u32[]{:S(2)}, u32[]{:S(2)}) collective-permute-start(bf16[8,512,128]{2,1,0:T(8,128)(2,1)S(1)} %all-to-all-done.mine), channel_id=1, source_target_pairs={{0,8},{1,9},{2,10},{3,11},{4,12},{5,13},{6,14},{7,15},{8,0},{9,1},... | collective-permute-start | bytes 3145736 | tf_op jit(solution)/shard_map/ppermute | solution.py:31
  49.0 7.1 %collective-permute-start.10 = (bf16[2,2,128,256]{3,2,1,0:T(8,128)(2,1)S(1)}, bf16[2,2,128,256]{3,2,1,0:T(8,128)(2,1)S(1)}, u32[]{:S(2)}, u32[]{:S(2)}) collective-permute-start(bf16[2,2,128,256]{3,2,1,0:T(8,128)(2,1)S(1)} %pad_maximum_fusion.refs_0_), channel_id=1, source_target_pairs={{0,4},{1,5},{2,6},{3,7},{4,0},{5,1},{6,2},{7,3},{8,136},{9,137},{1... | collective-permute-start | bytes 786440 | tf_op jit(solution)/shard_map/ppermute | solution.py:31
  52.1 6.9 %collective-permute-start.11 = (bf16[2,2,128,256]{3,2,1,0:T(8,128)(2,1)S(1)}, bf16[2,2,128,256]{3,2,1,0:T(8,128)(2,1)S(1)}, u32[]{:S(2)}, u32[]{:S(2)}) collective-permute-start(bf16[2,2,128,256]{3,2,1,0:T(8,128)(2,1)S(1)} %pad_maximum_fusion.refs_0_), channel_id=1, source_target_pairs={{0,6},{1,7},{2,4},{3,5},{4,2},{5,3},{6,0},{7,1},{8,200},{9,201},{1... | collective-permute-start | bytes 786440 | tf_op jit(solution)/shard_map/ppermute | solution.py:31
  52.6 6.7 %collective-permute-start.12 = (bf16[2,2,128,256]{3,2,1,0:T(8,128)(2,1)S(1)}, bf16[2,2,128,256]{3,2,1,0:T(8,128)(2,1)S(1)}, u32[]{:S(2)}, u32[]{:S(2)}) collective-permute-start(bf16[2,2,128,256]{3,2,1,0:T(8,128)(2,1)S(1)} %pad_maximum_fusion.refs_0_), channel_id=1, source_target_pairs={{0,2},{1,3},{2,0},{3,1},{4,6},{5,7},{6,4},{7,5},{8,72},{9,73},{10,... | collective-permute-start | bytes 786440 | tf_op jit(solution)/shard_map/ppermute | solution.py:31
  60.0 9.6 %collective-permute-start.13 = (bf16[4,2,128,256]{3,2,1,0:T(8,128)(2,1)S(1)}, bf16[4,2,128,256]{3,2,1,0:T(8,128)(2,1)S(1)}, u32[]{:S(2)}, u32[]{:S(2)}) collective-permute-start(bf16[4,2,128,256]{3,2,1,0:T(8,128)(2,1)S(1)} %get-tuple-element.44.low0), channel_id=1, source_target_pairs={{0,64},{1,65},{2,66},{3,67},{4,68},{5,69},{6,70},{7,71},{8,10},{9,... | collective-permute-start | bytes 1572872 | tf_op jit(solution)/shard_map/ppermute | solution.py:31
  61.3 9.2 %collective-permute-start.14 = (bf16[4,2,128,256]{3,2,1,0:T(8,128)(2,1)S(1)}, bf16[4,2,128,256]{3,2,1,0:T(8,128)(2,1)S(1)}, u32[]{:S(2)}, u32[]{:S(2)}) collective-permute-start(bf16[4,2,128,256]{3,2,1,0:T(8,128)(2,1)S(1)} %get-tuple-element.45.high0), channel_id=1, source_target_pairs={{0,192},{1,193},{2,194},{3,195},{4,196},{5,197},{6,198},{7,199},{8... | collective-permute-start | bytes 1572872 | tf_op jit(solution)/shard_map/ppermute | solution.py:31
  62.8 13.1 %collective-permute-start.16 = (bf16[4,2,128,256]{3,2,1,0:T(8,128)(2,1)S(1)}, bf16[4,2,128,256]{3,2,1,0:T(8,128)(2,1)S(1)}, u32[]{:S(2)}, u32[]{:S(2)}) collective-permute-start(bf16[4,2,128,256]{3,2,1,0:T(8,128)(2,1)S(1)} %get-tuple-element.44.low0), channel_id=1, source_target_pairs={{0,192},{1,193},{2,194},{3,195},{4,196},{5,197},{6,198},{7,199},{8... | collective-permute-start | bytes 1572872 | tf_op jit(solution)/shard_map/ppermute | solution.py:31
  69.6 9.5 %collective-permute-start.15 = (bf16[4,2,128,256]{3,2,1,0:T(8,128)(2,1)S(1)}, bf16[4,2,128,256]{3,2,1,0:T(8,128)(2,1)S(1)}, u32[]{:S(2)}, u32[]{:S(2)}) collective-permute-start(bf16[4,2,128,256]{3,2,1,0:T(8,128)(2,1)S(1)} %collective-permute-done.13.low1), channel_id=1, source_target_pairs={{0,64},{1,65},{2,66},{3,67},{4,68},{5,69},{6,70},{7,71},{8,10},{9,... | collective-permute-start | bytes 1572872 | tf_op jit(solution)/shard_map/ppermute | solution.py:31
  69.6 15.2 %collective-permute-start.17 = (bf16[4,2,128,256]{3,2,1,0:T(8,128)(2,1)S(1)}, bf16[4,2,128,256]{3,2,1,0:T(8,128)(2,1)S(1)}, u32[]{:S(2)}, u32[]{:S(2)}) collective-permute-start(bf16[4,2,128,256]{3,2,1,0:T(8,128)(2,1)S(1)} %get-tuple-element.45.high0), channel_id=1, source_target_pairs={{0,64},{1,65},{2,66},{3,67},{4,68},{5,69},{6,70},{7,71},{8,10},{9,... | collective-permute-start | bytes 1572872 | tf_op jit(solution)/shard_map/ppermute | solution.py:31
  70.5 14.3 %collective-permute-start.18 = (bf16[4,2,128,256]{3,2,1,0:T(8,128)(2,1)S(1)}, bf16[4,2,128,256]{3,2,1,0:T(8,128)(2,1)S(1)}, u32[]{:S(2)}, u32[]{:S(2)}) collective-permute-start(bf16[4,2,128,256]{3,2,1,0:T(8,128)(2,1)S(1)} %collective-permute-done.14.high3), channel_id=1, source_target_pairs={{0,192},{1,193},{2,194},{3,195},{4,196},{5,197},{6,198},{7,199},{8... | collective-permute-start | bytes 1572872 | tf_op jit(solution)/shard_map/ppermute | solution.py:31
  87.1 4.0 %collective-permute-start.19 = (bf16[512,1024]{1,0:T(8,128)(2,1)S(1)}, bf16[512,1024]{1,0:T(8,128)(2,1)S(1)}, u32[]{:S(2)}, u32[]{:S(2)}) collective-permute-start(bf16[512,1024]{1,0:T(8,128)(2,1)S(1)} %late.3), channel_id=1, source_target_pairs={{0,8},{1,9},{2,10},{3,11},{4,12},{5,13},{6,14},{7,15},{8,0},{9,1},... | collective-permute-start | bytes 3145736 | tf_op jit(solution)/shard_map/ppermute | solution.py:31

commit v4 on v3

--- a/solution.py
+++ b/solution.py
@@ -11,6 +11,7 @@
 AXES = ("grid", "orb")
 BLOCK = 512
 HALF = 256
+ORDER = ((2, 1), (0, 1), (2, 0), (3, 1), (1, 1), (3, 0), (1, 0), (0, 0))
 
 
 def moves(target):
@@ -51,8 +52,17 @@
     return send(value, lambda y, zh, c, x, zl: (y ^ (d * c), zh, c, x ^ (d * (1 - c)), zl))
 
 
+def to_owner(value, d, dz):
+    return send(value, lambda y, zh, c, x, zl: (y, zh, c, x ^ d, zl ^ dz))
+
+
 def second_axis(value, d):
     return send(value, lambda y, zh, c, x, zl: (y + d * (1 - c), zh, c, x + d * c, zl))
+
+
+def one_hot(places, wanted):
+    one, zero = jnp.ones((), jnp.bfloat16), jnp.zeros((), jnp.bfloat16)
+    return jnp.where(places == wanted.astype(jnp.int16), one, zero)
 
 
 def table_kernel(place, index, slot_ref, where_ref):
@@ -80,17 +90,16 @@
     high = lax.shift_right_logical(local, 6).astype(jnp.float32)
     low = (local & 63).astype(jnp.float32)
     where = jnp.zeros((BLOCK, 8), jnp.float32)
-    rows = lax.broadcasted_iota(jnp.int32, (BLOCK, BLOCK), 0)
+    rows = lax.broadcasted_iota(jnp.int32, (BLOCK, BLOCK), 0).astype(jnp.int16)
     pick_row = lax.broadcasted_iota(jnp.int32, (8, BLOCK), 0)
 
     def line(value, b):
         return jnp.concatenate([value[i : i + 1, :] for i in range(4 * b, 4 * b + 4)], axis=1)
 
     for b in range(8):
-        one_hot = (rows == line(slot, b)).astype(jnp.float32).astype(jnp.bfloat16)
         parts = jnp.where(pick_row == 0, line(high, b), jnp.where(pick_row == 1, line(low, b), 0.0))
         where = where + lax.dot_general(
-            one_hot, parts.astype(jnp.bfloat16), (((1,), (1,)), ((), ())), preferred_element_type=jnp.float32
+            one_hot(rows, line(slot, b)), parts.astype(jnp.bfloat16), (((1,), (1,)), ((), ())), preferred_element_type=jnp.float32
         )
     where_ref[...] = where
 
@@ -117,24 +126,23 @@
     line = (where[:, 0:1] * 64.0 + where[:, 1:2]).astype(jnp.int32)
     picked = []
     wide = 1024
-    lane = lax.broadcasted_iota(jnp.int32, (256, wide), 1)
+    lane = lax.broadcasted_iota(jnp.int32, (256, wide), 1).astype(jnp.int16)
     for s, block in enumerate((mine, other)):
         if s == 1:
             other_copy.wait()
         want = line[s * 256 : (s + 1) * 256, :]
         total = jnp.zeros((256, 128), jnp.float32)
         for k in range(4096 // wide):
-            one_hot = (want - k * wide == lane).astype(jnp.float32).astype(jnp.bfloat16)
-            total = total + jnp.dot(one_hot, block[k * wide : (k + 1) * wide, :], preferred_element_type=jnp.float32)
+            chosen = one_hot(lane, want - k * wide)
+            total = total + jnp.dot(chosen, block[k * wide : (k + 1) * wide, :], preferred_element_type=jnp.float32)
         picked.append(total)
     turned = jnp.concatenate(picked, axis=0).T.astype(jnp.bfloat16)
-    rows = lax.broadcasted_iota(jnp.int32, (BLOCK, BLOCK), 0)
+    rows = lax.broadcasted_iota(jnp.int32, (BLOCK, BLOCK), 0).astype(jnp.int16)
     for d in range(4):
         b = half * 4 + (y ^ d)
         four = slot_ref[pl.ds(b * 4, 4), :]
         row = jnp.concatenate([four[i : i + 1, :] for i in range(4)], axis=1)
-        one_hot = (rows == row).astype(jnp.float32).astype(jnp.bfloat16)
-        values = jnp.dot(turned, one_hot, preferred_element_type=jnp.float32).astype(jnp.bfloat16)
+        values = jnp.dot(turned, one_hot(rows, row), preferred_element_type=jnp.float32).astype(jnp.bfloat16)
         outs[d][0] = values[:, :HALF]
         outs[d][1] = values[:, HALF:]
 
@@ -282,54 +290,49 @@
         for k in range(4):
             first = jnp.concatenate([square(low0, k), square(low1, k)], axis=0)
             out[:, column_lanes(k)] = times(rows[:, : 2 * HALF], first)
-        for k in range(4):
             partial[:, column_lanes(k)] = times(rows[:, column_lanes(0)], square(high0, k)) + times(
                 rows[:, column_lanes(3)], square(high3, k)
             )
 
 
-def middle_kernel(place, rows, pot_mine, pot_theirs, before, low0, low1, low2, low3, out, scratch):
+def middle_kernel(place, rows, pot_mine, pot_theirs, low_before, high_before, low3, high1, partial, out, scratch):
     y, core = place[1], place[2]
-    pots = (pot_mine, pot_theirs)
-    lows = (low0, low1, low2, low3)
 
     @pl.when(core == 0)
     def _():
-        chunks = [(low2, low_block(core, y, 2)), (low3, low_block(core, y, 3))]
-        for n, total in whole_chunks(rows, pots, chunks, scratch):
-            out[:, column_lanes(n)] = before[:, column_lanes(n)] + total
+        chunks = [(low3, low_block(core, y, 3)), (high1, high_block(core, y, 1))]
+        for n, total in whole_chunks(rows, (pot_mine, pot_theirs), chunks, scratch):
+            out[:, column_lanes(n)] = low_before[:, column_lanes(n)] + total
 
     @pl.when(core == 1)
     def _():
         for k in range(4):
-            rest = jnp.concatenate([square(low2, k), square(low3, k)], axis=0)
-            density = before[:, column_lanes(k)] + times(rows[:, 2 * HALF :], rest)
-            scratch[:, column_lanes(k)] = weigh(pots, low_block(core, y, k), density)
-        for n in range(4):
-            out[:, column_lanes(n)] = spread(scratch[...], [square(lows[n], k) for k in range(4)])
-
-
-def late_kernel(side, place, rows, pot, before, partial, high0, high1, high2, high3, out, scratch):
+            lanes = column_lanes(k)
+            out[:, lanes] = low_before[:, lanes] + times(rows[:, column_lanes(3)], square(low3, k))
+            partial[:, lanes] = high_before[:, lanes] + times(rows[:, column_lanes(1)], square(high1, k))
+
+
+def late_kernel(side, place, rows, pot, before, partial, *refs):
+    lows, highs, (out, scratch) = refs[:4], refs[4:8], refs[8:]
     y, core = place[1], place[2]
     each = out.shape[0]
     part = slice(side * each, (side + 1) * each)
-    highs = (high0, high1, high2, high3)
 
     @pl.when(core == 0)
     def _():
-        chunks = [(high1, high_block(core, y, 1)), (high2, high_block(core, y, 2))]
+        chunks = [(lows[2], low_block(core, y, 2)), (highs[2], high_block(core, y, 2))]
         for n, total in whole_chunks(rows.at[part], (pot,), chunks, scratch):
             out[:, column_lanes(n)] = (before[part, column_lanes(n)] + total).astype(out.dtype)
 
     @pl.when(core == 1)
     def _():
-        for k in range(4):
-            rest = jnp.concatenate([square(high1, k), square(high2, k)], axis=0)
-            density = partial[part, column_lanes(k)] + times(rows[part, HALF : 3 * HALF], rest)
-            scratch[:, column_lanes(k)] = weigh((pot,), high_block(core, y, k), density)
+        for i, (known, messages, where) in enumerate(((before, lows, low_block), (partial, highs, high_block))):
+            for k in range(4):
+                density = known[part, column_lanes(k)] + times(rows[part, column_lanes(2)], square(messages[2], k))
+                scratch[:, column_lanes(4 * i + k)] = weigh((pot,), where(core, y, k), density)
         for n in range(4):
-            total = spread(scratch[...], [square(highs[n], k) for k in range(4)])
-            out[:, column_lanes(n)] = (before[part, column_lanes(n)] + total).astype(out.dtype)
+            parts = [square(lows[n], k) for k in range(4)] + [square(highs[n], k) for k in range(4)]
+            out[:, column_lanes(n)] = spread(scratch[...], parts).astype(out.dtype)
 
 
 def call(kernel, name, outs, work, *operands, aliases=None):
@@ -340,7 +343,7 @@
         out_shape=outs,
         in_specs=[pl.BlockSpec(memory_space=pltpu.SMEM)] + [vmem] * (len(operands) - 1),
         out_specs=[vmem] * len(outs),
-        scratch_shapes=[pltpu.VMEM((lines, 1024), jnp.bfloat16)],
+        scratch_shapes=[pltpu.VMEM((lines, 2048), jnp.bfloat16)],
         input_output_aliases=aliases or {},
         compiler_params=pltpu.CompilerParams(vmem_limit_bytes=16 * 1024 * 1024),
         cost_estimate=pl.CostEstimate(
@@ -350,27 +353,53 @@
     )(*operands)
 
 
-def total_kernel(place, mine, theirs, out):
-    x, core, zl = place[0], place[2], place[3]
-    for k in range(8):
-        first, second = x ^ (k // 2), (x - k // 2) & 3
-        here = jnp.where(core == 0, first, second) * 256 + (zl ^ (k % 2)) * 128
-        there = jnp.where(core == 0, second, first) * 256 + (zl ^ (k % 2)) * 128
-        value = mine[:, pl.ds(pl.multiple_of(here, 128), 128)]
-        value = value + theirs[:, pl.ds(pl.multiple_of(there, 128), 128)].astype(jnp.float32)
-        out[k] = (-value).astype(jnp.bfloat16)
+def total_kernel(place, mine, theirs, *outs):
+    x, core = place[0], place[2]
+    for d in range(4):
+        other = (x - (x ^ d)) & 3
+        here, there = jnp.where(core == 0, d, other), jnp.where(core == 0, other, d)
+        for dz in range(2):
+            value = mine[:, pl.ds(pl.multiple_of(here * 256 + dz * 128, 128), 128)]
+            value = value + theirs[:, pl.ds(pl.multiple_of(there * 256 + dz * 128, 128), 128)].astype(jnp.float32)
+            outs[2 * d + dz][...] = (-value).astype(jnp.bfloat16)
 
 
 def total(place, mine, theirs):
     vmem = pl.BlockSpec(memory_space=pltpu.VMEM)
     return pl.pallas_call(
         total_kernel,
-        out_shape=jax.ShapeDtypeStruct((8, mine.shape[0], 128), jnp.bfloat16),
+        out_shape=[jax.ShapeDtypeStruct((mine.shape[0], 128), jnp.bfloat16)] * 8,
         in_specs=[pl.BlockSpec(memory_space=pltpu.SMEM), vmem, vmem],
-        out_specs=vmem,
+        out_specs=[vmem] * 8,
         compiler_params=pltpu.CompilerParams(vmem_limit_bytes=16 * 1024 * 1024),
         name="total",
     )(place, mine, theirs)
+
+
+def put_kernel(place, *refs):
+    blocks, out, sem = refs[:8], refs[8], refs[9]
+    x, zl = place[0], place[3]
+    copies = []
+    for i, (d, dz) in enumerate(ORDER):
+        run = (x ^ d) * 2 + (zl ^ dz)
+        copies.append(pltpu.make_async_copy(blocks[i], out.at[run], sem.at[i]))
+    for copy in copies:
+        copy.start()
+    for copy in copies:
+        copy.wait()
+
+
+def put(place, blocks):
+    vmem = pl.BlockSpec(memory_space=pltpu.VMEM)
+    return pl.pallas_call(
+        put_kernel,
+        out_shape=jax.ShapeDtypeStruct((8,) + blocks[0].shape, jnp.bfloat16),
+        in_specs=[pl.BlockSpec(memory_space=pltpu.SMEM)] + [vmem] * 8,
+        out_specs=pl.BlockSpec(memory_space=pl.ANY),
+        scratch_shapes=[pltpu.SemaphoreType.DMA((8,))],
+        compiler_params=pltpu.CompilerParams(vmem_limit_bytes=16 * 1024 * 1024),
+        name="put",
+    )(place, *blocks)
 
 
 def shards(orbitals, potentials, point_index):
@@ -386,9 +415,9 @@
     rows_here = lax.all_to_all(orbitals.reshape(8, -1, 128), "orb", split_axis=0, concat_axis=0, tiled=True)
     slot, where = tables(pick_place, point_index.reshape(-1, 128))
     blocks = pick(pick_place, slot, where, orbitals, other)
-    here = to_y(blocks[2], 2) + to_y(blocks[1], 1) + to_y(blocks[3], 3) + blocks[0]
+    here = to_y(blocks[2], 2) + to_y(blocks[3], 3) + to_y(blocks[1], 1) + blocks[0]
     here, rows_here = lax.optimization_barrier((here, rows_here))
-    around = [to_zh(here, 2), to_zh(here, 1), to_zh(here, 3)]
+    around = [to_zh(here, 2), to_zh(here, 3), to_zh(here, 1)]
     pots = pack(place, potentials, other_pot)
     around, pots = lax.optimization_barrier((around, pots))
     here = here + around[0] + around[1] + around[2]
@@ -407,21 +436,21 @@
     lines = jax.ShapeDtypeStruct((2 * each, 1024), jnp.bfloat16)
     low0, low1, low2, low3 = lows
     high0, high1, high2, high3 = highs
-    lined, partial, early = call(
-        early_kernel, "early", [lines, sums, sums], 3, place, *rows, *pots, low0, low1, high0, high3
-    )
-    (acc,) = call(
-        middle_kernel, "middle", [sums], 3, place, lined, *pots, early, low0, low1, low2, low3, aliases={4: 0}
+    near = [low0, low1, high0, high3]
+    lined, partial, early = call(early_kernel, "early", [lines, sums, sums], 3, place, *rows, *pots, *near)
+    partial, early = call(
+        middle_kernel, "middle", [sums, sums], 2, place, lined, *pots, early, partial, low3, high1, aliases={5: 0, 4: 1}
     )
     halves = []
     for side, dtype in ((1, jnp.bfloat16), (0, jnp.float32)):
         out = jax.ShapeDtypeStruct((each, 1024), dtype)
         kernel = functools.partial(late_kernel, side)
-        halves += call(kernel, "late", [out], 3, place, lined, pots[side], acc, partial, *highs)
+        halves += call(kernel, "late", [out], 3, place, lined, pots[side], early, partial, *lows, *highs)
     sent, kept = halves
     theirs = to_core(sent)
-    result = total(place, kept, theirs)
-    return lax.all_to_all(result, "orb", split_axis=0, concat_axis=0, tiled=True).reshape(-1, 128)
+    blocks = total(place, kept, theirs)
+    arrived = [to_owner(blocks[2 * d + dz], d, dz) for d, dz in ORDER[:-1]] + [blocks[0]]
+    return put(place, arrived).reshape(-1, 128)
 
 
 def solution(mesh):

time: 112 us -> 109 us (0.973)
  blocking collectives: 18.6 us -> 0 us
  starting transfers between devices: 30.4 us -> 39.2 us
  waiting for transfers between devices: 36.8 us -> 41.8 us
  Pallas kernels: 21.7 us -> 23.8 us
    all_to_all x1 -> x0, blocking collectives: 18.6 us -> none  [shards(): lax.all_to_all(result, 'orb', split_axis=0, concat_axis=0, tiled=True)]
    ppermute x20 -> x27, starting transfers between devices: 26.8 us -> 35.5 us  [send(): return lax.ppermute(value, AXES, moves(target))]
    ppermute x20 -> x27, waiting for transfers between devices: 36.8 us -> 41.8 us  [send(): return lax.ppermute(value, AXES, moves(target))]
    pallas_call x1 -> x2, Pallas kernels: 1.09 us -> 2.62 us  [the longest x1 1.57 us: put(): pl.pallas_call(put_kernel, out_shape=jax.ShapeDtypeStruct((8,) + blocks[0...]
    unnamed x7 -> x6, local copies, waits for them, and re-layouts: 3.88 us -> 2.91 us
  transfers between devices with their start and end apart: 21 -> 28, of which waited for: 12 -> 16; matrix products, arithmetic and copies ran while one was open for 0% -> 0% of each run, Pallas kernels for 16% -> 16%
where the time goes in v4:
time: 109 us; the launch traced here: 108 us
  waiting for transfers between devices  41.8 us (38%)
  starting transfers between devices  39.2 us (36%)
  Pallas kernels  23.8 us (22%)
  local copies, waits for them, and re-layouts  2.91 us (3%)
    ppermute x27, waiting for transfers between devices, send(): return lax.ppermute(value, AXES, moves(target))  41.8 us
    ppermute x27, starting transfers between devices, send(): return lax.ppermute(value, AXES, moves(target))  35.5 us
    pallas_call x4, Pallas kernels, call(): pl.pallas_call(kernel, out_shape=outs, in_specs=[pl.BlockSpec(memory_spac...  13.3 us
    all_to_all x1, starting transfers between devices, shards(): lax.all_to_all(orbitals.reshape(8, -1, 128), 'orb', split_axis=0, concat_...  3.64 us
    unnamed x6, local copies, waits for them, and re-layouts  2.91 us
    pallas_call x1, Pallas kernels, pick(): pl.pallas_call(pick_kernel, out_shape=[block] * 4, in_specs=[pl.BlockSpec...  2.67 us
    pallas_call x1, Pallas kernels, pack(): pl.pallas_call(pack_kernel, out_shape=[jax.ShapeDtypeStruct((8, mine.shap...  2.51 us
  transfers between devices with their start and end apart: 28, of which 16 were waited for; matrix products, arithmetic and copies ran while one was open for 0% of the time, Pallas kernels for 16%

profile of v4, /device:TPU:1, one launch (start us, length us, event | category | flops | bytes accessed | tf_op | source)
XLA Modules:
  0.0 108.3 jit_solution(10592234734154679863)
XLA Ops:
  0.0 3.2 %collective-permute-start.7 = (bf16[512,4096]{1,0:T(8,128)(2,1)}, bf16[512,4096]{1,0:T(8,128)(2,1)}, u32[]{:S(2)}, u32[]{:S(2)}) collective-permute-start(bf16[512,4096]{1,0:T(8,128)(2,1)} %refs_0_.1), channel_id=1, source_target_pairs={{0,8},{1,9},{2,10},{3,11},{4,12},{5,13},{6,14},{7,15},{8,0},{9,1},... | collective-permute-start | bytes 12582920 | tf_op jit(solution)/shard_map/ppermute | solution.py:32
  3.2 3.6 %all-to-all-start = ((bf16[8,512,128]{2,1,0:T(8,128)(2,1)}), bf16[8,512,128]{2,1,0:T(8,128)(2,1)S(1)}, u32[]{:S(2)}, u32[]{:S(2)}) async-start(bf16[8,512,128]{2,1,0:T(8,128)(2,1)} %bitcast.10), calls=%async_computation | async-start | bytes 2097152 | tf_op jit(solution)/shard_map/all_to_all | solution.py:415
  11.7 2.7 %pick.1 = (bf16[2,128,256]{2,1,0:T(8,128)(2,1)S(1)}, bf16[2,128,256]{2,1,0:T(8,128)(2,1)S(1)}, bf16[2,128,256]{2,1,0:T(8,128)(2,1)S(1)}, bf16[2,128,256]{2,1,0:T(8,128)(2,1)S(1)}) custom-call(s32[3]{0:T(128)S(1)} %pad_add_fusion.1.place, s32[32,128]{1,0:T(8,128)S(1)} %get-tuple-element.37.slot_ref, f32[512,8]{1,0:T(8,128)S(1)} %get-tuple-element.38.where_ref, ...), custom_call_target="tpu_custom_call" | custom-call | flops 2500000000 | bytes 4000000 | tf_op jit(solution)/shard_map/pick/pallas_call | solution.py:153
  17.2 3.6 %collective-permute-done.1 = bf16[2,128,256]{2,1,0:T(8,128)(2,1)S(1)} collective-permute-done((bf16[2,128,256]{2,1,0:T(8,128)(2,1)S(1)}, bf16[2,128,256]{2,1,0:T(8,128)(2,1)S(1)}, u32[]{:S(2)}, u32[]{:S(2)}) %collective-permute-start.1) | collective-permute-done | bytes 131104 | tf_op jit(solution)/shard_map/ppermute | solution.py:32
  20.7 3.5 %collective-permute-done.2 = bf16[2,128,256]{2,1,0:T(8,128)(2,1)S(1)} collective-permute-done((bf16[2,128,256]{2,1,0:T(8,128)(2,1)S(1)}, bf16[2,128,256]{2,1,0:T(8,128)(2,1)S(1)}, u32[]{:S(2)}, u32[]{:S(2)}) %collective-permute-start.2) | collective-permute-done | bytes 131104 | tf_op jit(solution)/shard_map/ppermute | solution.py:32
  24.3 4.9 %collective-permute-start.4 = (bf16[2,128,256]{2,1,0:T(8,128)(2,1)S(1)}, bf16[2,128,256]{2,1,0:T(8,128)(2,1)S(1)}, u32[]{:S(2)}, u32[]{:S(2)}) collective-permute-start(bf16[2,128,256]{2,1,0:T(8,128)(2,1)S(1)} %add_add_fusion.1), channel_id=1, source_target_pairs={{0,32},{1,33},{2,34},{3,35},{4,36},{5,37},{6,38},{7,39},{8,40},{9,... | collective-permute-start | bytes 393224 | tf_op jit(solution)/shard_map/ppermute | solution.py:32
  32.6 2.5 %pack.1 = (bf16[8,512,256]{2,1,0:T(8,128)(2,1)S(1)}, bf16[8,512,256]{2,1,0:T(8,128)(2,1)S(1)}) custom-call(s32[4]{0:T(128)S(1)} %pad_add_fusion.place, bf16[512,4096]{1,0:T(8,128)(2,1)S(1)} %copy-done, bf16[512,4096]{1,0:T(8,128)(2,1)} %collective-permute-done.7.refs_1_), custom_call_target="tpu_custom_call" | custom-call | bytes 8000000 | tf_op jit(solution)/shard_map/pack/pallas_call | solution.py:212
  35.2 4.3 %collective-permute-done.5 = bf16[2,128,256]{2,1,0:T(8,128)(2,1)S(1)} collective-permute-done((bf16[2,128,256]{2,1,0:T(8,128)(2,1)S(1)}, bf16[2,128,256]{2,1,0:T(8,128)(2,1)S(1)}, u32[]{:S(2)}, u32[]{:S(2)}) %collective-permute-start.5) | collective-permute-done | bytes 131104 | tf_op jit(solution)/shard_map/ppermute | solution.py:32
  39.5 2.9 %collective-permute-done.6 = bf16[2,128,256]{2,1,0:T(8,128)(2,1)S(1)} collective-permute-done((bf16[2,128,256]{2,1,0:T(8,128)(2,1)S(1)}, bf16[2,128,256]{2,1,0:T(8,128)(2,1)S(1)}, u32[]{:S(2)}, u32[]{:S(2)}) %collective-permute-start.6) | collective-permute-done | bytes 131104 | tf_op jit(solution)/shard_map/ppermute | solution.py:32
  42.6 4.5 %collective-permute-done.8 = bf16[2,128,256]{2,1,0:T(8,128)(2,1)S(1)} collective-permute-done((bf16[2,128,256]{2,1,0:T(8,128)(2,1)S(1)}, bf16[2,128,256]{2,1,0:T(8,128)(2,1)S(1)}, u32[]{:S(2)}, u32[]{:S(2)}) %collective-permute-start.8) | collective-permute-done | bytes 131104 | tf_op jit(solution)/shard_map/ppermute | solution.py:32
  52.4 3.2 %collective-permute-done.10.refs_1_ = bf16[2,2,128,256]{3,2,1,0:T(8,128)(2,1)S(1)} collective-permute-done((bf16[2,2,128,256]{3,2,1,0:T(8,128)(2,1)S(1)}, bf16[2,2,128,256]{3,2,1,0:T(8,128)(2,1)S(1)}, u32[]{:S(2)}, u32[]{:S(2)}) %collective-permute-start.10) | collective-permute-done | bytes 262176 | tf_op jit(solution)/shard_map/ppermute | solution.py:32
  55.6 2.8 %collective-permute-done.11.refs_2_ = bf16[2,2,128,256]{3,2,1,0:T(8,128)(2,1)S(1)} collective-permute-done((bf16[2,2,128,256]{3,2,1,0:T(8,128)(2,1)S(1)}, bf16[2,2,128,256]{3,2,1,0:T(8,128)(2,1)S(1)}, u32[]{:S(2)}, u32[]{:S(2)}) %collective-permute-start.11) | collective-permute-done | bytes 262176 | tf_op jit(solution)/shard_map/ppermute | solution.py:32
  63.8 5.4 %collective-permute-done.13.low1.refs_1_ = bf16[4,2,128,256]{3,2,1,0:T(8,128)(2,1)S(1)} collective-permute-done((bf16[4,2,128,256]{3,2,1,0:T(8,128)(2,1)S(1)}, bf16[4,2,128,256]{3,2,1,0:T(8,128)(2,1)S(1)}, u32[]{:S(2)}, u32[]{:S(2)}) %collective-permute-start.13) | collective-permute-done | bytes 524320 | tf_op jit(solution)/shard_map/ppermute | solution.py:32
  69.2 2.7 %collective-permute-start.18 = (bf16[4,2,128,256]{3,2,1,0:T(8,128)(2,1)S(1)}, bf16[4,2,128,256]{3,2,1,0:T(8,128)(2,1)S(1)}, u32[]{:S(2)}, u32[]{:S(2)}) collective-permute-start(bf16[4,2,128,256]{3,2,1,0:T(8,128)(2,1)S(1)} %collective-permute-done.14.high3.refs_7_), channel_id=1, source_target_pairs={{0,192},{1,193},{2,194},{3,195},{4,196},{5,197},{6,198},{7,199},{8... | collective-permute-start | bytes 1572872 | tf_op jit(solution)/shard_map/ppermute | solution.py:32
  71.9 3.5 %early.1 = (bf16[1024,1024]{1,0:T(8,128)(2,1)S(1)}, f32[1024,1024]{1,0:T(8,128)S(1)}, f32[1024,1024]{1,0:T(8,128)S(1)}) custom-call(s32[4]{0:T(128)S(1)} %pad_add_fusion.place, bf16[8,512,128]{2,1,0:T(8,128)(2,1)S(1)} %all-to-all-done.mine, bf16[8,512,128]{2,1,0:T(8,128)(2,1)S(1)} %collective-permute-done.9.theirs, ...), custom_call_target="tpu_custom_call" | custom-call | flops 3221225472 | bytes 4194304 | tf_op jit(solution)/shard_map/early/pallas_call | solution.py:341
  75.4 2.8 %middle.1 = (f32[1024,1024]{1,0:T(8,128)S(1)}, f32[1024,1024]{1,0:T(8,128)S(1)}) custom-call(s32[4]{0:T(128)S(1)} %pad_add_fusion.place, bf16[1024,1024]{1,0:T(8,128)(2,1)S(1)} %get-tuple-element.56.rows, bf16[8,512,256]{2,1,0:T(8,128)(2,1)S(1)} %get-tuple-element.51.pot_mine.pot, ...), custom_call_target="tpu_custom_call", output_to_operand_aliasing={{0}: (5, {}), {1}: (4, {})} | custom-call | flops 2147483648 | bytes 4194304 | tf_op jit(solution)/shard_map/middle/pallas_call | solution.py:341
  78.2 2.3 %collective-permute-done.17.refs_2_ = bf16[4,2,128,256]{3,2,1,0:T(8,128)(2,1)S(1)} collective-permute-done((bf16[4,2,128,256]{3,2,1,0:T(8,128)(2,1)S(1)}, bf16[4,2,128,256]{3,2,1,0:T(8,128)(2,1)S(1)}, u32[]{:S(2)}, u32[]{:S(2)}) %collective-permute-start.17) | collective-permute-done | bytes 524320 | tf_op jit(solution)/shard_map/ppermute | solution.py:32
  80.4 3.6 %late.3 = bf16[512,1024]{1,0:T(8,128)(2,1)S(1)} custom-call(s32[4]{0:T(128)S(1)} %pad_add_fusion.place, bf16[1024,1024]{1,0:T(8,128)(2,1)S(1)} %get-tuple-element.56.rows, bf16[8,512,256]{2,1,0:T(8,128)(2,1)S(1)} %get-tuple-element.52.pot_theirs.pot, f32[1024,1024]{1,0:T(8,128)S(1)} %get-tuple-element.59.before, f32[1024,1024]{1,0:T(8,128)S(1)} %get-tuple-element.60.partial, ...), custom_call_target="tpu_custom_call" | custom-call | flops 1610612736 | bytes 4194304 | tf_op jit(solution)/shard_map/late/pallas_call | solution.py:341
  84.5 3.4 %late.2.mine = f32[512,1024]{1,0:T(8,128)S(1)} custom-call(s32[4]{0:T(128)S(1)} %pad_add_fusion.place, bf16[1024,1024]{1,0:T(8,128)(2,1)S(1)} %get-tuple-element.56.rows, bf16[8,512,256]{2,1,0:T(8,128)(2,1)S(1)} %get-tuple-element.51.pot_mine.pot, f32[1024,1024]{1,0:T(8,128)S(1)} %get-tuple-element.59.before, f32[1024,1024]{1,0:T(8,128)S(1)} %get-tuple-element.60.partial, ...), custom_call_target="tpu_custom_call" | custom-call | flops 1610612736 | bytes 4194304 | tf_op jit(solution)/shard_map/late/pallas_call | solution.py:341
  89.0 2.4 %collective-permute-start.20 = (bf16[512,128]{1,0:T(8,128)(2,1)S(1)}, bf16[512,128]{1,0:T(8,128)(2,1)S(1)}, u32[]{:S(2)}, u32[]{:S(2)}) collective-permute-start(bf16[512,128]{1,0:T(8,128)(2,1)S(1)} %get-tuple-element.61), channel_id=1, source_target_pairs={{0,5},{1,4},{2,7},{3,6},{4,1},{5,0},{6,3},{7,2},{8,13},{9,12},{10,... | collective-permute-start | bytes 393224 | tf_op jit(solution)/shard_map/ppermute | solution.py:32
  93.2 2.8 %collective-permute-start.23 = (bf16[512,128]{1,0:T(8,128)(2,1)S(1)}, bf16[512,128]{1,0:T(8,128)(2,1)S(1)}, u32[]{:S(2)}, u32[]{:S(2)}) collective-permute-start(bf16[512,128]{1,0:T(8,128)(2,1)S(1)} %get-tuple-element.64), channel_id=1, source_target_pairs={{0,7},{1,6},{2,5},{3,4},{4,3},{5,2},{6,1},{7,0},{8,15},{9,14},{10,... | collective-permute-start | bytes 393224 | tf_op jit(solution)/shard_map/ppermute | solution.py:32
  96.7 2.4 %collective-permute-start.25 = (bf16[512,128]{1,0:T(8,128)(2,1)S(1)}, bf16[512,128]{1,0:T(8,128)(2,1)S(1)}, u32[]{:S(2)}, u32[]{:S(2)}) collective-permute-start(bf16[512,128]{1,0:T(8,128)(2,1)S(1)} %get-tuple-element.66), channel_id=1, source_target_pairs={{0,6},{1,7},{2,4},{3,5},{4,2},{5,3},{6,0},{7,1},{8,14},{9,15},{10,... | collective-permute-start | bytes 393224 | tf_op jit(solution)/shard_map/ppermute | solution.py:32
  100.1 2.9 %collective-permute-done.23.refs_3_ = bf16[512,128]{1,0:T(8,128)(2,1)S(1)} collective-permute-done((bf16[512,128]{1,0:T(8,128)(2,1)S(1)}, bf16[512,128]{1,0:T(8,128)(2,1)S(1)}, u32[]{:S(2)}, u32[]{:S(2)}) %collective-permute-start.23) | collective-permute-done | bytes 131104 | tf_op jit(solution)/shard_map/ppermute | solution.py:32
  103.0 2.6 %collective-permute-done.24.refs_4_ = bf16[512,128]{1,0:T(8,128)(2,1)S(1)} collective-permute-done((bf16[512,128]{1,0:T(8,128)(2,1)S(1)}, bf16[512,128]{1,0:T(8,128)(2,1)S(1)}, u32[]{:S(2)}, u32[]{:S(2)}) %collective-permute-start.24) | collective-permute-done | bytes 131104 | tf_op jit(solution)/shard_map/ppermute | solution.py:32
  (53 shorter events, 29.5 us)
Async XLA Ops:
  0.0 30.5 %collective-permute-start.7 = (bf16[512,4096]{1,0:T(8,128)(2,1)}, bf16[512,4096]{1,0:T(8,128)(2,1)}, u32[]{:S(2)}, u32[]{:S(2)}) collective-permute-start(bf16[512,4096]{1,0:T(8,128)(2,1)} %refs_0_.1), channel_id=1, source_target_pairs={{0,8},{1,9},{2,10},{3,11},{4,12},{5,13},{6,14},{7,15},{8,0},{9,1},... | collective-permute-start | bytes 12582920 | tf_op jit(solution)/shard_map/ppermute | solution.py:32
  3.2 21.0 %all-to-all-start = ((bf16[8,512,128]{2,1,0:T(8,128)(2,1)}), bf16[8,512,128]{2,1,0:T(8,128)(2,1)S(1)}, u32[]{:S(2)}, u32[]{:S(2)}) async-start(bf16[8,512,128]{2,1,0:T(8,128)(2,1)} %bitcast.10), calls=%async_computation | async-start | bytes 2097152 | tf_op jit(solution)/shard_map/all_to_all | solution.py:415
  15.9 8.4 %collective-permute-start.2 = (bf16[2,128,256]{2,1,0:T(8,128)(2,1)S(1)}, bf16[2,128,256]{2,1,0:T(8,128)(2,1)S(1)}, u32[]{:S(2)}, u32[]{:S(2)}) collective-permute-start(bf16[2,128,256]{2,1,0:T(8,128)(2,1)S(1)} %get-tuple-element.40), channel_id=1, source_target_pairs={{0,192},{1,193},{2,194},{3,195},{4,196},{5,197},{6,198},{7,199},{8... | collective-permute-start | bytes 393224 | tf_op jit(solution)/shard_map/ppermute | solution.py:32
  16.6 7.6 %collective-permute-start.3 = (bf16[2,128,256]{2,1,0:T(8,128)(2,1)S(1)}, bf16[2,128,256]{2,1,0:T(8,128)(2,1)S(1)}, u32[]{:S(2)}, u32[]{:S(2)}) collective-permute-start(bf16[2,128,256]{2,1,0:T(8,128)(2,1)S(1)} %get-tuple-element.41), channel_id=1, source_target_pairs={{0,64},{1,65},{2,66},{3,67},{4,68},{5,69},{6,70},{7,71},{8,72},{9,... | collective-permute-start | bytes 393224 | tf_op jit(solution)/shard_map/ppermute | solution.py:32
  24.3 10.9 %collective-permute-start.4 = (bf16[2,128,256]{2,1,0:T(8,128)(2,1)S(1)}, bf16[2,128,256]{2,1,0:T(8,128)(2,1)S(1)}, u32[]{:S(2)}, u32[]{:S(2)}) collective-permute-start(bf16[2,128,256]{2,1,0:T(8,128)(2,1)S(1)} %add_add_fusion.1), channel_id=1, source_target_pairs={{0,32},{1,33},{2,34},{3,35},{4,36},{5,37},{6,38},{7,39},{8,40},{9,... | collective-permute-start | bytes 393224 | tf_op jit(solution)/shard_map/ppermute | solution.py:32
  29.2 10.3 %collective-permute-start.5 = (bf16[2,128,256]{2,1,0:T(8,128)(2,1)S(1)}, bf16[2,128,256]{2,1,0:T(8,128)(2,1)S(1)}, u32[]{:S(2)}, u32[]{:S(2)}) collective-permute-start(bf16[2,128,256]{2,1,0:T(8,128)(2,1)S(1)} %add_add_fusion.1), channel_id=1, source_target_pairs={{0,48},{1,49},{2,50},{3,51},{4,52},{5,53},{6,54},{7,55},{8,56},{9,... | collective-permute-start | bytes 393224 | tf_op jit(solution)/shard_map/ppermute | solution.py:32
  29.2 13.2 %collective-permute-start.6 = (bf16[2,128,256]{2,1,0:T(8,128)(2,1)S(1)}, bf16[2,128,256]{2,1,0:T(8,128)(2,1)S(1)}, u32[]{:S(2)}, u32[]{:S(2)}) collective-permute-start(bf16[2,128,256]{2,1,0:T(8,128)(2,1)S(1)} %add_add_fusion.1), channel_id=1, source_target_pairs={{0,16},{1,17},{2,18},{3,19},{4,20},{5,21},{6,22},{7,23},{8,24},{9,... | collective-permute-start | bytes 393224 | tf_op jit(solution)/shard_map/ppermute | solution.py:32
  47.1 24.8 %collective-permute-start.9 = (bf16[8,512,128]{2,1,0:T(8,128)(2,1)S(1)}, bf16[8,512,128]{2,1,0:T(8,128)(2,1)S(1)}, u32[]{:S(2)}, u32[]{:S(2)}) collective-permute-start(bf16[8,512,128]{2,1,0:T(8,128)(2,1)S(1)} %all-to-all-done.mine), channel_id=1, source_target_pairs={{0,8},{1,9},{2,10},{3,11},{4,12},{5,13},{6,14},{7,15},{8,0},{9,1},... | collective-permute-start | bytes 3145736 | tf_op jit(solution)/shard_map/ppermute | solution.py:32
  48.6 7.0 %collective-permute-start.10 = (bf16[2,2,128,256]{3,2,1,0:T(8,128)(2,1)S(1)}, bf16[2,2,128,256]{3,2,1,0:T(8,128)(2,1)S(1)}, u32[]{:S(2)}, u32[]{:S(2)}) collective-permute-start(bf16[2,2,128,256]{3,2,1,0:T(8,128)(2,1)S(1)} %pad_maximum_fusion.refs_0_), channel_id=1, source_target_pairs={{0,4},{1,5},{2,6},{3,7},{4,0},{5,1},{6,2},{7,3},{8,136},{9,137},{1... | collective-permute-start | bytes 786440 | tf_op jit(solution)/shard_map/ppermute | solution.py:32
  50.3 8.1 %collective-permute-start.11 = (bf16[2,2,128,256]{3,2,1,0:T(8,128)(2,1)S(1)}, bf16[2,2,128,256]{3,2,1,0:T(8,128)(2,1)S(1)}, u32[]{:S(2)}, u32[]{:S(2)}) collective-permute-start(bf16[2,2,128,256]{3,2,1,0:T(8,128)(2,1)S(1)} %pad_maximum_fusion.refs_0_), channel_id=1, source_target_pairs={{0,6},{1,7},{2,4},{3,5},{4,2},{5,3},{6,0},{7,1},{8,200},{9,201},{1... | collective-permute-start | bytes 786440 | tf_op jit(solution)/shard_map/ppermute | solution.py:32
  52.4 6.5 %collective-permute-start.12 = (bf16[2,2,128,256]{3,2,1,0:T(8,128)(2,1)S(1)}, bf16[2,2,128,256]{3,2,1,0:T(8,128)(2,1)S(1)}, u32[]{:S(2)}, u32[]{:S(2)}) collective-permute-start(bf16[2,2,128,256]{3,2,1,0:T(8,128)(2,1)S(1)} %pad_maximum_fusion.refs_0_), channel_id=1, source_target_pairs={{0,2},{1,3},{2,0},{3,1},{4,6},{5,7},{6,4},{7,5},{8,72},{9,73},{10,... | collective-permute-start | bytes 786440 | tf_op jit(solution)/shard_map/ppermute | solution.py:32
  59.6 9.6 %collective-permute-start.13 = (bf16[4,2,128,256]{3,2,1,0:T(8,128)(2,1)S(1)}, bf16[4,2,128,256]{3,2,1,0:T(8,128)(2,1)S(1)}, u32[]{:S(2)}, u32[]{:S(2)}) collective-permute-start(bf16[4,2,128,256]{3,2,1,0:T(8,128)(2,1)S(1)} %get-tuple-element.54.low0.refs_0_), channel_id=1, source_target_pairs={{0,64},{1,65},{2,66},{3,67},{4,68},{5,69},{6,70},{7,71},{8,10},{9,... | collective-permute-start | bytes 1572872 | tf_op jit(solution)/shard_map/ppermute | solution.py:32
  60.8 8.4 %collective-permute-start.14 = (bf16[4,2,128,256]{3,2,1,0:T(8,128)(2,1)S(1)}, bf16[4,2,128,256]{3,2,1,0:T(8,128)(2,1)S(1)}, u32[]{:S(2)}, u32[]{:S(2)}) collective-permute-start(bf16[4,2,128,256]{3,2,1,0:T(8,128)(2,1)S(1)} %get-tuple-element.55.high0.refs_4_), channel_id=1, source_target_pairs={{0,192},{1,193},{2,194},{3,195},{4,196},{5,197},{6,198},{7,199},{8... | collective-permute-start | bytes 1572872 | tf_op jit(solution)/shard_map/ppermute | solution.py:32
  62.3 13.0 %collective-permute-start.15 = (bf16[4,2,128,256]{3,2,1,0:T(8,128)(2,1)S(1)}, bf16[4,2,128,256]{3,2,1,0:T(8,128)(2,1)S(1)}, u32[]{:S(2)}, u32[]{:S(2)}) collective-permute-start(bf16[4,2,128,256]{3,2,1,0:T(8,128)(2,1)S(1)} %get-tuple-element.54.low0.refs_0_), channel_id=1, source_target_pairs={{0,192},{1,193},{2,194},{3,195},{4,196},{5,197},{6,198},{7,199},{8... | collective-permute-start | bytes 1572872 | tf_op jit(solution)/shard_map/ppermute | solution.py:32
  63.5 11.9 %collective-permute-start.16 = (bf16[4,2,128,256]{3,2,1,0:T(8,128)(2,1)S(1)}, bf16[4,2,128,256]{3,2,1,0:T(8,128)(2,1)S(1)}, u32[]{:S(2)}, u32[]{:S(2)}) collective-permute-start(bf16[4,2,128,256]{3,2,1,0:T(8,128)(2,1)S(1)} %get-tuple-element.55.high0.refs_4_), channel_id=1, source_target_pairs={{0,64},{1,65},{2,66},{3,67},{4,68},{5,69},{6,70},{7,71},{8,10},{9,... | collective-permute-start | bytes 1572872 | tf_op jit(solution)/shard_map/ppermute | solution.py:32
  69.2 11.2 %collective-permute-start.17 = (bf16[4,2,128,256]{3,2,1,0:T(8,128)(2,1)S(1)}, bf16[4,2,128,256]{3,2,1,0:T(8,128)(2,1)S(1)}, u32[]{:S(2)}, u32[]{:S(2)}) collective-permute-start(bf16[4,2,128,256]{3,2,1,0:T(8,128)(2,1)S(1)} %collective-permute-done.13.low1.refs_1_), channel_id=1, source_target_pairs={{0,64},{1,65},{2,66},{3,67},{4,68},{5,69},{6,70},{7,71},{8,10},{9,... | collective-permute-start | bytes 1572872 | tf_op jit(solution)/shard_map/ppermute | solution.py:32
  69.2 11.2 %collective-permute-start.18 = (bf16[4,2,128,256]{3,2,1,0:T(8,128)(2,1)S(1)}, bf16[4,2,128,256]{3,2,1,0:T(8,128)(2,1)S(1)}, u32[]{:S(2)}, u32[]{:S(2)}) collective-permute-start(bf16[4,2,128,256]{3,2,1,0:T(8,128)(2,1)S(1)} %collective-permute-done.14.high3.refs_7_), channel_id=1, source_target_pairs={{0,192},{1,193},{2,194},{3,195},{4,196},{5,197},{6,198},{7,199},{8... | collective-permute-start | bytes 1572872 | tf_op jit(solution)/shard_map/ppermute | solution.py:32
  89.0 7.7 %collective-permute-start.20 = (bf16[512,128]{1,0:T(8,128)(2,1)S(1)}, bf16[512,128]{1,0:T(8,128)(2,1)S(1)}, u32[]{:S(2)}, u32[]{:S(2)}) collective-permute-start(bf16[512,128]{1,0:T(8,128)(2,1)S(1)} %get-tuple-element.61), channel_id=1, source_target_pairs={{0,5},{1,4},{2,7},{3,6},{4,1},{5,0},{6,3},{7,2},{8,13},{9,12},{10,... | collective-permute-start | bytes 393224 | tf_op jit(solution)/shard_map/ppermute | solution.py:32
  91.4 7.7 %collective-permute-start.21 = (bf16[512,128]{1,0:T(8,128)(2,1)S(1)}, bf16[512,128]{1,0:T(8,128)(2,1)S(1)}, u32[]{:S(2)}, u32[]{:S(2)}) collective-permute-start(bf16[512,128]{1,0:T(8,128)(2,1)S(1)} %get-tuple-element.62), channel_id=1, source_target_pairs={{0,1},{1,0},{2,3},{3,2},{4,5},{5,4},{6,7},{7,6},{8,9},{9,8},{10,11... | collective-permute-start | bytes 393224 | tf_op jit(solution)/shard_map/ppermute | solution.py:32
  92.3 7.8 %collective-permute-start.22 = (bf16[512,128]{1,0:T(8,128)(2,1)S(1)}, bf16[512,128]{1,0:T(8,128)(2,1)S(1)}, u32[]{:S(2)}, u32[]{:S(2)}) collective-permute-start(bf16[512,128]{1,0:T(8,128)(2,1)S(1)} %get-tuple-element.63), channel_id=1, source_target_pairs={{0,4},{1,5},{2,6},{3,7},{4,0},{5,1},{6,2},{7,3},{8,12},{9,13},{10,... | collective-permute-start | bytes 393224 | tf_op jit(solution)/shard_map/ppermute | solution.py:32
  93.2 9.8 %collective-permute-start.23 = (bf16[512,128]{1,0:T(8,128)(2,1)S(1)}, bf16[512,128]{1,0:T(8,128)(2,1)S(1)}, u32[]{:S(2)}, u32[]{:S(2)}) collective-permute-start(bf16[512,128]{1,0:T(8,128)(2,1)S(1)} %get-tuple-element.64), channel_id=1, source_target_pairs={{0,7},{1,6},{2,5},{3,4},{4,3},{5,2},{6,1},{7,0},{8,15},{9,14},{10,... | collective-permute-start | bytes 393224 | tf_op jit(solution)/shard_map/ppermute | solution.py:32
  96.0 9.5 %collective-permute-start.24 = (bf16[512,128]{1,0:T(8,128)(2,1)S(1)}, bf16[512,128]{1,0:T(8,128)(2,1)S(1)}, u32[]{:S(2)}, u32[]{:S(2)}) collective-permute-start(bf16[512,128]{1,0:T(8,128)(2,1)S(1)} %get-tuple-element.65), channel_id=1, source_target_pairs={{0,3},{1,2},{2,1},{3,0},{4,7},{5,6},{6,5},{7,4},{8,11},{9,10},{10,... | collective-permute-start | bytes 393224 | tf_op jit(solution)/shard_map/ppermute | solution.py:32
  96.7 9.0 %collective-permute-start.25 = (bf16[512,128]{1,0:T(8,128)(2,1)S(1)}, bf16[512,128]{1,0:T(8,128)(2,1)S(1)}, u32[]{:S(2)}, u32[]{:S(2)}) collective-permute-start(bf16[512,128]{1,0:T(8,128)(2,1)S(1)} %get-tuple-element.66), channel_id=1, source_target_pairs={{0,6},{1,7},{2,4},{3,5},{4,2},{5,3},{6,0},{7,1},{8,14},{9,15},{10,... | collective-permute-start | bytes 393224 | tf_op jit(solution)/shard_map/ppermute | solution.py:32
  99.1 7.4 %collective-permute-start.26 = (bf16[512,128]{1,0:T(8,128)(2,1)S(1)}, bf16[512,128]{1,0:T(8,128)(2,1)S(1)}, u32[]{:S(2)}, u32[]{:S(2)}) collective-permute-start(bf16[512,128]{1,0:T(8,128)(2,1)S(1)} %get-tuple-element.67), channel_id=1, source_target_pairs={{0,2},{1,3},{2,0},{3,1},{4,6},{5,7},{6,4},{7,5},{8,10},{9,11},{10,... | collective-permute-start | bytes 393224 | tf_op jit(solution)/shard_map/ppermute | solution.py:32
  (7 other events, 27.3 us)

commit v5 on v4

--- a/solution.py
+++ b/solution.py
@@ -376,11 +376,11 @@
     )(place, mine, theirs)
 
 
-def put_kernel(place, *refs):
-    blocks, out, sem = refs[:8], refs[8], refs[9]
+def put_kernel(order, place, *refs):
+    blocks, out, sem = refs[: len(order)], refs[-2], refs[-1]
     x, zl = place[0], place[3]
     copies = []
-    for i, (d, dz) in enumerate(ORDER):
+    for i, (d, dz) in enumerate(order):
         run = (x ^ d) * 2 + (zl ^ dz)
         copies.append(pltpu.make_async_copy(blocks[i], out.at[run], sem.at[i]))
     for copy in copies:
@@ -389,17 +389,21 @@
         copy.wait()
 
 
-def put(place, blocks):
-    vmem = pl.BlockSpec(memory_space=pltpu.VMEM)
-    return pl.pallas_call(
-        put_kernel,
+def put(order, place, blocks, before=None):
+    vmem = pl.BlockSpec(memory_space=pltpu.VMEM)
+    anyspace = pl.BlockSpec(memory_space=pl.ANY)
+    number = len(order)
+    return pl.pallas_call(
+        functools.partial(put_kernel, order),
         out_shape=jax.ShapeDtypeStruct((8,) + blocks[0].shape, jnp.bfloat16),
-        in_specs=[pl.BlockSpec(memory_space=pltpu.SMEM)] + [vmem] * 8,
-        out_specs=pl.BlockSpec(memory_space=pl.ANY),
-        scratch_shapes=[pltpu.SemaphoreType.DMA((8,))],
-        compiler_params=pltpu.CompilerParams(vmem_limit_bytes=16 * 1024 * 1024),
+        in_specs=[pl.BlockSpec(memory_space=pltpu.SMEM)] + [vmem] * number + [anyspace] * (before is not None),
+        out_specs=anyspace,
+        scratch_shapes=[pltpu.SemaphoreType.DMA((number,))],
+        input_output_aliases={} if before is None else {number + 1: 0},
+        compiler_params=pltpu.CompilerParams(vmem_limit_bytes=16 * 1024 * 1024),
+        cost_estimate=pl.CostEstimate(flops=0, bytes_accessed=number * 300_000, transcendentals=0),
         name="put",
-    )(place, *blocks)
+    )(place, *blocks, *([] if before is None else [before]))
 
 
 def shards(orbitals, potentials, point_index):
@@ -450,7 +454,8 @@
     theirs = to_core(sent)
     blocks = total(place, kept, theirs)
     arrived = [to_owner(blocks[2 * d + dz], d, dz) for d, dz in ORDER[:-1]] + [blocks[0]]
-    return put(place, arrived).reshape(-1, 128)
+    first = put(ORDER[:4] + ORDER[7:], place, arrived[:4] + arrived[7:])
+    return put(ORDER[4:7], place, arrived[4:7], first).reshape(-1, 128)
 
 
 def solution(mesh):

time: 109 us -> 108 us (level)
  waiting for transfers between devices: 41.8 us -> 40.4 us
  Pallas kernels: 23.8 us -> 25 us
    ppermute x27, waiting for transfers between devices: 41.8 us -> 40.4 us  [send(): return lax.ppermute(value, AXES, moves(target))]
    pallas_call x1 -> x2, Pallas kernels: 1.57 us -> 2.73 us  [put(): pl.pallas_call(functools.partial(put_kernel, order), out_shape=jax.ShapeD...]
  transfers between devices with their start and end apart: 28 -> 28, of which waited for: 16 -> 16; matrix products, arithmetic and copies ran while one was open for 0% -> 0% of each run, Pallas kernels for 16% -> 18%
where the time goes in v5:
time: 108 us
  waiting for transfers between devices  40.4 us (37%)
  starting transfers between devices  39.2 us (36%)
  Pallas kernels  25 us (23%)
  local copies, waits for them, and re-layouts  2.91 us (3%)
    ppermute x27, waiting for transfers between devices, send(): return lax.ppermute(value, AXES, moves(target))  40.4 us
    ppermute x27, starting transfers between devices, send(): return lax.ppermute(value, AXES, moves(target))  35.5 us
    pallas_call x4, Pallas kernels, call(): pl.pallas_call(kernel, out_shape=outs, in_specs=[pl.BlockSpec(memory_spac...  13.3 us
    all_to_all x1, starting transfers between devices, shards(): lax.all_to_all(orbitals.reshape(8, -1, 128), 'orb', split_axis=0, concat_...  3.64 us
    unnamed x6, local copies, waits for them, and re-layouts  2.91 us
    pallas_call x2, Pallas kernels, put(): pl.pallas_call(functools.partial(put_kernel, order), out_shape=jax.ShapeD...  2.73 us
    pallas_call x1, Pallas kernels, pick(): pl.pallas_call(pick_kernel, out_shape=[block] * 4, in_specs=[pl.BlockSpec...  2.67 us
    pallas_call x1, Pallas kernels, pack(): pl.pallas_call(pack_kernel, out_shape=[jax.ShapeDtypeStruct((8, mine.shap...  2.51 us
  transfers between devices with their start and end apart: 28, of which 16 were waited for; matrix products, arithmetic and copies ran while one was open for 0% of the time, Pallas kernels for 18%

profile of v5, /device:TPU:1, one launch (start us, length us, event | category | flops | bytes accessed | tf_op | source)
XLA Modules:
  0.0 108.0 jit_solution(14535889348184362332)
XLA Ops:
  0.0 3.2 %collective-permute-start.7 = (bf16[512,4096]{1,0:T(8,128)(2,1)}, bf16[512,4096]{1,0:T(8,128)(2,1)}, u32[]{:S(2)}, u32[]{:S(2)}) collective-permute-start(bf16[512,4096]{1,0:T(8,128)(2,1)} %refs_0_.1), channel_id=1, source_target_pairs={{0,8},{1,9},{2,10},{3,11},{4,12},{5,13},{6,14},{7,15},{8,0},{9,1},... | collective-permute-start | bytes 12582920 | tf_op jit(solution)/shard_map/ppermute | solution.py:32
  3.2 3.6 %all-to-all-start = ((bf16[8,512,128]{2,1,0:T(8,128)(2,1)}), bf16[8,512,128]{2,1,0:T(8,128)(2,1)S(1)}, u32[]{:S(2)}, u32[]{:S(2)}) async-start(bf16[8,512,128]{2,1,0:T(8,128)(2,1)} %bitcast.10), calls=%async_computation | async-start | bytes 2097152 | tf_op jit(solution)/shard_map/all_to_all | solution.py:419
  11.7 2.7 %pick.1 = (bf16[2,128,256]{2,1,0:T(8,128)(2,1)S(1)}, bf16[2,128,256]{2,1,0:T(8,128)(2,1)S(1)}, bf16[2,128,256]{2,1,0:T(8,128)(2,1)S(1)}, bf16[2,128,256]{2,1,0:T(8,128)(2,1)S(1)}) custom-call(s32[3]{0:T(128)S(1)} %pad_add_fusion.1.place, s32[32,128]{1,0:T(8,128)S(1)} %get-tuple-element.37.slot_ref, f32[512,8]{1,0:T(8,128)S(1)} %get-tuple-element.38.where_ref, ...), custom_call_target="tpu_custom_call" | custom-call | flops 2500000000 | bytes 4000000 | tf_op jit(solution)/shard_map/pick/pallas_call | solution.py:153
  17.2 3.6 %collective-permute-done.1 = bf16[2,128,256]{2,1,0:T(8,128)(2,1)S(1)} collective-permute-done((bf16[2,128,256]{2,1,0:T(8,128)(2,1)S(1)}, bf16[2,128,256]{2,1,0:T(8,128)(2,1)S(1)}, u32[]{:S(2)}, u32[]{:S(2)}) %collective-permute-start.1) | collective-permute-done | bytes 131104 | tf_op jit(solution)/shard_map/ppermute | solution.py:32
  20.7 3.5 %collective-permute-done.2 = bf16[2,128,256]{2,1,0:T(8,128)(2,1)S(1)} collective-permute-done((bf16[2,128,256]{2,1,0:T(8,128)(2,1)S(1)}, bf16[2,128,256]{2,1,0:T(8,128)(2,1)S(1)}, u32[]{:S(2)}, u32[]{:S(2)}) %collective-permute-start.2) | collective-permute-done | bytes 131104 | tf_op jit(solution)/shard_map/ppermute | solution.py:32
  24.3 4.9 %collective-permute-start.4 = (bf16[2,128,256]{2,1,0:T(8,128)(2,1)S(1)}, bf16[2,128,256]{2,1,0:T(8,128)(2,1)S(1)}, u32[]{:S(2)}, u32[]{:S(2)}) collective-permute-start(bf16[2,128,256]{2,1,0:T(8,128)(2,1)S(1)} %add_add_fusion.1), channel_id=1, source_target_pairs={{0,32},{1,33},{2,34},{3,35},{4,36},{5,37},{6,38},{7,39},{8,40},{9,... | collective-permute-start | bytes 393224 | tf_op jit(solution)/shard_map/ppermute | solution.py:32
  30.5 2.2 %copy-done = bf16[512,4096]{1,0:T(8,128)(2,1)S(1)} copy-done((bf16[512,4096]{1,0:T(8,128)(2,1)S(1)}, bf16[512,4096]{1,0:T(8,128)(2,1)}, u32[]{:S(2)}) %copy-start) | copy-done | bytes 4194328
  32.6 2.5 %pack.1 = (bf16[8,512,256]{2,1,0:T(8,128)(2,1)S(1)}, bf16[8,512,256]{2,1,0:T(8,128)(2,1)S(1)}) custom-call(s32[4]{0:T(128)S(1)} %pad_add_fusion.place, bf16[512,4096]{1,0:T(8,128)(2,1)S(1)} %copy-done, bf16[512,4096]{1,0:T(8,128)(2,1)} %collective-permute-done.7.refs_1_), custom_call_target="tpu_custom_call" | custom-call | bytes 8000000 | tf_op jit(solution)/shard_map/pack/pallas_call | solution.py:212
  35.2 4.3 %collective-permute-done.5 = bf16[2,128,256]{2,1,0:T(8,128)(2,1)S(1)} collective-permute-done((bf16[2,128,256]{2,1,0:T(8,128)(2,1)S(1)}, bf16[2,128,256]{2,1,0:T(8,128)(2,1)S(1)}, u32[]{:S(2)}, u32[]{:S(2)}) %collective-permute-start.5) | collective-permute-done | bytes 131104 | tf_op jit(solution)/shard_map/ppermute | solution.py:32
  39.5 2.9 %collective-permute-done.6 = bf16[2,128,256]{2,1,0:T(8,128)(2,1)S(1)} collective-permute-done((bf16[2,128,256]{2,1,0:T(8,128)(2,1)S(1)}, bf16[2,128,256]{2,1,0:T(8,128)(2,1)S(1)}, u32[]{:S(2)}, u32[]{:S(2)}) %collective-permute-start.6) | collective-permute-done | bytes 131104 | tf_op jit(solution)/shard_map/ppermute | solution.py:32
  42.6 4.5 %collective-permute-done.8 = bf16[2,128,256]{2,1,0:T(8,128)(2,1)S(1)} collective-permute-done((bf16[2,128,256]{2,1,0:T(8,128)(2,1)S(1)}, bf16[2,128,256]{2,1,0:T(8,128)(2,1)S(1)}, u32[]{:S(2)}, u32[]{:S(2)}) %collective-permute-start.8) | collective-permute-done | bytes 131104 | tf_op jit(solution)/shard_map/ppermute | solution.py:32
  52.4 3.2 %collective-permute-done.10.refs_1_ = bf16[2,2,128,256]{3,2,1,0:T(8,128)(2,1)S(1)} collective-permute-done((bf16[2,2,128,256]{3,2,1,0:T(8,128)(2,1)S(1)}, bf16[2,2,128,256]{3,2,1,0:T(8,128)(2,1)S(1)}, u32[]{:S(2)}, u32[]{:S(2)}) %collective-permute-start.10) | collective-permute-done | bytes 262176 | tf_op jit(solution)/shard_map/ppermute | solution.py:32
  55.6 2.8 %collective-permute-done.11.refs_2_ = bf16[2,2,128,256]{3,2,1,0:T(8,128)(2,1)S(1)} collective-permute-done((bf16[2,2,128,256]{3,2,1,0:T(8,128)(2,1)S(1)}, bf16[2,2,128,256]{3,2,1,0:T(8,128)(2,1)S(1)}, u32[]{:S(2)}, u32[]{:S(2)}) %collective-permute-start.11) | collective-permute-done | bytes 262176 | tf_op jit(solution)/shard_map/ppermute | solution.py:32
  63.8 5.4 %collective-permute-done.13.low1.refs_1_ = bf16[4,2,128,256]{3,2,1,0:T(8,128)(2,1)S(1)} collective-permute-done((bf16[4,2,128,256]{3,2,1,0:T(8,128)(2,1)S(1)}, bf16[4,2,128,256]{3,2,1,0:T(8,128)(2,1)S(1)}, u32[]{:S(2)}, u32[]{:S(2)}) %collective-permute-start.13) | collective-permute-done | bytes 524320 | tf_op jit(solution)/shard_map/ppermute | solution.py:32
  69.2 2.7 %collective-permute-start.18 = (bf16[4,2,128,256]{3,2,1,0:T(8,128)(2,1)S(1)}, bf16[4,2,128,256]{3,2,1,0:T(8,128)(2,1)S(1)}, u32[]{:S(2)}, u32[]{:S(2)}) collective-permute-start(bf16[4,2,128,256]{3,2,1,0:T(8,128)(2,1)S(1)} %collective-permute-done.14.high3.refs_7_), channel_id=1, source_target_pairs={{0,192},{1,193},{2,194},{3,195},{4,196},{5,197},{6,198},{7,199},{8... | collective-permute-start | bytes 1572872 | tf_op jit(solution)/shard_map/ppermute | solution.py:32
  71.9 3.5 %early.1 = (bf16[1024,1024]{1,0:T(8,128)(2,1)S(1)}, f32[1024,1024]{1,0:T(8,128)S(1)}, f32[1024,1024]{1,0:T(8,128)S(1)}) custom-call(s32[4]{0:T(128)S(1)} %pad_add_fusion.place, bf16[8,512,128]{2,1,0:T(8,128)(2,1)S(1)} %all-to-all-done.mine, bf16[8,512,128]{2,1,0:T(8,128)(2,1)S(1)} %collective-permute-done.9.theirs, ...), custom_call_target="tpu_custom_call" | custom-call | flops 3221225472 | bytes 4194304 | tf_op jit(solution)/shard_map/early/pallas_call | solution.py:341
  75.4 2.8 %middle.1 = (f32[1024,1024]{1,0:T(8,128)S(1)}, f32[1024,1024]{1,0:T(8,128)S(1)}) custom-call(s32[4]{0:T(128)S(1)} %pad_add_fusion.place, bf16[1024,1024]{1,0:T(8,128)(2,1)S(1)} %get-tuple-element.56.rows, bf16[8,512,256]{2,1,0:T(8,128)(2,1)S(1)} %get-tuple-element.51.pot_mine.pot, ...), custom_call_target="tpu_custom_call", output_to_operand_aliasing={{0}: (5, {}), {1}: (4, {})} | custom-call | flops 2147483648 | bytes 4194304 | tf_op jit(solution)/shard_map/middle/pallas_call | solution.py:341
  78.2 2.3 %collective-permute-done.17.refs_2_ = bf16[4,2,128,256]{3,2,1,0:T(8,128)(2,1)S(1)} collective-permute-done((bf16[4,2,128,256]{3,2,1,0:T(8,128)(2,1)S(1)}, bf16[4,2,128,256]{3,2,1,0:T(8,128)(2,1)S(1)}, u32[]{:S(2)}, u32[]{:S(2)}) %collective-permute-start.17) | collective-permute-done | bytes 524320 | tf_op jit(solution)/shard_map/ppermute | solution.py:32
  80.4 3.6 %late.3 = bf16[512,1024]{1,0:T(8,128)(2,1)S(1)} custom-call(s32[4]{0:T(128)S(1)} %pad_add_fusion.place, bf16[1024,1024]{1,0:T(8,128)(2,1)S(1)} %get-tuple-element.56.rows, bf16[8,512,256]{2,1,0:T(8,128)(2,1)S(1)} %get-tuple-element.52.pot_theirs.pot, f32[1024,1024]{1,0:T(8,128)S(1)} %get-tuple-element.59.before, f32[1024,1024]{1,0:T(8,128)S(1)} %get-tuple-element.60.partial, ...), custom_call_target="tpu_custom_call" | custom-call | flops 1610612736 | bytes 4194304 | tf_op jit(solution)/shard_map/late/pallas_call | solution.py:341
  84.5 3.4 %late.2.mine = f32[512,1024]{1,0:T(8,128)S(1)} custom-call(s32[4]{0:T(128)S(1)} %pad_add_fusion.place, bf16[1024,1024]{1,0:T(8,128)(2,1)S(1)} %get-tuple-element.56.rows, bf16[8,512,256]{2,1,0:T(8,128)(2,1)S(1)} %get-tuple-element.51.pot_mine.pot, f32[1024,1024]{1,0:T(8,128)S(1)} %get-tuple-element.59.before, f32[1024,1024]{1,0:T(8,128)S(1)} %get-tuple-element.60.partial, ...), custom_call_target="tpu_custom_call" | custom-call | flops 1610612736 | bytes 4194304 | tf_op jit(solution)/shard_map/late/pallas_call | solution.py:341
  89.0 2.4 %collective-permute-start.23 = (bf16[512,128]{1,0:T(8,128)(2,1)S(1)}, bf16[512,128]{1,0:T(8,128)(2,1)S(1)}, u32[]{:S(2)}, u32[]{:S(2)}) collective-permute-start(bf16[512,128]{1,0:T(8,128)(2,1)S(1)} %get-tuple-element.64), channel_id=1, source_target_pairs={{0,5},{1,4},{2,7},{3,6},{4,1},{5,0},{6,3},{7,2},{8,13},{9,12},{10,... | collective-permute-start | bytes 393224 | tf_op jit(solution)/shard_map/ppermute | solution.py:32
  93.2 2.8 %collective-permute-start.26 = (bf16[512,128]{1,0:T(8,128)(2,1)S(1)}, bf16[512,128]{1,0:T(8,128)(2,1)S(1)}, u32[]{:S(2)}, u32[]{:S(2)}) collective-permute-start(bf16[512,128]{1,0:T(8,128)(2,1)S(1)} %get-tuple-element.67), channel_id=1, source_target_pairs={{0,7},{1,6},{2,5},{3,4},{4,3},{5,2},{6,1},{7,0},{8,15},{9,14},{10,... | collective-permute-start | bytes 393224 | tf_op jit(solution)/shard_map/ppermute | solution.py:32
  96.7 2.4 %collective-permute-start.21 = (bf16[512,128]{1,0:T(8,128)(2,1)S(1)}, bf16[512,128]{1,0:T(8,128)(2,1)S(1)}, u32[]{:S(2)}, u32[]{:S(2)}) collective-permute-start(bf16[512,128]{1,0:T(8,128)(2,1)S(1)} %get-tuple-element.62), channel_id=1, source_target_pairs={{0,6},{1,7},{2,4},{3,5},{4,2},{5,3},{6,0},{7,1},{8,14},{9,15},{10,... | collective-permute-start | bytes 393224 | tf_op jit(solution)/shard_map/ppermute | solution.py:32
  100.1 2.9 %collective-permute-done.26.refs_3_ = bf16[512,128]{1,0:T(8,128)(2,1)S(1)} collective-permute-done((bf16[512,128]{1,0:T(8,128)(2,1)S(1)}, bf16[512,128]{1,0:T(8,128)(2,1)S(1)}, u32[]{:S(2)}, u32[]{:S(2)}) %collective-permute-start.26) | collective-permute-done | bytes 131104 | tf_op jit(solution)/shard_map/ppermute | solution.py:32
  (54 shorter events, 29.7 us)
Async XLA Ops:
  0.0 30.5 %collective-permute-start.7 = (bf16[512,4096]{1,0:T(8,128)(2,1)}, bf16[512,4096]{1,0:T(8,128)(2,1)}, u32[]{:S(2)}, u32[]{:S(2)}) collective-permute-start(bf16[512,4096]{1,0:T(8,128)(2,1)} %refs_0_.1), channel_id=1, source_target_pairs={{0,8},{1,9},{2,10},{3,11},{4,12},{5,13},{6,14},{7,15},{8,0},{9,1},... | collective-permute-start | bytes 12582920 | tf_op jit(solution)/shard_map/ppermute | solution.py:32
  3.2 21.0 %all-to-all-start = ((bf16[8,512,128]{2,1,0:T(8,128)(2,1)}), bf16[8,512,128]{2,1,0:T(8,128)(2,1)S(1)}, u32[]{:S(2)}, u32[]{:S(2)}) async-start(bf16[8,512,128]{2,1,0:T(8,128)(2,1)} %bitcast.10), calls=%async_computation | async-start | bytes 2097152 | tf_op jit(solution)/shard_map/all_to_all | solution.py:419
  15.9 8.4 %collective-permute-start.2 = (bf16[2,128,256]{2,1,0:T(8,128)(2,1)S(1)}, bf16[2,128,256]{2,1,0:T(8,128)(2,1)S(1)}, u32[]{:S(2)}, u32[]{:S(2)}) collective-permute-start(bf16[2,128,256]{2,1,0:T(8,128)(2,1)S(1)} %get-tuple-element.40), channel_id=1, source_target_pairs={{0,192},{1,193},{2,194},{3,195},{4,196},{5,197},{6,198},{7,199},{8... | collective-permute-start | bytes 393224 | tf_op jit(solution)/shard_map/ppermute | solution.py:32
  16.6 7.6 %collective-permute-start.3 = (bf16[2,128,256]{2,1,0:T(8,128)(2,1)S(1)}, bf16[2,128,256]{2,1,0:T(8,128)(2,1)S(1)}, u32[]{:S(2)}, u32[]{:S(2)}) collective-permute-start(bf16[2,128,256]{2,1,0:T(8,128)(2,1)S(1)} %get-tuple-element.41), channel_id=1, source_target_pairs={{0,64},{1,65},{2,66},{3,67},{4,68},{5,69},{6,70},{7,71},{8,72},{9,... | collective-permute-start | bytes 393224 | tf_op jit(solution)/shard_map/ppermute | solution.py:32
  24.3 10.9 %collective-permute-start.4 = (bf16[2,128,256]{2,1,0:T(8,128)(2,1)S(1)}, bf16[2,128,256]{2,1,0:T(8,128)(2,1)S(1)}, u32[]{:S(2)}, u32[]{:S(2)}) collective-permute-start(bf16[2,128,256]{2,1,0:T(8,128)(2,1)S(1)} %add_add_fusion.1), channel_id=1, source_target_pairs={{0,32},{1,33},{2,34},{3,35},{4,36},{5,37},{6,38},{7,39},{8,40},{9,... | collective-permute-start | bytes 393224 | tf_op jit(solution)/shard_map/ppermute | solution.py:32
  29.2 10.3 %collective-permute-start.5 = (bf16[2,128,256]{2,1,0:T(8,128)(2,1)S(1)}, bf16[2,128,256]{2,1,0:T(8,128)(2,1)S(1)}, u32[]{:S(2)}, u32[]{:S(2)}) collective-permute-start(bf16[2,128,256]{2,1,0:T(8,128)(2,1)S(1)} %add_add_fusion.1), channel_id=1, source_target_pairs={{0,48},{1,49},{2,50},{3,51},{4,52},{5,53},{6,54},{7,55},{8,56},{9,... | collective-permute-start | bytes 393224 | tf_op jit(solution)/shard_map/ppermute | solution.py:32
  29.2 13.2 %collective-permute-start.6 = (bf16[2,128,256]{2,1,0:T(8,128)(2,1)S(1)}, bf16[2,128,256]{2,1,0:T(8,128)(2,1)S(1)}, u32[]{:S(2)}, u32[]{:S(2)}) collective-permute-start(bf16[2,128,256]{2,1,0:T(8,128)(2,1)S(1)} %add_add_fusion.1), channel_id=1, source_target_pairs={{0,16},{1,17},{2,18},{3,19},{4,20},{5,21},{6,22},{7,23},{8,24},{9,... | collective-permute-start | bytes 393224 | tf_op jit(solution)/shard_map/ppermute | solution.py:32
  47.1 24.8 %collective-permute-start.9 = (bf16[8,512,128]{2,1,0:T(8,128)(2,1)S(1)}, bf16[8,512,128]{2,1,0:T(8,128)(2,1)S(1)}, u32[]{:S(2)}, u32[]{:S(2)}) collective-permute-start(bf16[8,512,128]{2,1,0:T(8,128)(2,1)S(1)} %all-to-all-done.mine), channel_id=1, source_target_pairs={{0,8},{1,9},{2,10},{3,11},{4,12},{5,13},{6,14},{7,15},{8,0},{9,1},... | collective-permute-start | bytes 3145736 | tf_op jit(solution)/shard_map/ppermute | solution.py:32
  48.6 7.0 %collective-permute-start.10 = (bf16[2,2,128,256]{3,2,1,0:T(8,128)(2,1)S(1)}, bf16[2,2,128,256]{3,2,1,0:T(8,128)(2,1)S(1)}, u32[]{:S(2)}, u32[]{:S(2)}) collective-permute-start(bf16[2,2,128,256]{3,2,1,0:T(8,128)(2,1)S(1)} %pad_maximum_fusion.refs_0_), channel_id=1, source_target_pairs={{0,4},{1,5},{2,6},{3,7},{4,0},{5,1},{6,2},{7,3},{8,136},{9,137},{1... | collective-permute-start | bytes 786440 | tf_op jit(solution)/shard_map/ppermute | solution.py:32
  50.3 8.1 %collective-permute-start.11 = (bf16[2,2,128,256]{3,2,1,0:T(8,128)(2,1)S(1)}, bf16[2,2,128,256]{3,2,1,0:T(8,128)(2,1)S(1)}, u32[]{:S(2)}, u32[]{:S(2)}) collective-permute-start(bf16[2,2,128,256]{3,2,1,0:T(8,128)(2,1)S(1)} %pad_maximum_fusion.refs_0_), channel_id=1, source_target_pairs={{0,6},{1,7},{2,4},{3,5},{4,2},{5,3},{6,0},{7,1},{8,200},{9,201},{1... | collective-permute-start | bytes 786440 | tf_op jit(solution)/shard_map/ppermute | solution.py:32
  52.4 6.5 %collective-permute-start.12 = (bf16[2,2,128,256]{3,2,1,0:T(8,128)(2,1)S(1)}, bf16[2,2,128,256]{3,2,1,0:T(8,128)(2,1)S(1)}, u32[]{:S(2)}, u32[]{:S(2)}) collective-permute-start(bf16[2,2,128,256]{3,2,1,0:T(8,128)(2,1)S(1)} %pad_maximum_fusion.refs_0_), channel_id=1, source_target_pairs={{0,2},{1,3},{2,0},{3,1},{4,6},{5,7},{6,4},{7,5},{8,72},{9,73},{10,... | collective-permute-start | bytes 786440 | tf_op jit(solution)/shard_map/ppermute | solution.py:32
  59.6 9.6 %collective-permute-start.13 = (bf16[4,2,128,256]{3,2,1,0:T(8,128)(2,1)S(1)}, bf16[4,2,128,256]{3,2,1,0:T(8,128)(2,1)S(1)}, u32[]{:S(2)}, u32[]{:S(2)}) collective-permute-start(bf16[4,2,128,256]{3,2,1,0:T(8,128)(2,1)S(1)} %get-tuple-element.54.low0.refs_0_), channel_id=1, source_target_pairs={{0,64},{1,65},{2,66},{3,67},{4,68},{5,69},{6,70},{7,71},{8,10},{9,... | collective-permute-start | bytes 1572872 | tf_op jit(solution)/shard_map/ppermute | solution.py:32
  60.8 8.4 %collective-permute-start.14 = (bf16[4,2,128,256]{3,2,1,0:T(8,128)(2,1)S(1)}, bf16[4,2,128,256]{3,2,1,0:T(8,128)(2,1)S(1)}, u32[]{:S(2)}, u32[]{:S(2)}) collective-permute-start(bf16[4,2,128,256]{3,2,1,0:T(8,128)(2,1)S(1)} %get-tuple-element.55.high0.refs_4_), channel_id=1, source_target_pairs={{0,192},{1,193},{2,194},{3,195},{4,196},{5,197},{6,198},{7,199},{8... | collective-permute-start | bytes 1572872 | tf_op jit(solution)/shard_map/ppermute | solution.py:32
  62.3 13.0 %collective-permute-start.15 = (bf16[4,2,128,256]{3,2,1,0:T(8,128)(2,1)S(1)}, bf16[4,2,128,256]{3,2,1,0:T(8,128)(2,1)S(1)}, u32[]{:S(2)}, u32[]{:S(2)}) collective-permute-start(bf16[4,2,128,256]{3,2,1,0:T(8,128)(2,1)S(1)} %get-tuple-element.54.low0.refs_0_), channel_id=1, source_target_pairs={{0,192},{1,193},{2,194},{3,195},{4,196},{5,197},{6,198},{7,199},{8... | collective-permute-start | bytes 1572872 | tf_op jit(solution)/shard_map/ppermute | solution.py:32
  63.5 11.9 %collective-permute-start.16 = (bf16[4,2,128,256]{3,2,1,0:T(8,128)(2,1)S(1)}, bf16[4,2,128,256]{3,2,1,0:T(8,128)(2,1)S(1)}, u32[]{:S(2)}, u32[]{:S(2)}) collective-permute-start(bf16[4,2,128,256]{3,2,1,0:T(8,128)(2,1)S(1)} %get-tuple-element.55.high0.refs_4_), channel_id=1, source_target_pairs={{0,64},{1,65},{2,66},{3,67},{4,68},{5,69},{6,70},{7,71},{8,10},{9,... | collective-permute-start | bytes 1572872 | tf_op jit(solution)/shard_map/ppermute | solution.py:32
  69.2 11.2 %collective-permute-start.17 = (bf16[4,2,128,256]{3,2,1,0:T(8,128)(2,1)S(1)}, bf16[4,2,128,256]{3,2,1,0:T(8,128)(2,1)S(1)}, u32[]{:S(2)}, u32[]{:S(2)}) collective-permute-start(bf16[4,2,128,256]{3,2,1,0:T(8,128)(2,1)S(1)} %collective-permute-done.13.low1.refs_1_), channel_id=1, source_target_pairs={{0,64},{1,65},{2,66},{3,67},{4,68},{5,69},{6,70},{7,71},{8,10},{9,... | collective-permute-start | bytes 1572872 | tf_op jit(solution)/shard_map/ppermute | solution.py:32
  69.2 11.2 %collective-permute-start.18 = (bf16[4,2,128,256]{3,2,1,0:T(8,128)(2,1)S(1)}, bf16[4,2,128,256]{3,2,1,0:T(8,128)(2,1)S(1)}, u32[]{:S(2)}, u32[]{:S(2)}) collective-permute-start(bf16[4,2,128,256]{3,2,1,0:T(8,128)(2,1)S(1)} %collective-permute-done.14.high3.refs_7_), channel_id=1, source_target_pairs={{0,192},{1,193},{2,194},{3,195},{4,196},{5,197},{6,198},{7,199},{8... | collective-permute-start | bytes 1572872 | tf_op jit(solution)/shard_map/ppermute | solution.py:32
  89.0 7.7 %collective-permute-start.23 = (bf16[512,128]{1,0:T(8,128)(2,1)S(1)}, bf16[512,128]{1,0:T(8,128)(2,1)S(1)}, u32[]{:S(2)}, u32[]{:S(2)}) collective-permute-start(bf16[512,128]{1,0:T(8,128)(2,1)S(1)} %get-tuple-element.64), channel_id=1, source_target_pairs={{0,5},{1,4},{2,7},{3,6},{4,1},{5,0},{6,3},{7,2},{8,13},{9,12},{10,... | collective-permute-start | bytes 393224 | tf_op jit(solution)/shard_map/ppermute | solution.py:32
  91.4 7.7 %collective-permute-start.24 = (bf16[512,128]{1,0:T(8,128)(2,1)S(1)}, bf16[512,128]{1,0:T(8,128)(2,1)S(1)}, u32[]{:S(2)}, u32[]{:S(2)}) collective-permute-start(bf16[512,128]{1,0:T(8,128)(2,1)S(1)} %get-tuple-element.65), channel_id=1, source_target_pairs={{0,1},{1,0},{2,3},{3,2},{4,5},{5,4},{6,7},{7,6},{8,9},{9,8},{10,11... | collective-permute-start | bytes 393224 | tf_op jit(solution)/shard_map/ppermute | solution.py:32
  92.3 7.8 %collective-permute-start.25 = (bf16[512,128]{1,0:T(8,128)(2,1)S(1)}, bf16[512,128]{1,0:T(8,128)(2,1)S(1)}, u32[]{:S(2)}, u32[]{:S(2)}) collective-permute-start(bf16[512,128]{1,0:T(8,128)(2,1)S(1)} %get-tuple-element.66), channel_id=1, source_target_pairs={{0,4},{1,5},{2,6},{3,7},{4,0},{5,1},{6,2},{7,3},{8,12},{9,13},{10,... | collective-permute-start | bytes 393224 | tf_op jit(solution)/shard_map/ppermute | solution.py:32
  93.2 9.8 %collective-permute-start.26 = (bf16[512,128]{1,0:T(8,128)(2,1)S(1)}, bf16[512,128]{1,0:T(8,128)(2,1)S(1)}, u32[]{:S(2)}, u32[]{:S(2)}) collective-permute-start(bf16[512,128]{1,0:T(8,128)(2,1)S(1)} %get-tuple-element.67), channel_id=1, source_target_pairs={{0,7},{1,6},{2,5},{3,4},{4,3},{5,2},{6,1},{7,0},{8,15},{9,14},{10,... | collective-permute-start | bytes 393224 | tf_op jit(solution)/shard_map/ppermute | solution.py:32
  96.0 9.5 %collective-permute-start.20 = (bf16[512,128]{1,0:T(8,128)(2,1)S(1)}, bf16[512,128]{1,0:T(8,128)(2,1)S(1)}, u32[]{:S(2)}, u32[]{:S(2)}) collective-permute-start(bf16[512,128]{1,0:T(8,128)(2,1)S(1)} %get-tuple-element.61), channel_id=1, source_target_pairs={{0,3},{1,2},{2,1},{3,0},{4,7},{5,6},{6,5},{7,4},{8,11},{9,10},{10,... | collective-permute-start | bytes 393224 | tf_op jit(solution)/shard_map/ppermute | solution.py:32
  96.7 9.0 %collective-permute-start.21 = (bf16[512,128]{1,0:T(8,128)(2,1)S(1)}, bf16[512,128]{1,0:T(8,128)(2,1)S(1)}, u32[]{:S(2)}, u32[]{:S(2)}) collective-permute-start(bf16[512,128]{1,0:T(8,128)(2,1)S(1)} %get-tuple-element.62), channel_id=1, source_target_pairs={{0,6},{1,7},{2,4},{3,5},{4,2},{5,3},{6,0},{7,1},{8,14},{9,15},{10,... | collective-permute-start | bytes 393224 | tf_op jit(solution)/shard_map/ppermute | solution.py:32
  99.1 7.4 %collective-permute-start.22 = (bf16[512,128]{1,0:T(8,128)(2,1)S(1)}, bf16[512,128]{1,0:T(8,128)(2,1)S(1)}, u32[]{:S(2)}, u32[]{:S(2)}) collective-permute-start(bf16[512,128]{1,0:T(8,128)(2,1)S(1)} %get-tuple-element.63), channel_id=1, source_target_pairs={{0,2},{1,3},{2,0},{3,1},{4,6},{5,7},{6,4},{7,5},{8,10},{9,11},{10,... | collective-permute-start | bytes 393224 | tf_op jit(solution)/shard_map/ppermute | solution.py:32
  (7 other events, 27.3 us)

commit v6 on v5

--- a/solution.py
+++ b/solution.py
@@ -267,7 +267,7 @@
 
 
 def early_kernel(
-    place, mine, theirs, pot_mine, pot_theirs, low0, low1, high0, high3, rows, partial, out, scratch
+    place, mine, theirs, pot_mine, pot_theirs, low0, high0, rows, partial, out, scratch
 ):
     x, y, core, zl = place[0], place[1], place[2], place[3]
     each = mine.shape[1]
@@ -280,27 +280,25 @@
 
     @pl.when(core == 0)
     def _():
-        chunks = [(low0, low_block(core, y, 0)), (low1, low_block(core, y, 1))]
-        chunks += [(high0, high_block(core, y, 0)), (high3, high_block(core, y, 3))]
+        chunks = [(low0, low_block(core, y, 0)), (high0, high_block(core, y, 0))]
         for n, total in whole_chunks(rows, pots, chunks, scratch):
             out[:, column_lanes(n)] = total
 
     @pl.when(core == 1)
     def _():
         for k in range(4):
-            first = jnp.concatenate([square(low0, k), square(low1, k)], axis=0)
-            out[:, column_lanes(k)] = times(rows[:, : 2 * HALF], first)
-            partial[:, column_lanes(k)] = times(rows[:, column_lanes(0)], square(high0, k)) + times(
-                rows[:, column_lanes(3)], square(high3, k)
-            )
-
-
-def middle_kernel(place, rows, pot_mine, pot_theirs, low_before, high_before, low3, high1, partial, out, scratch):
+            out[:, column_lanes(k)] = times(rows[:, column_lanes(0)], square(low0, k))
+            partial[:, column_lanes(k)] = times(rows[:, column_lanes(0)], square(high0, k))
+
+
+def middle_kernel(
+    a, b, place, rows, pot_mine, pot_theirs, low_before, high_before, low, high, partial, out, scratch
+):
     y, core = place[1], place[2]
 
     @pl.when(core == 0)
     def _():
-        chunks = [(low3, low_block(core, y, 3)), (high1, high_block(core, y, 1))]
+        chunks = [(low, low_block(core, y, a)), (high, high_block(core, y, b))]
         for n, total in whole_chunks(rows, (pot_mine, pot_theirs), chunks, scratch):
             out[:, column_lanes(n)] = low_before[:, column_lanes(n)] + total
 
@@ -308,8 +306,8 @@
     def _():
         for k in range(4):
             lanes = column_lanes(k)
-            out[:, lanes] = low_before[:, lanes] + times(rows[:, column_lanes(3)], square(low3, k))
-            partial[:, lanes] = high_before[:, lanes] + times(rows[:, column_lanes(1)], square(high1, k))
+            out[:, lanes] = low_before[:, lanes] + times(rows[:, column_lanes(a)], square(low, k))
+            partial[:, lanes] = high_before[:, lanes] + times(rows[:, column_lanes(b)], square(high, k))
 
 
 def late_kernel(side, place, rows, pot, before, partial, *refs):
@@ -440,11 +438,11 @@
     lines = jax.ShapeDtypeStruct((2 * each, 1024), jnp.bfloat16)
     low0, low1, low2, low3 = lows
     high0, high1, high2, high3 = highs
-    near = [low0, low1, high0, high3]
-    lined, partial, early = call(early_kernel, "early", [lines, sums, sums], 3, place, *rows, *pots, *near)
-    partial, early = call(
-        middle_kernel, "middle", [sums, sums], 2, place, lined, *pots, early, partial, low3, high1, aliases={5: 0, 4: 1}
-    )
+    lined, partial, early = call(early_kernel, "early", [lines, sums, sums], 2, place, *rows, *pots, low0, high0)
+    for a, b in ((1, 3), (3, 1)):
+        kernel = functools.partial(middle_kernel, a, b)
+        args = [place, lined, *pots, early, partial, lows[a], highs[b]]
+        partial, early = call(kernel, "middle", [sums, sums], 2, *args, aliases={5: 0, 4: 1})
     halves = []
     for side, dtype in ((1, jnp.bfloat16), (0, jnp.float32)):
         out = jax.ShapeDtypeStruct((each, 1024), dtype)

time: 108 us -> 109 us (level)
  Pallas kernels: 25 us -> 26.6 us
  waiting for transfers between devices: 40.4 us -> 38.8 us
    pallas_call x4 -> x5, Pallas kernels: 13.3 us -> 15 us  [call(): pl.pallas_call(kernel, out_shape=outs, in_specs=[pl.BlockSpec(memory_spac...]
    ppermute x27, waiting for transfers between devices: 40.4 us -> 38.8 us  [send(): return lax.ppermute(value, AXES, moves(target))]
  transfers between devices with their start and end apart: 28 -> 28, of which waited for: 16 -> 16; matrix products, arithmetic and copies ran while one was open for 0% -> 0% of each run, Pallas kernels for 18% -> 19%
where the time goes in v6:
time: 109 us
  starting transfers between devices  40.2 us (37%)
  waiting for transfers between devices  38.8 us (36%)
  Pallas kernels  26.6 us (24%)
  local copies, waits for them, and re-layouts  2.91 us (3%)
    ppermute x27, waiting for transfers between devices, send(): return lax.ppermute(value, AXES, moves(target))  38.8 us
    ppermute x27, starting transfers between devices, send(): return lax.ppermute(value, AXES, moves(target))  36.5 us
    pallas_call x5, Pallas kernels, call(): pl.pallas_call(kernel, out_shape=outs, in_specs=[pl.BlockSpec(memory_spac...  15 us
    all_to_all x1, starting transfers between devices, shards(): lax.all_to_all(orbitals.reshape(8, -1, 128), 'orb', split_axis=0, concat_...  3.64 us
    unnamed x6, local copies, waits for them, and re-layouts  2.91 us
    pallas_call x2, Pallas kernels, put(): pl.pallas_call(functools.partial(put_kernel, order), out_shape=jax.ShapeD...  2.73 us
    pallas_call x1, Pallas kernels, pick(): pl.pallas_call(pick_kernel, out_shape=[block] * 4, in_specs=[pl.BlockSpec...  2.67 us
    pallas_call x1, Pallas kernels, pack(): pl.pallas_call(pack_kernel, out_shape=[jax.ShapeDtypeStruct((8, mine.shap...  2.51 us
  transfers between devices with their start and end apart: 28, of which 16 were waited for; matrix products, arithmetic and copies ran while one was open for 0% of the time, Pallas kernels for 19%

profile of v6, /device:TPU:1, one launch (start us, length us, event | category | flops | bytes accessed | tf_op | source)
XLA Modules:
  0.0 109.1 jit_solution(14510784146120528260)
XLA Ops:
  0.0 3.2 %collective-permute-start.7 = (bf16[512,4096]{1,0:T(8,128)(2,1)}, bf16[512,4096]{1,0:T(8,128)(2,1)}, u32[]{:S(2)}, u32[]{:S(2)}) collective-permute-start(bf16[512,4096]{1,0:T(8,128)(2,1)} %refs_0_.1), channel_id=1, source_target_pairs={{0,8},{1,9},{2,10},{3,11},{4,12},{5,13},{6,14},{7,15},{8,0},{9,1},... | collective-permute-start | bytes 12582920 | tf_op jit(solution)/shard_map/ppermute | solution.py:32
  3.2 3.6 %all-to-all-start = ((bf16[8,512,128]{2,1,0:T(8,128)(2,1)}), bf16[8,512,128]{2,1,0:T(8,128)(2,1)S(1)}, u32[]{:S(2)}, u32[]{:S(2)}) async-start(bf16[8,512,128]{2,1,0:T(8,128)(2,1)} %bitcast.10), calls=%async_computation | async-start | bytes 2097152 | tf_op jit(solution)/shard_map/all_to_all | solution.py:417
  11.7 2.7 %pick.1 = (bf16[2,128,256]{2,1,0:T(8,128)(2,1)S(1)}, bf16[2,128,256]{2,1,0:T(8,128)(2,1)S(1)}, bf16[2,128,256]{2,1,0:T(8,128)(2,1)S(1)}, bf16[2,128,256]{2,1,0:T(8,128)(2,1)S(1)}) custom-call(s32[3]{0:T(128)S(1)} %pad_add_fusion.1.place, s32[32,128]{1,0:T(8,128)S(1)} %get-tuple-element.39.slot_ref, f32[512,8]{1,0:T(8,128)S(1)} %get-tuple-element.40.where_ref, ...), custom_call_target="tpu_custom_call" | custom-call | flops 2500000000 | bytes 4000000 | tf_op jit(solution)/shard_map/pick/pallas_call | solution.py:153
  17.2 3.6 %collective-permute-done.1 = bf16[2,128,256]{2,1,0:T(8,128)(2,1)S(1)} collective-permute-done((bf16[2,128,256]{2,1,0:T(8,128)(2,1)S(1)}, bf16[2,128,256]{2,1,0:T(8,128)(2,1)S(1)}, u32[]{:S(2)}, u32[]{:S(2)}) %collective-permute-start.1) | collective-permute-done | bytes 131104 | tf_op jit(solution)/shard_map/ppermute | solution.py:32
  20.7 3.5 %collective-permute-done.2 = bf16[2,128,256]{2,1,0:T(8,128)(2,1)S(1)} collective-permute-done((bf16[2,128,256]{2,1,0:T(8,128)(2,1)S(1)}, bf16[2,128,256]{2,1,0:T(8,128)(2,1)S(1)}, u32[]{:S(2)}, u32[]{:S(2)}) %collective-permute-start.2) | collective-permute-done | bytes 131104 | tf_op jit(solution)/shard_map/ppermute | solution.py:32
  24.3 4.9 %collective-permute-start.4 = (bf16[2,128,256]{2,1,0:T(8,128)(2,1)S(1)}, bf16[2,128,256]{2,1,0:T(8,128)(2,1)S(1)}, u32[]{:S(2)}, u32[]{:S(2)}) collective-permute-start(bf16[2,128,256]{2,1,0:T(8,128)(2,1)S(1)} %add_add_fusion.1), channel_id=1, source_target_pairs={{0,32},{1,33},{2,34},{3,35},{4,36},{5,37},{6,38},{7,39},{8,40},{9,... | collective-permute-start | bytes 393224 | tf_op jit(solution)/shard_map/ppermute | solution.py:32
  30.5 2.2 %copy-done = bf16[512,4096]{1,0:T(8,128)(2,1)S(1)} copy-done((bf16[512,4096]{1,0:T(8,128)(2,1)S(1)}, bf16[512,4096]{1,0:T(8,128)(2,1)}, u32[]{:S(2)}) %copy-start) | copy-done | bytes 4194328
  32.6 2.5 %pack.1 = (bf16[8,512,256]{2,1,0:T(8,128)(2,1)S(1)}, bf16[8,512,256]{2,1,0:T(8,128)(2,1)S(1)}) custom-call(s32[4]{0:T(128)S(1)} %pad_add_fusion.place, bf16[512,4096]{1,0:T(8,128)(2,1)S(1)} %copy-done, bf16[512,4096]{1,0:T(8,128)(2,1)} %collective-permute-done.7.refs_1_), custom_call_target="tpu_custom_call" | custom-call | bytes 8000000 | tf_op jit(solution)/shard_map/pack/pallas_call | solution.py:212
  35.2 4.3 %collective-permute-done.5 = bf16[2,128,256]{2,1,0:T(8,128)(2,1)S(1)} collective-permute-done((bf16[2,128,256]{2,1,0:T(8,128)(2,1)S(1)}, bf16[2,128,256]{2,1,0:T(8,128)(2,1)S(1)}, u32[]{:S(2)}, u32[]{:S(2)}) %collective-permute-start.5) | collective-permute-done | bytes 131104 | tf_op jit(solution)/shard_map/ppermute | solution.py:32
  39.5 2.9 %collective-permute-done.6 = bf16[2,128,256]{2,1,0:T(8,128)(2,1)S(1)} collective-permute-done((bf16[2,128,256]{2,1,0:T(8,128)(2,1)S(1)}, bf16[2,128,256]{2,1,0:T(8,128)(2,1)S(1)}, u32[]{:S(2)}, u32[]{:S(2)}) %collective-permute-start.6) | collective-permute-done | bytes 131104 | tf_op jit(solution)/shard_map/ppermute | solution.py:32
  42.6 4.5 %collective-permute-done.8 = bf16[2,128,256]{2,1,0:T(8,128)(2,1)S(1)} collective-permute-done((bf16[2,128,256]{2,1,0:T(8,128)(2,1)S(1)}, bf16[2,128,256]{2,1,0:T(8,128)(2,1)S(1)}, u32[]{:S(2)}, u32[]{:S(2)}) %collective-permute-start.8) | collective-permute-done | bytes 131104 | tf_op jit(solution)/shard_map/ppermute | solution.py:32
  52.4 3.2 %collective-permute-done.10.refs_1_ = bf16[2,2,128,256]{3,2,1,0:T(8,128)(2,1)S(1)} collective-permute-done((bf16[2,2,128,256]{3,2,1,0:T(8,128)(2,1)S(1)}, bf16[2,2,128,256]{3,2,1,0:T(8,128)(2,1)S(1)}, u32[]{:S(2)}, u32[]{:S(2)}) %collective-permute-start.10) | collective-permute-done | bytes 262176 | tf_op jit(solution)/shard_map/ppermute | solution.py:32
  55.6 2.8 %collective-permute-done.11.refs_2_ = bf16[2,2,128,256]{3,2,1,0:T(8,128)(2,1)S(1)} collective-permute-done((bf16[2,2,128,256]{3,2,1,0:T(8,128)(2,1)S(1)}, bf16[2,2,128,256]{3,2,1,0:T(8,128)(2,1)S(1)}, u32[]{:S(2)}, u32[]{:S(2)}) %collective-permute-start.11) | collective-permute-done | bytes 262176 | tf_op jit(solution)/shard_map/ppermute | solution.py:32
  63.8 5.4 %collective-permute-done.13.low.refs_1_ = bf16[4,2,128,256]{3,2,1,0:T(8,128)(2,1)S(1)} collective-permute-done((bf16[4,2,128,256]{3,2,1,0:T(8,128)(2,1)S(1)}, bf16[4,2,128,256]{3,2,1,0:T(8,128)(2,1)S(1)}, u32[]{:S(2)}, u32[]{:S(2)}) %collective-permute-start.13) | collective-permute-done | bytes 524320 | tf_op jit(solution)/shard_map/ppermute | solution.py:32
  69.2 2.7 %collective-permute-start.18 = (bf16[4,2,128,256]{3,2,1,0:T(8,128)(2,1)S(1)}, bf16[4,2,128,256]{3,2,1,0:T(8,128)(2,1)S(1)}, u32[]{:S(2)}, u32[]{:S(2)}) collective-permute-start(bf16[4,2,128,256]{3,2,1,0:T(8,128)(2,1)S(1)} %collective-permute-done.14.high.refs_7_), channel_id=1, source_target_pairs={{0,192},{1,193},{2,194},{3,195},{4,196},{5,197},{6,198},{7,199},{8... | collective-permute-start | bytes 1572872 | tf_op jit(solution)/shard_map/ppermute | solution.py:32
  71.9 2.4 %early.1 = (bf16[1024,1024]{1,0:T(8,128)(2,1)S(1)}, f32[1024,1024]{1,0:T(8,128)S(1)}, f32[1024,1024]{1,0:T(8,128)S(1)}) custom-call(s32[4]{0:T(128)S(1)} %pad_add_fusion.place, bf16[8,512,128]{2,1,0:T(8,128)(2,1)S(1)} %all-to-all-done.mine, bf16[8,512,128]{2,1,0:T(8,128)(2,1)S(1)} %collective-permute-done.9.theirs, ...), custom_call_target="tpu_custom_call" | custom-call | flops 2147483648 | bytes 4194304 | tf_op jit(solution)/shard_map/early/pallas_call | solution.py:339
  74.3 2.7 %middle.2 = (f32[1024,1024]{1,0:T(8,128)S(1)}, f32[1024,1024]{1,0:T(8,128)S(1)}) custom-call(s32[4]{0:T(128)S(1)} %pad_add_fusion.place, bf16[1024,1024]{1,0:T(8,128)(2,1)S(1)} %get-tuple-element.58.rows, bf16[8,512,256]{2,1,0:T(8,128)(2,1)S(1)} %get-tuple-element.53.pot_mine.pot, ...), custom_call_target="tpu_custom_call", output_to_operand_aliasing={{0}: (5, {}), {1}: (4, {})} | custom-call | flops 2147483648 | bytes 4194304 | tf_op jit(solution)/shard_map/middle/pallas_call | solution.py:339
  77.1 3.0 %middle.3 = (f32[1024,1024]{1,0:T(8,128)S(1)}, f32[1024,1024]{1,0:T(8,128)S(1)}) custom-call(s32[4]{0:T(128)S(1)} %pad_add_fusion.place, bf16[1024,1024]{1,0:T(8,128)(2,1)S(1)} %get-tuple-element.58.rows, bf16[8,512,256]{2,1,0:T(8,128)(2,1)S(1)} %get-tuple-element.53.pot_mine.pot, ...), custom_call_target="tpu_custom_call", output_to_operand_aliasing={{0}: (5, {}), {1}: (4, {})} | custom-call | flops 2147483648 | bytes 4194304 | tf_op jit(solution)/shard_map/middle/pallas_call | solution.py:339
  80.4 3.4 %late.3 = bf16[512,1024]{1,0:T(8,128)(2,1)S(1)} custom-call(s32[4]{0:T(128)S(1)} %pad_add_fusion.place, bf16[1024,1024]{1,0:T(8,128)(2,1)S(1)} %get-tuple-element.58.rows, bf16[8,512,256]{2,1,0:T(8,128)(2,1)S(1)} %get-tuple-element.54.pot_theirs.pot, f32[1024,1024]{1,0:T(8,128)S(1)} %get-tuple-element.63.before, f32[1024,1024]{1,0:T(8,128)S(1)} %get-tuple-element.64.partial, ...), custom_call_target="tpu_custom_call" | custom-call | flops 1610612736 | bytes 4194304 | tf_op jit(solution)/shard_map/late/pallas_call | solution.py:339
  85.2 3.4 %late.2.mine = f32[512,1024]{1,0:T(8,128)S(1)} custom-call(s32[4]{0:T(128)S(1)} %pad_add_fusion.place, bf16[1024,1024]{1,0:T(8,128)(2,1)S(1)} %get-tuple-element.58.rows, bf16[8,512,256]{2,1,0:T(8,128)(2,1)S(1)} %get-tuple-element.53.pot_mine.pot, f32[1024,1024]{1,0:T(8,128)S(1)} %get-tuple-element.63.before, f32[1024,1024]{1,0:T(8,128)S(1)} %get-tuple-element.64.partial, ...), custom_call_target="tpu_custom_call" | custom-call | flops 1610612736 | bytes 4194304 | tf_op jit(solution)/shard_map/late/pallas_call | solution.py:339
  89.7 2.3 %collective-permute-start.23 = (bf16[512,128]{1,0:T(8,128)(2,1)S(1)}, bf16[512,128]{1,0:T(8,128)(2,1)S(1)}, u32[]{:S(2)}, u32[]{:S(2)}) collective-permute-start(bf16[512,128]{1,0:T(8,128)(2,1)S(1)} %get-tuple-element.68), channel_id=1, source_target_pairs={{0,5},{1,4},{2,7},{3,6},{4,1},{5,0},{6,3},{7,2},{8,13},{9,12},{10,... | collective-permute-start | bytes 393224 | tf_op jit(solution)/shard_map/ppermute | solution.py:32
  94.0 2.8 %collective-permute-start.26 = (bf16[512,128]{1,0:T(8,128)(2,1)S(1)}, bf16[512,128]{1,0:T(8,128)(2,1)S(1)}, u32[]{:S(2)}, u32[]{:S(2)}) collective-permute-start(bf16[512,128]{1,0:T(8,128)(2,1)S(1)} %get-tuple-element.71), channel_id=1, source_target_pairs={{0,7},{1,6},{2,5},{3,4},{4,3},{5,2},{6,1},{7,0},{8,15},{9,14},{10,... | collective-permute-start | bytes 393224 | tf_op jit(solution)/shard_map/ppermute | solution.py:32
  97.4 2.4 %collective-permute-start.21 = (bf16[512,128]{1,0:T(8,128)(2,1)S(1)}, bf16[512,128]{1,0:T(8,128)(2,1)S(1)}, u32[]{:S(2)}, u32[]{:S(2)}) collective-permute-start(bf16[512,128]{1,0:T(8,128)(2,1)S(1)} %get-tuple-element.66), channel_id=1, source_target_pairs={{0,6},{1,7},{2,4},{3,5},{4,2},{5,3},{6,0},{7,1},{8,14},{9,15},{10,... | collective-permute-start | bytes 393224 | tf_op jit(solution)/shard_map/ppermute | solution.py:32
  100.8 2.9 %collective-permute-done.26.refs_3_ = bf16[512,128]{1,0:T(8,128)(2,1)S(1)} collective-permute-done((bf16[512,128]{1,0:T(8,128)(2,1)S(1)}, bf16[512,128]{1,0:T(8,128)(2,1)S(1)}, u32[]{:S(2)}, u32[]{:S(2)}) %collective-permute-start.26) | collective-permute-done | bytes 131104 | tf_op jit(solution)/shard_map/ppermute | solution.py:32
  (55 shorter events, 31.4 us)
Async XLA Ops:
  0.0 30.5 %collective-permute-start.7 = (bf16[512,4096]{1,0:T(8,128)(2,1)}, bf16[512,4096]{1,0:T(8,128)(2,1)}, u32[]{:S(2)}, u32[]{:S(2)}) collective-permute-start(bf16[512,4096]{1,0:T(8,128)(2,1)} %refs_0_.1), channel_id=1, source_target_pairs={{0,8},{1,9},{2,10},{3,11},{4,12},{5,13},{6,14},{7,15},{8,0},{9,1},... | collective-permute-start | bytes 12582920 | tf_op jit(solution)/shard_map/ppermute | solution.py:32
  3.2 21.0 %all-to-all-start = ((bf16[8,512,128]{2,1,0:T(8,128)(2,1)}), bf16[8,512,128]{2,1,0:T(8,128)(2,1)S(1)}, u32[]{:S(2)}, u32[]{:S(2)}) async-start(bf16[8,512,128]{2,1,0:T(8,128)(2,1)} %bitcast.10), calls=%async_computation | async-start | bytes 2097152 | tf_op jit(solution)/shard_map/all_to_all | solution.py:417
  15.9 8.4 %collective-permute-start.2 = (bf16[2,128,256]{2,1,0:T(8,128)(2,1)S(1)}, bf16[2,128,256]{2,1,0:T(8,128)(2,1)S(1)}, u32[]{:S(2)}, u32[]{:S(2)}) collective-permute-start(bf16[2,128,256]{2,1,0:T(8,128)(2,1)S(1)} %get-tuple-element.42), channel_id=1, source_target_pairs={{0,192},{1,193},{2,194},{3,195},{4,196},{5,197},{6,198},{7,199},{8... | collective-permute-start | bytes 393224 | tf_op jit(solution)/shard_map/ppermute | solution.py:32
  16.6 7.6 %collective-permute-start.3 = (bf16[2,128,256]{2,1,0:T(8,128)(2,1)S(1)}, bf16[2,128,256]{2,1,0:T(8,128)(2,1)S(1)}, u32[]{:S(2)}, u32[]{:S(2)}) collective-permute-start(bf16[2,128,256]{2,1,0:T(8,128)(2,1)S(1)} %get-tuple-element.43), channel_id=1, source_target_pairs={{0,64},{1,65},{2,66},{3,67},{4,68},{5,69},{6,70},{7,71},{8,72},{9,... | collective-permute-start | bytes 393224 | tf_op jit(solution)/shard_map/ppermute | solution.py:32
  24.3 10.9 %collective-permute-start.4 = (bf16[2,128,256]{2,1,0:T(8,128)(2,1)S(1)}, bf16[2,128,256]{2,1,0:T(8,128)(2,1)S(1)}, u32[]{:S(2)}, u32[]{:S(2)}) collective-permute-start(bf16[2,128,256]{2,1,0:T(8,128)(2,1)S(1)} %add_add_fusion.1), channel_id=1, source_target_pairs={{0,32},{1,33},{2,34},{3,35},{4,36},{5,37},{6,38},{7,39},{8,40},{9,... | collective-permute-start | bytes 393224 | tf_op jit(solution)/shard_map/ppermute | solution.py:32
  29.2 10.3 %collective-permute-start.5 = (bf16[2,128,256]{2,1,0:T(8,128)(2,1)S(1)}, bf16[2,128,256]{2,1,0:T(8,128)(2,1)S(1)}, u32[]{:S(2)}, u32[]{:S(2)}) collective-permute-start(bf16[2,128,256]{2,1,0:T(8,128)(2,1)S(1)} %add_add_fusion.1), channel_id=1, source_target_pairs={{0,48},{1,49},{2,50},{3,51},{4,52},{5,53},{6,54},{7,55},{8,56},{9,... | collective-permute-start | bytes 393224 | tf_op jit(solution)/shard_map/ppermute | solution.py:32
  29.2 13.2 %collective-permute-start.6 = (bf16[2,128,256]{2,1,0:T(8,128)(2,1)S(1)}, bf16[2,128,256]{2,1,0:T(8,128)(2,1)S(1)}, u32[]{:S(2)}, u32[]{:S(2)}) collective-permute-start(bf16[2,128,256]{2,1,0:T(8,128)(2,1)S(1)} %add_add_fusion.1), channel_id=1, source_target_pairs={{0,16},{1,17},{2,18},{3,19},{4,20},{5,21},{6,22},{7,23},{8,24},{9,... | collective-permute-start | bytes 393224 | tf_op jit(solution)/shard_map/ppermute | solution.py:32
  47.1 24.8 %collective-permute-start.9 = (bf16[8,512,128]{2,1,0:T(8,128)(2,1)S(1)}, bf16[8,512,128]{2,1,0:T(8,128)(2,1)S(1)}, u32[]{:S(2)}, u32[]{:S(2)}) collective-permute-start(bf16[8,512,128]{2,1,0:T(8,128)(2,1)S(1)} %all-to-all-done.mine), channel_id=1, source_target_pairs={{0,8},{1,9},{2,10},{3,11},{4,12},{5,13},{6,14},{7,15},{8,0},{9,1},... | collective-permute-start | bytes 3145736 | tf_op jit(solution)/shard_map/ppermute | solution.py:32
  48.6 7.0 %collective-permute-start.10 = (bf16[2,2,128,256]{3,2,1,0:T(8,128)(2,1)S(1)}, bf16[2,2,128,256]{3,2,1,0:T(8,128)(2,1)S(1)}, u32[]{:S(2)}, u32[]{:S(2)}) collective-permute-start(bf16[2,2,128,256]{3,2,1,0:T(8,128)(2,1)S(1)} %pad_maximum_fusion.refs_0_), channel_id=1, source_target_pairs={{0,4},{1,5},{2,6},{3,7},{4,0},{5,1},{6,2},{7,3},{8,136},{9,137},{1... | collective-permute-start | bytes 786440 | tf_op jit(solution)/shard_map/ppermute | solution.py:32
  50.3 8.1 %collective-permute-start.11 = (bf16[2,2,128,256]{3,2,1,0:T(8,128)(2,1)S(1)}, bf16[2,2,128,256]{3,2,1,0:T(8,128)(2,1)S(1)}, u32[]{:S(2)}, u32[]{:S(2)}) collective-permute-start(bf16[2,2,128,256]{3,2,1,0:T(8,128)(2,1)S(1)} %pad_maximum_fusion.refs_0_), channel_id=1, source_target_pairs={{0,6},{1,7},{2,4},{3,5},{4,2},{5,3},{6,0},{7,1},{8,200},{9,201},{1... | collective-permute-start | bytes 786440 | tf_op jit(solution)/shard_map/ppermute | solution.py:32
  52.4 6.5 %collective-permute-start.12 = (bf16[2,2,128,256]{3,2,1,0:T(8,128)(2,1)S(1)}, bf16[2,2,128,256]{3,2,1,0:T(8,128)(2,1)S(1)}, u32[]{:S(2)}, u32[]{:S(2)}) collective-permute-start(bf16[2,2,128,256]{3,2,1,0:T(8,128)(2,1)S(1)} %pad_maximum_fusion.refs_0_), channel_id=1, source_target_pairs={{0,2},{1,3},{2,0},{3,1},{4,6},{5,7},{6,4},{7,5},{8,72},{9,73},{10,... | collective-permute-start | bytes 786440 | tf_op jit(solution)/shard_map/ppermute | solution.py:32
  59.6 9.6 %collective-permute-start.13 = (bf16[4,2,128,256]{3,2,1,0:T(8,128)(2,1)S(1)}, bf16[4,2,128,256]{3,2,1,0:T(8,128)(2,1)S(1)}, u32[]{:S(2)}, u32[]{:S(2)}) collective-permute-start(bf16[4,2,128,256]{3,2,1,0:T(8,128)(2,1)S(1)} %get-tuple-element.56.low0.refs_0_), channel_id=1, source_target_pairs={{0,64},{1,65},{2,66},{3,67},{4,68},{5,69},{6,70},{7,71},{8,10},{9,... | collective-permute-start | bytes 1572872 | tf_op jit(solution)/shard_map/ppermute | solution.py:32
  60.8 8.4 %collective-permute-start.14 = (bf16[4,2,128,256]{3,2,1,0:T(8,128)(2,1)S(1)}, bf16[4,2,128,256]{3,2,1,0:T(8,128)(2,1)S(1)}, u32[]{:S(2)}, u32[]{:S(2)}) collective-permute-start(bf16[4,2,128,256]{3,2,1,0:T(8,128)(2,1)S(1)} %get-tuple-element.57.high0.refs_4_), channel_id=1, source_target_pairs={{0,192},{1,193},{2,194},{3,195},{4,196},{5,197},{6,198},{7,199},{8... | collective-permute-start | bytes 1572872 | tf_op jit(solution)/shard_map/ppermute | solution.py:32
  62.3 14.7 %collective-permute-start.15 = (bf16[4,2,128,256]{3,2,1,0:T(8,128)(2,1)S(1)}, bf16[4,2,128,256]{3,2,1,0:T(8,128)(2,1)S(1)}, u32[]{:S(2)}, u32[]{:S(2)}) collective-permute-start(bf16[4,2,128,256]{3,2,1,0:T(8,128)(2,1)S(1)} %get-tuple-element.56.low0.refs_0_), channel_id=1, source_target_pairs={{0,192},{1,193},{2,194},{3,195},{4,196},{5,197},{6,198},{7,199},{8... | collective-permute-start | bytes 1572872 | tf_op jit(solution)/shard_map/ppermute | solution.py:32
  63.5 13.6 %collective-permute-start.16 = (bf16[4,2,128,256]{3,2,1,0:T(8,128)(2,1)S(1)}, bf16[4,2,128,256]{3,2,1,0:T(8,128)(2,1)S(1)}, u32[]{:S(2)}, u32[]{:S(2)}) collective-permute-start(bf16[4,2,128,256]{3,2,1,0:T(8,128)(2,1)S(1)} %get-tuple-element.57.high0.refs_4_), channel_id=1, source_target_pairs={{0,64},{1,65},{2,66},{3,67},{4,68},{5,69},{6,70},{7,71},{8,10},{9,... | collective-permute-start | bytes 1572872 | tf_op jit(solution)/shard_map/ppermute | solution.py:32
  69.2 11.2 %collective-permute-start.17 = (bf16[4,2,128,256]{3,2,1,0:T(8,128)(2,1)S(1)}, bf16[4,2,128,256]{3,2,1,0:T(8,128)(2,1)S(1)}, u32[]{:S(2)}, u32[]{:S(2)}) collective-permute-start(bf16[4,2,128,256]{3,2,1,0:T(8,128)(2,1)S(1)} %collective-permute-done.13.low.refs_1_), channel_id=1, source_target_pairs={{0,64},{1,65},{2,66},{3,67},{4,68},{5,69},{6,70},{7,71},{8,10},{9,... | collective-permute-start | bytes 1572872 | tf_op jit(solution)/shard_map/ppermute | solution.py:32
  69.2 11.2 %collective-permute-start.18 = (bf16[4,2,128,256]{3,2,1,0:T(8,128)(2,1)S(1)}, bf16[4,2,128,256]{3,2,1,0:T(8,128)(2,1)S(1)}, u32[]{:S(2)}, u32[]{:S(2)}) collective-permute-start(bf16[4,2,128,256]{3,2,1,0:T(8,128)(2,1)S(1)} %collective-permute-done.14.high.refs_7_), channel_id=1, source_target_pairs={{0,192},{1,193},{2,194},{3,195},{4,196},{5,197},{6,198},{7,199},{8... | collective-permute-start | bytes 1572872 | tf_op jit(solution)/shard_map/ppermute | solution.py:32
  89.7 7.7 %collective-permute-start.23 = (bf16[512,128]{1,0:T(8,128)(2,1)S(1)}, bf16[512,128]{1,0:T(8,128)(2,1)S(1)}, u32[]{:S(2)}, u32[]{:S(2)}) collective-permute-start(bf16[512,128]{1,0:T(8,128)(2,1)S(1)} %get-tuple-element.68), channel_id=1, source_target_pairs={{0,5},{1,4},{2,7},{3,6},{4,1},{5,0},{6,3},{7,2},{8,13},{9,12},{10,... | collective-permute-start | bytes 393224 | tf_op jit(solution)/shard_map/ppermute | solution.py:32
  92.0 7.8 %collective-permute-start.24 = (bf16[512,128]{1,0:T(8,128)(2,1)S(1)}, bf16[512,128]{1,0:T(8,128)(2,1)S(1)}, u32[]{:S(2)}, u32[]{:S(2)}) collective-permute-start(bf16[512,128]{1,0:T(8,128)(2,1)S(1)} %get-tuple-element.69), channel_id=1, source_target_pairs={{0,1},{1,0},{2,3},{3,2},{4,5},{5,4},{6,7},{7,6},{8,9},{9,8},{10,11... | collective-permute-start | bytes 393224 | tf_op jit(solution)/shard_map/ppermute | solution.py:32
  92.8 8.0 %collective-permute-start.25 = (bf16[512,128]{1,0:T(8,128)(2,1)S(1)}, bf16[512,128]{1,0:T(8,128)(2,1)S(1)}, u32[]{:S(2)}, u32[]{:S(2)}) collective-permute-start(bf16[512,128]{1,0:T(8,128)(2,1)S(1)} %get-tuple-element.70), channel_id=1, source_target_pairs={{0,4},{1,5},{2,6},{3,7},{4,0},{5,1},{6,2},{7,3},{8,12},{9,13},{10,... | collective-permute-start | bytes 393224 | tf_op jit(solution)/shard_map/ppermute | solution.py:32
  94.0 9.8 %collective-permute-start.26 = (bf16[512,128]{1,0:T(8,128)(2,1)S(1)}, bf16[512,128]{1,0:T(8,128)(2,1)S(1)}, u32[]{:S(2)}, u32[]{:S(2)}) collective-permute-start(bf16[512,128]{1,0:T(8,128)(2,1)S(1)} %get-tuple-element.71), channel_id=1, source_target_pairs={{0,7},{1,6},{2,5},{3,4},{4,3},{5,2},{6,1},{7,0},{8,15},{9,14},{10,... | collective-permute-start | bytes 393224 | tf_op jit(solution)/shard_map/ppermute | solution.py:32
  96.7 9.2 %collective-permute-start.20 = (bf16[512,128]{1,0:T(8,128)(2,1)S(1)}, bf16[512,128]{1,0:T(8,128)(2,1)S(1)}, u32[]{:S(2)}, u32[]{:S(2)}) collective-permute-start(bf16[512,128]{1,0:T(8,128)(2,1)S(1)} %get-tuple-element.65), channel_id=1, source_target_pairs={{0,3},{1,2},{2,1},{3,0},{4,7},{5,6},{6,5},{7,4},{8,11},{9,10},{10,... | collective-permute-start | bytes 393224 | tf_op jit(solution)/shard_map/ppermute | solution.py:32
  97.4 9.0 %collective-permute-start.21 = (bf16[512,128]{1,0:T(8,128)(2,1)S(1)}, bf16[512,128]{1,0:T(8,128)(2,1)S(1)}, u32[]{:S(2)}, u32[]{:S(2)}) collective-permute-start(bf16[512,128]{1,0:T(8,128)(2,1)S(1)} %get-tuple-element.66), channel_id=1, source_target_pairs={{0,6},{1,7},{2,4},{3,5},{4,2},{5,3},{6,0},{7,1},{8,14},{9,15},{10,... | collective-permute-start | bytes 393224 | tf_op jit(solution)/shard_map/ppermute | solution.py:32
  99.8 7.8 %collective-permute-start.22 = (bf16[512,128]{1,0:T(8,128)(2,1)S(1)}, bf16[512,128]{1,0:T(8,128)(2,1)S(1)}, u32[]{:S(2)}, u32[]{:S(2)}) collective-permute-start(bf16[512,128]{1,0:T(8,128)(2,1)S(1)} %get-tuple-element.67), channel_id=1, source_target_pairs={{0,2},{1,3},{2,0},{3,1},{4,6},{5,7},{6,4},{7,5},{8,10},{9,11},{10,... | collective-permute-start | bytes 393224 | tf_op jit(solution)/shard_map/ppermute | solution.py:32
  (7 other events, 28.3 us)
